TPU v7x, 512 devices: a whole 4x8x8 slice. The times are simulated.
512 devices in a mesh: dp: 32 (over y, z_lo, core), tensor: 16 (over x, z_hi).
Axes of the slice: x: 4, y: 8, z: 8 (z_hi: 4, z_lo: 2; z = z_hi * 2 + z_lo), core: 2. Of those that a mesh axis runs over, the one named last changes fastest.
Arguments:
- inputs: bfloat16 [32, 384, 5120], P('dp', None, 'tensor'), may hold values from -6 to 6, as said below
- w_query: bfloat16 [5120, 4096], P('dp', 'tensor'), as said below
- w_key: bfloat16 [5120, 4096], P('dp', 'tensor'), as said below
- w_value: bfloat16 [5120, 4096], P('dp', 'tensor'), may hold values from -0.078125 to 0.078125
- tangent: bfloat16 [5120, 4096], P('dp', 'tensor'), as said below
- gain_query: float32 [4096], P('tensor'), may hold values from 0.3 to 3, as said below
- gain_key: float32 [4096], P('tensor'), may hold values from 0.1 to 1.9
Outputs:
- curvature: float32 [5120, 4096], P('dp', 'tensor')
Inputs may be any that keep to these rules, and one draw needn't show every extreme that they name: Layer inputs of order one. `w_query`: entries of order one over the square root of 5120. `w_key`: entries of order one over the square root of 5120. `tangent`: entries of order one over the square root of 5120. `gain_query`: positive gains of order one.
All inputs are finite; a program needn't handle non-finite values.
Results may differ from a plain program's by a relative error of at most 0.03.
Values may be sent and summed in bfloat16 or wider, within the bound.
No kernel may reach another device: no remote copies, remote signals or barrier semaphores. Data moves between devices by JAX's collectives and lax.ppermute only.
A program may use at most 64 MiB of HBM per device.

v0:
```python
import jax
import jax.numpy as jnp
from jax import lax
from jax.sharding import PartitionSpec as P

HEADS = 32
HD = 128


EPS = 1e-06


def on_device(inputs, w_query, w_key, w_value, tangent, gain_query, gain_key):
    tokens = lax.all_gather(inputs, "tensor", axis=2, tiled=True)[0]
    length = tokens.shape[0]
    cols = w_query.shape[1]
    heads = cols // HD
    total_cols = HEADS * HD
    scale = 1.0 / HD**0.5
    pieces = (
        lax.all_gather(w_query, "dp", axis=0, tiled=True),
        lax.all_gather(w_key, "dp", axis=0, tiled=True),
        lax.all_gather(w_value, "dp", axis=0, tiled=True),
        lax.all_gather(tangent, "dp", axis=0, tiled=True),
    )
    part = tokens
    query, key, value_raw, dquery = tuple(
        (jnp.dot(part, piece, preferred_element_type=jnp.float32) for piece in pieces)
    )
    value = value_raw.astype(jnp.bfloat16)
    sum_query, sum_key = lax.psum(
        (jnp.sum(query * query, axis=1), jnp.sum(key * key, axis=1)), "tensor"
    )
    rq = lax.rsqrt(sum_query[:, None] / total_cols + EPS)
    rk = lax.rsqrt(sum_key[:, None] / total_cols + EPS)
    cross = lax.psum(jnp.sum(query * dquery, axis=1), "tensor")
    tq = cross[:, None] / total_cols
    qn = (gain_query * query * rq).astype(jnp.bfloat16).reshape(length, heads, HD)
    kn = (gain_key * key * rk).astype(jnp.bfloat16).reshape(length, heads, HD)
    dqn = (
        (gain_query * rq * (dquery - query * rq * rq * tq))
        .astype(jnp.bfloat16)
        .reshape(length, heads, HD)
    )
    vh = value.reshape(length, heads, HD)
    places = lax.broadcasted_iota(jnp.int32, (length, length), 0)
    others = lax.broadcasted_iota(jnp.int32, (length, length), 1)
    causal = others <= places
    scores = jnp.einsum("qhd,khd->hqk", qn, kn, preferred_element_type=jnp.float32) * scale
    scores = jnp.where(causal[None], scores, -jnp.inf)
    top = jnp.max(scores, axis=2, keepdims=True)
    expo = jnp.exp(scores - top)
    probs = expo / jnp.sum(expo, axis=2, keepdims=True)
    dscore = jnp.einsum("qhd,khd->hqk", dqn, kn, preferred_element_type=jnp.float32) * scale
    dprob = probs * (dscore - jnp.sum(probs * dscore, axis=2, keepdims=True))
    dpb = dprob.astype(jnp.bfloat16)
    upper = jnp.einsum("hqk,khd->qhd", dpb, vh, preferred_element_type=jnp.float32).astype(
        jnp.bfloat16
    )
    gprob = jnp.einsum("qhd,khd->hqk", upper, vh, preferred_element_type=jnp.float32)
    gscore = (probs * (gprob - jnp.sum(probs * gprob, axis=2, keepdims=True))).astype(jnp.bfloat16)
    gqn = (
        jnp.einsum("hqk,khd->qhd", gscore, kn, preferred_element_type=jnp.float32) * scale
    ).reshape(length, cols)
    weighted = gain_query * gqn
    back = lax.psum(jnp.sum(query * weighted, axis=1), "tensor")
    tb = back[:, None] / total_cols
    grad_query = (rq * weighted - query * rq * rq * rq * tb).astype(jnp.bfloat16)
    part = tokens
    return lax.psum_scatter(
        lax.dot_general(
            part, grad_query, (((0,), (0,)), ((), ())), preferred_element_type=jnp.float32
        ).astype(jnp.bfloat16),
        "dp",
        scatter_dimension=0,
        tiled=True,
    ).astype(jnp.float32)


def solution(mesh):
    return jax.shard_map(
        on_device,
        mesh=mesh,
        in_specs=(
            P("dp", None, "tensor"),
            P("dp", "tensor"),
            P("dp", "tensor"),
            P("dp", "tensor"),
            P("dp", "tensor"),
            P("tensor"),
            P("tensor"),
        ),
        out_specs=P("dp", "tensor"),
        check_vma=False,
    )
```

profile of v0, /device:TPU:1, one launch (start us, length us, event | category | flops | bytes accessed | tf_op | source)
XLA Modules:
  0.0 556.5 jit_solution(9939662634985640153)
XLA Ops:
  6.5 0.0 all-gather.14.cloned.1.call-start
  6.5 0.7 all-gather.14.cloned.1.call-update
  7.3 0.0 all-gather.6.cloned.1.call-start
  7.3 0.7 all-gather.6.cloned.1.call-update
  8.0 0.0 all-gather.10.cloned.1.call-start
  8.1 0.7 all-gather.10.cloned.1.call-update
  8.7 0.0 all-gather.8.cloned.1.call-start
  8.8 0.5 all-gather.8.cloned.1.call-update
  9.3 0.0 all-gather.12.cloned.1.call-start
  9.4 0.5 all-gather.12.cloned.1.call-update
  9.9 0.0 reduce-scatter.4.cloned.1.call-start
  10.0 73.6 %all-gather.14.cloned.1.call-done = bf16[5120,256]{1,0:T(8,128)(2,1)} async-done(((bf16[160,256]{1,0:T(8,128)(2,1)}), bf16[5120,256]{1,0:T(8,128)(2,1)}) %all-gather.14.cloned.1.call-update) | async-done | bytes 2621456 | tf_op jit(solution)/shard_map/all_gather | solution.py:24
  83.6 83.9 %all-gather.6.cloned.1.call-done = bf16[1,384,5120]{1,2,0:T(8,128)(2,1)} async-done(((bf16[1,384,320]{1,2,0:T(8,128)(2,1)}), bf16[1,384,5120]{1,2,0:T(8,128)(2,1)}) %all-gather.6.cloned.1.call-update) | async-done | bytes 3932176 | tf_op jit(solution)/shard_map/all_gather | solution.py:14
  167.5 4.5 fusion.3
  172.0 63.9 %all-gather.10.cloned.1.call-done = bf16[5120,256]{1,0:T(8,128)(2,1)} async-done(((bf16[160,256]{1,0:T(8,128)(2,1)}), bf16[5120,256]{1,0:T(8,128)(2,1)}) %all-gather.10.cloned.1.call-update) | async-done | bytes 2621456 | tf_op jit(solution)/shard_map/all_gather | solution.py:22
  235.9 4.5 multiply_reduce_fusion.4
  240.4 0.0 copy-start.1
  240.5 0.0 copy-start
  240.5 65.3 %all-gather.8.cloned.1.call-done = bf16[5120,256]{1,0:T(8,128)(2,1)} async-done(((bf16[160,256]{1,0:T(8,128)(2,1)}), bf16[5120,256]{1,0:T(8,128)(2,1)}) %all-gather.8.cloned.1.call-update) | async-done | bytes 2621456 | tf_op jit(solution)/shard_map/all_gather | solution.py:21
  305.7 4.5 multiply_reduce_fusion.5
  310.2 38.6 %all-reduce = (f32[384]{0:T(512)S(1)}, f32[384]{0:T(512)S(1)}, f32[384]{0:T(512)S(1)}) all-reduce(f32[384]{0:T(512)S(1)} %get-tuple-element.12, f32[384]{0:T(512)S(1)} %get-tuple-element.6, f32[384]{0:T(512)S(1)} %get-tuple-element.5), channel_id=1, replica_groups=mesh['dp'=32,'tensor'=16] {'tensor'}, use_global_device_ids=true, to_apply=%region_3.0 | all-reduce | flops 1152 | bytes 9216 | tf_op jit(solution)/shard_map/psum | solution.py:31
  348.9 0.0 copy-done.1
  348.9 0.1 multiply_convert_fusion.7
  349.0 0.0 copy-done
  349.0 0.2 multiply_convert_fusion.6
  349.2 0.6 fusion.25
  349.8 1.4 multiply_reduce_fusion.1
  351.2 24.3 %all-gather.12.cloned.1.call-done = bf16[5120,256]{1,0:T(8,128)(2,1)} async-done(((bf16[160,256]{1,0:T(8,128)(2,1)}), bf16[5120,256]{1,0:T(8,128)(2,1)}) %all-gather.12.cloned.1.call-update) | async-done | bytes 2621456 | tf_op jit(solution)/shard_map/all_gather | solution.py:23
  375.4 4.5 fusion.14
  380.0 2.9 multiply_reduce_fusion
  382.8 1.6 convolution_multiply_fusion.2
  384.5 0.1 multiply_reduce_fusion.2
  384.6 38.0 %psum.31 = f32[384]{0:T(512)S(1)} all-reduce(f32[384]{0:T(512)S(1)} %multiply_reduce_fusion.2), channel_id=1, replica_groups=mesh['dp'=32,'tensor'=16] {'tensor'}, use_global_device_ids=true, to_apply=%region_11.12 | all-reduce | flops 384 | bytes 3072 | tf_op jit(solution)/shard_map/psum | solution.py:66
  422.6 0.1 subtract_convert_fusion
  422.7 3.7 fusion.1
  426.4 2.6 copy.39
  429.0 0.0 reduce-scatter.4.cloned.1.call-update
  429.0 119.1 %reduce-scatter.4.cloned.1.call-done = bf16[160,256]{1,0:T(8,128)(2,1)} async-done(((bf16[5120,256]{1,0:T(8,128)(2,1)}), bf16[160,256]{1,0:T(8,128)(2,1)}) %reduce-scatter.4.cloned.1.call-update) | async-done | bytes 81936 | tf_op jit(solution)/shard_map/reduce_scatter | solution.py:70
  548.1 1.6 convert_element_type.47
  (4 shorter events, 0.1 us)
Async XLA Ops:
  6.5 77.0 %all-gather.14.cloned.1.call-start = ((), (), s32[]{:S(2)}) async-start(), calls=%async_computation.5 | async-start | bytes 2703360 | tf_op jit(solution)/shard_map/all_gather | solution.py:24
  7.3 160.2 %all-gather.6.cloned.1.call-start = ((), (), s32[]{:S(2)}) async-start(), calls=%async_computation.1 | async-start | bytes 4177920 | tf_op jit(solution)/shard_map/all_gather | solution.py:14
  8.0 227.9 %all-gather.10.cloned.1.call-start = ((), (), s32[]{:S(2)}) async-start(), calls=%async_computation.3 | async-start | bytes 2703360 | tf_op jit(solution)/shard_map/all_gather | solution.py:22
  8.7 297.0 %all-gather.8.cloned.1.call-start = ((), (), s32[]{:S(2)}) async-start(), calls=%async_computation.2 | async-start | bytes 2703360 | tf_op jit(solution)/shard_map/all_gather | solution.py:21
  9.3 366.1 %all-gather.12.cloned.1.call-start = ((), (), s32[]{:S(2)}) async-start(), calls=%async_computation.4 | async-start | bytes 2703360 | tf_op jit(solution)/shard_map/all_gather | solution.py:23
  9.9 538.2 %reduce-scatter.4.cloned.1.call-start = ((), (), s32[]{:S(2)}) async-start(), calls=%async_computation.6 | async-start | bytes 2703360 | tf_op jit(solution)/shard_map/reduce_scatter | solution.py:70
  240.4 108.4 %copy-start.1 = (f32[256]{0:T(256)S(1)}, f32[256]{0:T(256)}, u32[]{:S(2)}) copy-start(f32[256]{0:T(256)} %param.13) | copy-start | bytes 3076
  240.5 108.5 %copy-start = (f32[256]{0:T(256)S(1)}, f32[256]{0:T(256)}, u32[]{:S(2)}) copy-start(f32[256]{0:T(256)} %param.12) | copy-start | bytes 3076
Sparse Core Ops, SparseCore 0:
  9.5 74.0 all-gather.13
  86.6 80.8 all-gather.5
  169.6 66.2 all-gather.9
  237.9 67.7 all-gather.7
  307.7 67.6 all-gather.11
  429.2 118.8 reduce-scatter.3
where the time goes:
time: 559 us; the launch traced here: 557 us
  waiting for transfers between devices  433 us (77%)
  blocking collectives  76.6 us (14%)
  matrix products  28.2 us (5%)
  between operations  13.6 us (2%)
    reduce_scatter x1, waiting for transfers between devices, on_device(): lax.psum_scatter(lax.dot_general(part, grad_query, (((0,), (0,)), ((), ()...  119 us
    all_gather x1, waiting for transfers between devices, on_device(): tokens = lax.all_gather(inputs, 'tensor', axis=2, tiled=True)[0]  83.9 us
    all_gather x1, waiting for transfers between devices, on_device(): lax.all_gather(tangent, 'dp', axis=0, tiled=True)  73.6 us
    all_gather x1, waiting for transfers between devices, on_device(): lax.all_gather(w_query, 'dp', axis=0, tiled=True)  65.3 us
    all_gather x1, waiting for transfers between devices, on_device(): lax.all_gather(w_key, 'dp', axis=0, tiled=True)  63.9 us
    psum x1, blocking collectives, on_device(): lax.psum((jnp.sum(query * query, axis=1), jnp.sum(key * key, axis=1)), 't...  38.6 us
    psum x1, blocking collectives, on_device(): back = lax.psum(jnp.sum(query * weighted, axis=1), 'tensor')  38 us
    all_gather x1, waiting for transfers between devices, on_device(): lax.all_gather(w_value, 'dp', axis=0, tiled=True)  24.3 us
  transfers between devices with their start and end apart: 6, of which 6 were waited for; matrix products, arithmetic and copies ran while one was open for 3% of the time, Pallas kernels for 0%

commit v1 on v0

v1 whole, which is shorter than its diff:
```python
import functools

import jax
import jax.numpy as jnp
from jax import lax
from jax.experimental import pallas as pl
from jax.experimental.pallas import tpu as pltpu
from jax.sharding import Mesh, PartitionSpec as P

HEADS = 32
HD = 128
EPS = 1e-06
BF = jnp.bfloat16
F32 = jnp.float32
VMEM_LIMIT = 48 * 1024 * 1024


def shift(value, axis, by, size):
    return lax.ppermute(value, axis, [(i, (i + by) % size) for i in range(size)])


def ring(block, axis, size):
    half = block.shape[0] // 2
    up, down = [block], []
    low, high = block, block
    for _ in range(size // 2 - 1):
        low, high = shift(low, axis, 1, size), shift(high, axis, -1, size)
        up.append(low)
        down.append(high)
    up.append(shift(low[:half], axis, 1, size))
    down.append(shift(high[half:], axis, -1, size))
    return up + down[::-1]


def project_kernel(place, xt_hbm, mine, theirs, qkd, value, stats, xr, acc, sem, *, wide, rows, chunk):
    k = pl.program_id(0)
    steps = pl.num_programs(0)
    half = steps // 2
    y, zl, c = place[0], place[1], place[2]

    @pl.when(k == 0)
    def _():
        for side in range(2):
            for i in range(8):
                for j in range(2):
                    source = lax.rem(y + 8 - i, 8) * 4 + lax.rem(zl + j, 2) * 2 + lax.rem(c + side, 2)
                    pltpu.make_async_copy(
                        xt_hbm.at[pl.ds(pl.multiple_of(source * rows, rows), rows), :],
                        xr.at[pl.ds((side * 16 + i * 2 + j) * rows, rows), :],
                        sem,
                    ).start()
        acc[...] = jnp.zeros_like(acc)
        pltpu.make_async_copy(xt_hbm, xr, sem).wait()

    x = xr[pl.ds(pl.multiple_of(k * chunk, chunk), chunk), :]

    @pl.when(k < half)
    def _():
        acc[...] += lax.dot_general(x, mine[...], (((0,), (0,)), ((), ())), preferred_element_type=F32)

    @pl.when(k >= half)
    def _():
        acc[...] += lax.dot_general(x, theirs[...], (((0,), (0,)), ((), ())), preferred_element_type=F32)

    @pl.when(k == steps - 1)
    def _():
        q, key, dq = acc[:, :wide], acc[:, wide : 2 * wide], acc[:, 2 * wide : 3 * wide]
        qkd[...] = acc[:, : 3 * wide]
        value[...] = acc[:, 3 * wide :].astype(BF)
        lane = lax.broadcasted_iota(jnp.int32, (q.shape[0], 128), 1)
        sums = [jnp.sum(t, axis=1, keepdims=True) for t in (q * q, key * key, q * dq)]
        packed = jnp.where(lane == 0, sums[0], jnp.where(lane == 1, sums[1], jnp.where(lane == 2, sums[2], 0.0)))
        stats[...] = packed.T[:8]


def project(place, xt, mine, theirs, wide):
    length = xt.shape[1]
    depth = mine.shape[0]
    rows = xt.shape[0] // 32
    chunk = 512
    half = depth // chunk
    return pl.pallas_call(
        functools.partial(project_kernel, wide=wide, rows=rows, chunk=chunk),
        grid=(2 * half,),
        in_specs=[
            pl.BlockSpec(memory_space=pltpu.SMEM),
            pl.BlockSpec(memory_space=pl.ANY),
            pl.BlockSpec((chunk, 4 * wide), lambda k: (jnp.minimum(k, half - 1), 0)),
            pl.BlockSpec((chunk, 4 * wide), lambda k: (jnp.maximum(k - half, 0), 0)),
        ],
        out_specs=[
            pl.BlockSpec((length, 3 * wide), lambda k: (0, 0)),
            pl.BlockSpec((length, wide), lambda k: (0, 0)),
            pl.BlockSpec((8, length), lambda k: (0, 0)),
        ],
        out_shape=[
            jax.ShapeDtypeStruct((length, 3 * wide), F32),
            jax.ShapeDtypeStruct((length, wide), BF),
            jax.ShapeDtypeStruct((8, length), F32),
        ],
        scratch_shapes=[
            pltpu.VMEM(xt.shape, BF),
            pltpu.VMEM((length, 4 * wide), F32),
            pltpu.SemaphoreType.DMA,
        ],
        compiler_params=pltpu.CompilerParams(vmem_limit_bytes=VMEM_LIMIT),
        name="project",
    )(place, xt, mine, theirs)


def columns(sums):
    full = jnp.concatenate([sums, jnp.zeros((120, sums.shape[1]), F32)], axis=0)
    return full.T


def attend_kernel(sums, qkd, value, gains, weighted, stats, *, wide, total):
    length = qkd.shape[0]
    scale = 1.0 / HD**0.5
    cols = columns(sums[...])
    rq = lax.rsqrt(cols[:, 0:1] / total + EPS)
    rk = lax.rsqrt(cols[:, 1:2] / total + EPS)
    tq = cols[:, 2:3] / total
    causal = lax.broadcasted_iota(jnp.int32, (length, length), 1) <= lax.broadcasted_iota(
        jnp.int32, (length, length), 0
    )
    nt = (((1,), (1,)), ((), ()))
    back = jnp.zeros((length, 1), F32)
    for h in range(wide // HD):
        at = slice(h * HD, (h + 1) * HD)
        q = qkd[:, h * HD : (h + 1) * HD]
        key = qkd[:, wide + h * HD : wide + (h + 1) * HD]
        dq = qkd[:, 2 * wide + h * HD : 2 * wide + (h + 1) * HD]
        v = value[:, at]
        gq, gk = gains[0:1, at], gains[1:2, at]
        qn = (gq * q * rq).astype(BF)
        kn = (gk * key * rk).astype(BF)
        dqn = (gq * rq * (dq - q * rq * rq * tq)).astype(BF)
        scores = lax.dot_general(qn, kn, nt, preferred_element_type=F32) * scale
        scores = jnp.where(causal, scores, -jnp.inf)
        expo = jnp.exp(scores - jnp.max(scores, axis=1, keepdims=True))
        probs = expo / jnp.sum(expo, axis=1, keepdims=True)
        ds = lax.dot_general(dqn, kn, nt, preferred_element_type=F32) * scale
        dpb = (probs * (ds - jnp.sum(probs * ds, axis=1, keepdims=True))).astype(BF)
        upper = jnp.dot(dpb, v, preferred_element_type=F32).astype(BF)
        gp = lax.dot_general(upper, v, nt, preferred_element_type=F32)
        gs = (probs * (gp - jnp.sum(probs * gp, axis=1, keepdims=True))).astype(BF)
        w = gq * (jnp.dot(gs, kn, preferred_element_type=F32) * scale)
        weighted[:, at] = w
        back += jnp.sum(q * w, axis=1, keepdims=True)
    lane = lax.broadcasted_iota(jnp.int32, (length, 128), 1)
    stats[...] = jnp.where(lane == 0, back, 0.0).T[:8]


def attend(sums, qkd, value, gains, wide, total):
    length = qkd.shape[0]
    return pl.pallas_call(
        functools.partial(attend_kernel, wide=wide, total=total),
        out_shape=[
            jax.ShapeDtypeStruct((length, wide), F32),
            jax.ShapeDtypeStruct((8, length), F32),
        ],
        compiler_params=pltpu.CompilerParams(vmem_limit_bytes=VMEM_LIMIT),
        name="attend",
    )(sums, qkd, value, gains)


def outer_kernel(place, sums, back, q, weighted, xt, keep, send, gq, *, total, rows):
    c = place[2]

    @pl.when(pl.program_id(0) == 0)
    def _():
        rq = lax.rsqrt(columns(sums[...])[:, 0:1] / total + EPS)
        tb = columns(back[...])[:, 0:1] / total
        gq[...] = (rq * weighted[...] - q[...] * rq * rq * rq * tb).astype(BF)

    term = jnp.dot(xt[...], gq[...], preferred_element_type=F32)
    for i in range(term.shape[0] // (2 * rows)):
        first = term[2 * i * rows : (2 * i + 1) * rows]
        second = term[(2 * i + 1) * rows : (2 * i + 2) * rows]
        keep[i * rows : (i + 1) * rows, :] = jnp.where(c == 0, first, second)
        send[i * rows : (i + 1) * rows, :] = jnp.where(c == 0, second, first).astype(BF)


def outer(place, sums, back, qkd, weighted, xt, total):
    depth, length = xt.shape
    wide = weighted.shape[1]
    steps = 4
    block = depth // steps
    return pl.pallas_call(
        functools.partial(outer_kernel, total=total, rows=depth // 32),
        grid=(steps,),
        in_specs=[
            pl.BlockSpec(memory_space=pltpu.SMEM),
            pl.BlockSpec((8, length), lambda k: (0, 0)),
            pl.BlockSpec((8, length), lambda k: (0, 0)),
            pl.BlockSpec((length, wide), lambda k: (0, 0)),
            pl.BlockSpec((length, wide), lambda k: (0, 0)),
            pl.BlockSpec((block, length), lambda k: (k, 0)),
        ],
        out_specs=[
            pl.BlockSpec((block // 2, wide), lambda k: (k, 0)),
            pl.BlockSpec((block // 2, wide), lambda k: (k, 0)),
        ],
        out_shape=[
            jax.ShapeDtypeStruct((depth // 2, wide), F32),
            jax.ShapeDtypeStruct((depth // 2, wide), BF),
        ],
        scratch_shapes=[pltpu.VMEM((length, wide), BF)],
        compiler_params=pltpu.CompilerParams(vmem_limit_bytes=VMEM_LIMIT),
        name="outer",
    )(place, sums, back, qkd, weighted, xt)


def sum_over_heads(stats, count):
    n = stats.shape[1]
    mine = stats[:count].reshape(1, count * n // 128, 128)
    got = lax.all_to_all(jnp.broadcast_to(mine, (16,) + mine.shape[1:]), ("x", "zh"), 0, 0, tiled=True)
    summed = jnp.sum(got, axis=0).reshape(count, n)
    return jnp.concatenate([summed, jnp.zeros((8 - count, n), F32)], axis=0)


def on_device(inputs, w_query, w_key, w_value, tangent, gain_query, gain_key):
    wide = w_query.shape[1]
    total = HEADS * HD
    place = jnp.stack([lax.axis_index("y"), lax.axis_index("zl"), lax.axis_index("c")]).astype(jnp.int32)

    weights = jnp.concatenate([w_query, w_key, tangent, w_value], axis=1)
    other = shift(weights, "zl", 1, 2)
    xt = lax.all_gather(inputs[0].T, "zh", axis=0, tiled=True)
    xt = lax.all_gather(xt, "x", axis=0, tiled=True)
    mine = jnp.concatenate(ring(jnp.concatenate([weights, other], axis=0), "y", 8), axis=0)
    theirs = shift(mine, "c", 1, 2)

    qkd, value, stats = project(place, xt, mine, theirs, wide)
    sums = sum_over_heads(stats, 3)
    gains = jnp.concatenate([gain_query[None], gain_key[None], jnp.zeros((6, wide), F32)], axis=0)
    weighted, stats = attend(sums, qkd, value, gains, wide, total)
    back = sum_over_heads(stats, 1)
    keep, send = outer(place, sums, back, qkd, weighted, xt, total)

    part = (keep + shift(send, "c", 1, 2).astype(F32)).astype(BF)
    got = lax.all_to_all(part.reshape(16, part.shape[0] // 16, wide), ("y", "zl"), 0, 0, tiled=True)
    return jnp.sum(got.astype(F32), axis=0)


def solution(mesh):
    fine = Mesh(mesh.devices.reshape(8, 2, 2, 4, 4), ("y", "zl", "c", "x", "zh"))
    dp, tensor = ("y", "zl", "c"), ("x", "zh")
    return jax.shard_map(
        on_device,
        mesh=fine,
        in_specs=(
            P(dp, None, tensor),
            P(dp, tensor),
            P(dp, tensor),
            P(dp, tensor),
            P(dp, tensor),
            P(tensor),
            P(tensor),
        ),
        out_specs=P(dp, tensor),
        check_vma=False,
    )
```

time: 559 us -> 260 us (0.47)
  waiting for transfers between devices: 433 us -> 66.8 us
  starting transfers between devices: 0.19 us -> 56.5 us
  matrix products: 28.2 us -> 0 us
  Pallas kernels: 0 us -> 23 us
  local copies, waits for them, and re-layouts: 2.59 us -> 19 us
    all_gather x5 -> x1, waiting for transfers between devices: 311 us -> 30.3 us  [on_device(): xt = lax.all_gather(xt, 'x', axis=0, tiled=True)]
    reduce_scatter x1 -> x0, waiting for transfers between devices: 119 us -> none  [on_device(): lax.psum_scatter(lax.dot_general(part, grad_query, (((0,), (0,)), ((), ()...]
    psum x2 -> x0, blocking collectives: 76.6 us -> none  [the longest x1 38.6 us: on_device(): lax.psum((jnp.sum(query * query, axis=1), jnp.sum(key * key, axis=1)), 't...]
    all_to_all x0 -> x2, blocking collectives: none -> 51.8 us  [the longest x1 40.3 us: on_device(): lax.all_to_all(part.reshape(16, part.shape[0] // 16, wide), ('y', 'zl'),...]
    ppermute x0 -> x11, starting transfers between devices: none -> 47.9 us  [shift(): lax.ppermute(value, axis, [(i, (i + by) % size) for i in range(size)])]
    dot_general x8 -> x0, matrix products: 27.6 us -> none  [the longest x4 18 us: on_device(): jnp.dot(part, piece, preferred_element_type=jnp.float32)]
    ppermute x0 -> x11, waiting for transfers between devices: none -> 26.8 us  [shift(): lax.ppermute(value, axis, [(i, (i + by) % size) for i in range(size)])]
    all_gather x0 -> x1, blocking collectives: none -> 26.1 us  [on_device(): xt = lax.all_gather(inputs[0].T, 'zh', axis=0, tiled=True)]
  transfers between devices with their start and end apart: 6 -> 13, of which waited for: 6 -> 7; matrix products, arithmetic and copies ran while one was open for 3% -> 4% of each run, Pallas kernels for 0% -> 0%
where the time goes in v1:
time: 260 us; the launch traced here: 258 us
  blocking collectives  77.9 us (30%)
  waiting for transfers between devices  66.8 us (26%)
  starting transfers between devices  56.5 us (22%)
  Pallas kernels  23 us (9%)
  local copies, waits for them, and re-layouts  19 us (7%)
  between operations  13.6 us (5%)
    ppermute x11, starting transfers between devices, shift(): lax.ppermute(value, axis, [(i, (i + by) % size) for i in range(size)])  47.9 us
    all_to_all x1, blocking collectives, on_device(): lax.all_to_all(part.reshape(16, part.shape[0] // 16, wide), ('y', 'zl'),...  40.3 us
    all_gather x1, waiting for transfers between devices, on_device(): xt = lax.all_gather(xt, 'x', axis=0, tiled=True)  30.3 us
    ppermute x11, waiting for transfers between devices, shift(): lax.ppermute(value, axis, [(i, (i + by) % size) for i in range(size)])  26.8 us
    all_gather x1, blocking collectives, on_device(): xt = lax.all_gather(inputs[0].T, 'zh', axis=0, tiled=True)  26.1 us
    pallas_call x1, Pallas kernels, project(): pl.pallas_call(functools.partial(project_kernel, wide=wide, rows=rows, ch...  16.3 us
    unnamed x20, local copies, waits for them, and re-layouts  15.8 us
    all_to_all x1, blocking collectives, sum_over_heads(): lax.all_to_all(jnp.broadcast_to(mine, (16,) + mine.shape[1:]), ('x', 'zh'...  11.5 us
  transfers between devices with their start and end apart: 13, of which 7 were waited for; matrix products, arithmetic and copies ran while one was open for 4% of the time, Pallas kernels for 0%

profile of v1, /device:TPU:1, one launch (start us, length us, event | category | flops | bytes accessed | tf_op | source)
XLA Modules:
  0.0 258.4 jit_solution(1453855667452301766)
XLA Ops:
  6.5 1.5 constant_dynamic-update-slice_fusion.3
  8.1 1.5 constant_dynamic-update-slice_fusion.2
  9.6 1.6 constant_dynamic-update-slice_fusion.1
  11.2 1.5 constant_dynamic-update-slice_fusion
  12.7 4.8 %collective-permute-start = (bf16[160,1024]{1,0:T(8,128)(2,1)S(1)}, bf16[160,1024]{1,0:T(8,128)(2,1)S(1)}, u32[]{:S(2)}, u32[]{:S(2)}) collective-permute-start(bf16[160,1024]{1,0:T(8,128)(2,1)S(1)} %get-tuple-element.19), channel_id=1, source_target_pairs={{0,32},{32,0},{1,33},{33,1},{2,34},{34,2},{3,35},{35,3},{4,36},{36... | collective-permute-start | bytes 983048 | tf_op jit(solution)/shard_map/ppermute | solution.py:19
  17.5 4.4 %collective-permute-done = bf16[160,1024]{1,0:T(8,128)(2,1)S(1)} collective-permute-done((bf16[160,1024]{1,0:T(8,128)(2,1)S(1)}, bf16[160,1024]{1,0:T(8,128)(2,1)S(1)}, u32[]{:S(2)}, u32[]{:S(2)}) %collective-permute-start) | collective-permute-done | bytes 327712 | tf_op jit(solution)/shard_map/ppermute | solution.py:19
  22.0 6.2 %collective-permute-start.1 = (bf16[320,1024]{1,0:T(8,128)(2,1)S(1)}, bf16[320,1024]{1,0:T(8,128)(2,1)S(1)}, u32[]{:S(2)}, u32[]{:S(2)}) collective-permute-start(bf16[320,1024]{1,0:T(8,128)(2,1)S(1)} %pad_maximum_fusion), channel_id=1, source_target_pairs={{0,64},{64,128},{128,192},{192,256},{256,320},{320,384},{384,448},... | collective-permute-start | bytes 1966088 | tf_op jit(solution)/shard_map/ppermute | solution.py:19
  28.2 3.8 %collective-permute-start.5 = (bf16[320,1024]{1,0:T(8,128)(2,1)S(1)}, bf16[320,1024]{1,0:T(8,128)(2,1)S(1)}, u32[]{:S(2)}, u32[]{:S(2)}) collective-permute-start(bf16[320,1024]{1,0:T(8,128)(2,1)S(1)} %pad_maximum_fusion), channel_id=1, source_target_pairs={{0,448},{64,0},{128,64},{192,128},{256,192},{320,256},{384,320},{4... | collective-permute-start | bytes 1966088 | tf_op jit(solution)/shard_map/ppermute | solution.py:19
  32.0 9.8 %collective-permute-done.1 = bf16[320,1024]{1,0:T(8,128)(2,1)S(1)} collective-permute-done((bf16[320,1024]{1,0:T(8,128)(2,1)S(1)}, bf16[320,1024]{1,0:T(8,128)(2,1)S(1)}, u32[]{:S(2)}, u32[]{:S(2)}) %collective-permute-start.1) | collective-permute-done | bytes 655392 | tf_op jit(solution)/shard_map/ppermute | solution.py:19
  41.8 2.5 collective-permute-start.2
  44.3 0.0 collective-permute-done.5
  44.3 4.6 %collective-permute-start.6 = (bf16[320,1024]{1,0:T(8,128)(2,1)S(1)}, bf16[320,1024]{1,0:T(8,128)(2,1)S(1)}, u32[]{:S(2)}, u32[]{:S(2)}) collective-permute-start(bf16[320,1024]{1,0:T(8,128)(2,1)S(1)} %collective-permute-done.5), channel_id=1, source_target_pairs={{0,448},{64,0},{128,64},{192,128},{256,192},{320,256},{384,320},{4... | collective-permute-start | bytes 1966088 | tf_op jit(solution)/shard_map/ppermute | solution.py:19
  48.9 9.6 %collective-permute-done.2 = bf16[320,1024]{1,0:T(8,128)(2,1)} collective-permute-done((bf16[320,1024]{1,0:T(8,128)(2,1)S(1)}, bf16[320,1024]{1,0:T(8,128)(2,1)}, u32[]{:S(2)}, u32[]{:S(2)}) %collective-permute-start.2) | collective-permute-done | bytes 655392 | tf_op jit(solution)/shard_map/ppermute | solution.py:19
  58.5 1.9 collective-permute-start.3
  60.4 0.0 collective-permute-done.6
  60.4 4.6 %collective-permute-start.7 = (bf16[320,1024]{1,0:T(8,128)(2,1)S(1)}, bf16[320,1024]{1,0:T(8,128)(2,1)S(1)}, u32[]{:S(2)}, u32[]{:S(2)}) collective-permute-start(bf16[320,1024]{1,0:T(8,128)(2,1)S(1)} %collective-permute-done.6), channel_id=1, source_target_pairs={{0,448},{64,0},{128,64},{192,128},{256,192},{320,256},{384,320},{4... | collective-permute-start | bytes 1966088 | tf_op jit(solution)/shard_map/ppermute | solution.py:19
  65.0 26.1 %all_gather.6 = bf16[1280,384]{1,0:T(8,128)(2,1)} all-gather(bf16[320,384]{1,0:T(8,128)(2,1)} %bitcast.16), channel_id=1, replica_groups=mesh['y'=8,'zl'=2,'c'=2,'x'=4,'zh'=4] {'zh'}, dimensions={0}, use_global_device_ids=true | all-gather | bytes 1228800 | tf_op jit(solution)/shard_map/all_gather | solution.py:229
  91.1 0.0 all-gather.2.cloned.1.call-update
  91.1 0.7 constant_dynamic-update-slice_fusion.12
  91.9 1.9 collective-permute-start.4
  93.9 2.0 constant_dynamic-update-slice_fusion.11
  95.9 4.6 %collective-permute-start.8 = (bf16[160,1024]{1,0:T(8,128)(2,1)S(1)}, bf16[160,1024]{1,0:T(8,128)(2,1)S(1)}, u32[]{:S(2)}, u32[]{:S(2)}) collective-permute-start(bf16[160,1024]{1,0:T(8,128)(2,1)S(1)} %slice.17), channel_id=1, source_target_pairs={{0,448},{64,0},{128,64},{192,128},{256,192},{320,256},{384,320},{4... | collective-permute-start | bytes 983048 | tf_op jit(solution)/shard_map/ppermute | solution.py:19
  100.4 2.0 constant_dynamic-update-slice_fusion.10
  102.4 0.9 constant_dynamic-update-slice_fusion.9
  103.3 0.8 constant_dynamic-update-slice_fusion.8
  104.1 0.4 collective-permute-done.8
  104.4 0.8 constant_dynamic-update-slice_fusion.7
  105.2 1.0 constant_dynamic-update-slice_fusion.6
  106.2 0.9 constant_dynamic-update-slice_fusion.5
  107.1 0.9 constant_dynamic-update-slice_fusion.4.mine
  108.0 8.2 %collective-permute-start.9 = (bf16[2560,1024]{1,0:T(8,128)(2,1)}, bf16[2560,1024]{1,0:T(8,128)(2,1)}, u32[]{:S(2)}, u32[]{:S(2)}) collective-permute-start(bf16[2560,1024]{1,0:T(8,128)(2,1)} %constant_dynamic-update-slice_fusion.4.mine), channel_id=1, source_target_pairs={{0,16},{16,0},{1,17},{17,1},{2,18},{18,2},{3,19},{19,3},{4,20},{20... | collective-permute-start | bytes 15728648 | tf_op jit(solution)/shard_map/ppermute | solution.py:19
  116.2 0.1 pad.4.clone
  116.2 0.1 pad_add_fusion.place
  116.3 30.3 %all-gather.2.cloned.1.call-done.xt_hbm.xt = bf16[5120,384]{1,0:T(8,128)(2,1)} async-done(((bf16[1280,384]{1,0:T(8,128)(2,1)}), bf16[5120,384]{1,0:T(8,128)(2,1)}) %all-gather.2.cloned.1.call-update) | async-done | bytes 3932176 | tf_op jit(solution)/shard_map/all_gather | solution.py:230
  146.6 2.1 copy-done
  148.7 16.3 %project.1 = (f32[384,768]{1,0:T(8,128)S(1)}, bf16[384,256]{1,0:T(8,128)(2,1)S(1)}, f32[8,384]{1,0:T(8,128)S(1)}) custom-call(s32[3]{0:T(128)S(1)} %pad_add_fusion.place, bf16[5120,384]{1,0:T(8,128)(2,1)S(1)} %copy-done, bf16[2560,1024]{1,0:T(8,128)(2,1)} %constant_dynamic-update-slice_fusion.4.mine, bf16[2560,1024]{1,0:T(8,128)(2,1)} %collective-permute-done.9.theirs), custom_call_target="tpu_custom_call" | custom-call | tf_op jit(solution)/shard_map/project/pallas_call | solution.py:82
  165.0 0.7 broadcast_in_dim.26
  165.7 8.7 %all-to-all-start = ((f32[16,9,128]{2,1,0:T(8,128)}), f32[16,9,128]{2,1,0:T(8,128)S(1)}, u32[]{:S(2)}, u32[]{:S(2)}) async-start(f32[16,9,128]{2,1,0:T(8,128)} %broadcast_in_dim.26), calls=%async_computation | async-start | bytes 262144 | tf_op jit(solution)/shard_map/all_to_all | solution.py:217
  174.4 0.1 maximum_maximum_fusion.gains
  174.4 9.8 %all-to-all-done = f32[16,9,128]{2,1,0:T(8,128)S(1)} async-done(((f32[16,9,128]{2,1,0:T(8,128)}), f32[16,9,128]{2,1,0:T(8,128)S(1)}, u32[]{:S(2)}, u32[]{:S(2)}) %all-to-all-start) | async-done | bytes 73760 | tf_op jit(solution)/shard_map/all_to_all | solution.py:217
  184.3 2.4 attend.1
  186.7 11.5 %all_to_all.15 = f32[16,3,128]{2,1,0:T(4,128)S(1)} all-to-all(f32[16,3,128]{2,1,0:T(4,128)S(1)} %broadcast_in_dim.31), channel_id=1, replica_groups=mesh['y'=8,'zl'=2,'c'=2,'x'=4,'zh'=4] {'x','zh'}, dimensions={0} | all-to-all | bytes 49152 | tf_op jit(solution)/shard_map/all_to_all | solution.py:217
  198.2 4.4 %outer.1 = (f32[2560,256]{1,0:T(8,128)S(1)}, bf16[2560,256]{1,0:T(8,128)(2,1)S(1)}) custom-call(s32[3]{0:T(128)S(1)} %pad_add_fusion.place, f32[8,384]{1,0:T(8,128)S(1)} %concatenate.22.sums, f32[8,384]{1,0:T(8,128)S(1)} %concatenate.24.back, f32[384,768]{1,0:T(8,128)S(1)} %get-tuple-element.13.qkd.q, f32[384,256]{1,0:T(8,128)S(1)} %get-tuple-element.16.weighted, ...), custom_call_target="tpu_custom_call" | custom-call | tf_op jit(solution)/shard_map/outer/pallas_call | solution.py:189
  202.6 4.8 %collective-permute-start.10 = (bf16[2560,256]{1,0:T(8,128)(2,1)S(1)}, bf16[2560,256]{1,0:T(8,128)(2,1)S(1)}, u32[]{:S(2)}, u32[]{:S(2)}) collective-permute-start(bf16[2560,256]{1,0:T(8,128)(2,1)S(1)} %get-tuple-element.18), channel_id=1, source_target_pairs={{0,16},{16,0},{1,17},{17,1},{2,18},{18,2},{3,19},{19,3},{4,20},{20... | collective-permute-start | bytes 3932168 | tf_op jit(solution)/shard_map/ppermute | solution.py:19
  207.4 2.6 %collective-permute-done.10 = bf16[2560,256]{1,0:T(8,128)(2,1)S(1)} collective-permute-done((bf16[2560,256]{1,0:T(8,128)(2,1)S(1)}, bf16[2560,256]{1,0:T(8,128)(2,1)S(1)}, u32[]{:S(2)}, u32[]{:S(2)}) %collective-permute-start.10) | collective-permute-done | bytes 1310752 | tf_op jit(solution)/shard_map/ppermute | solution.py:19
  210.1 0.4 add_convert_fusion
  210.5 40.3 %all_to_all.16 = bf16[16,160,256]{2,1,0:T(8,128)(2,1)S(1)} all-to-all(bf16[16,160,256]{2,1,0:T(8,128)(2,1)S(1)} %bitcast.15), channel_id=1, replica_groups=mesh['y'=8,'zl'=2,'c'=2,'x'=4,'zh'=4] {'y','zl'}, dimensions={0} | all-to-all | bytes 2621440 | tf_op jit(solution)/shard_map/all_to_all | solution.py:242
  250.8 0.8 convert_reduce_fusion
  (26 shorter events, 0.2 us)
Async XLA Ops:
  6.5 140.1 %all-gather.2.cloned.1.call-start = ((), (), s32[]{:S(2)}) async-start(), calls=%async_computation.3 | async-start | bytes 4915200 | tf_op jit(solution)/shard_map/all_gather | solution.py:230
  12.7 9.3 %collective-permute-start = (bf16[160,1024]{1,0:T(8,128)(2,1)S(1)}, bf16[160,1024]{1,0:T(8,128)(2,1)S(1)}, u32[]{:S(2)}, u32[]{:S(2)}) collective-permute-start(bf16[160,1024]{1,0:T(8,128)(2,1)S(1)} %get-tuple-element.19), channel_id=1, source_target_pairs={{0,32},{32,0},{1,33},{33,1},{2,34},{34,2},{3,35},{35,3},{4,36},{36... | collective-permute-start | bytes 983048 | tf_op jit(solution)/shard_map/ppermute | solution.py:19
  22.0 19.8 %collective-permute-start.1 = (bf16[320,1024]{1,0:T(8,128)(2,1)S(1)}, bf16[320,1024]{1,0:T(8,128)(2,1)S(1)}, u32[]{:S(2)}, u32[]{:S(2)}) collective-permute-start(bf16[320,1024]{1,0:T(8,128)(2,1)S(1)} %pad_maximum_fusion), channel_id=1, source_target_pairs={{0,64},{64,128},{128,192},{192,256},{256,320},{320,384},{384,448},... | collective-permute-start | bytes 1966088 | tf_op jit(solution)/shard_map/ppermute | solution.py:19
  28.2 16.1 %collective-permute-start.5 = (bf16[320,1024]{1,0:T(8,128)(2,1)S(1)}, bf16[320,1024]{1,0:T(8,128)(2,1)S(1)}, u32[]{:S(2)}, u32[]{:S(2)}) collective-permute-start(bf16[320,1024]{1,0:T(8,128)(2,1)S(1)} %pad_maximum_fusion), channel_id=1, source_target_pairs={{0,448},{64,0},{128,64},{192,128},{256,192},{320,256},{384,320},{4... | collective-permute-start | bytes 1966088 | tf_op jit(solution)/shard_map/ppermute | solution.py:19
  41.8 18.6 %copy-start.1 = (bf16[320,1024]{1,0:T(8,128)(2,1)}, bf16[320,1024]{1,0:T(8,128)(2,1)S(1)}, u32[]{:S(2)}) copy-start(bf16[320,1024]{1,0:T(8,128)(2,1)S(1)} %collective-permute-done.1) | copy-start | bytes 1966084
  41.8 16.7 %collective-permute-start.2 = (bf16[320,1024]{1,0:T(8,128)(2,1)S(1)}, bf16[320,1024]{1,0:T(8,128)(2,1)}, u32[]{:S(2)}, u32[]{:S(2)}) collective-permute-start(bf16[320,1024]{1,0:T(8,128)(2,1)S(1)} %collective-permute-done.1), channel_id=1, source_target_pairs={{0,64},{64,128},{128,192},{192,256},{256,320},{320,384},{384,448},... | collective-permute-start | bytes 1966088 | tf_op jit(solution)/shard_map/ppermute | solution.py:19
  44.3 16.1 %collective-permute-start.6 = (bf16[320,1024]{1,0:T(8,128)(2,1)S(1)}, bf16[320,1024]{1,0:T(8,128)(2,1)S(1)}, u32[]{:S(2)}, u32[]{:S(2)}) collective-permute-start(bf16[320,1024]{1,0:T(8,128)(2,1)S(1)} %collective-permute-done.5), channel_id=1, source_target_pairs={{0,448},{64,0},{128,64},{192,128},{256,192},{320,256},{384,320},{4... | collective-permute-start | bytes 1966088 | tf_op jit(solution)/shard_map/ppermute | solution.py:19
  58.5 33.4 %collective-permute-start.3 = (bf16[320,1024]{1,0:T(8,128)(2,1)}, bf16[320,1024]{1,0:T(8,128)(2,1)S(1)}, u32[]{:S(2)}, u32[]{:S(2)}) collective-permute-start(bf16[320,1024]{1,0:T(8,128)(2,1)} %collective-permute-done.2), channel_id=1, source_target_pairs={{0,64},{64,128},{128,192},{192,256},{256,320},{320,384},{384,448},... | collective-permute-start | bytes 1966088 | tf_op jit(solution)/shard_map/ppermute | solution.py:19
  60.4 35.4 %collective-permute-start.7 = (bf16[320,1024]{1,0:T(8,128)(2,1)S(1)}, bf16[320,1024]{1,0:T(8,128)(2,1)S(1)}, u32[]{:S(2)}, u32[]{:S(2)}) collective-permute-start(bf16[320,1024]{1,0:T(8,128)(2,1)S(1)} %collective-permute-done.6), channel_id=1, source_target_pairs={{0,448},{64,0},{128,64},{192,128},{256,192},{320,256},{384,320},{4... | collective-permute-start | bytes 1966088 | tf_op jit(solution)/shard_map/ppermute | solution.py:19
  91.9 11.4 %collective-permute-start.4 = (bf16[160,1024]{1,0:T(8,128)(2,1)S(1)}, bf16[160,1024]{1,0:T(8,128)(2,1)S(1)}, u32[]{:S(2)}, u32[]{:S(2)}) collective-permute-start(bf16[160,1024]{1,0:T(8,128)(2,1)S(1)} %slice.16), channel_id=1, source_target_pairs={{0,64},{64,128},{128,192},{192,256},{256,320},{320,384},{384,448},... | collective-permute-start | bytes 983048 | tf_op jit(solution)/shard_map/ppermute | solution.py:19
  95.9 8.6 %collective-permute-start.8 = (bf16[160,1024]{1,0:T(8,128)(2,1)S(1)}, bf16[160,1024]{1,0:T(8,128)(2,1)S(1)}, u32[]{:S(2)}, u32[]{:S(2)}) collective-permute-start(bf16[160,1024]{1,0:T(8,128)(2,1)S(1)} %slice.17), channel_id=1, source_target_pairs={{0,448},{64,0},{128,64},{192,128},{256,192},{320,256},{384,320},{4... | collective-permute-start | bytes 983048 | tf_op jit(solution)/shard_map/ppermute | solution.py:19
  108.0 38.6 %collective-permute-start.9 = (bf16[2560,1024]{1,0:T(8,128)(2,1)}, bf16[2560,1024]{1,0:T(8,128)(2,1)}, u32[]{:S(2)}, u32[]{:S(2)}) collective-permute-start(bf16[2560,1024]{1,0:T(8,128)(2,1)} %constant_dynamic-update-slice_fusion.4.mine), channel_id=1, source_target_pairs={{0,16},{16,0},{1,17},{17,1},{2,18},{18,2},{3,19},{19,3},{4,20},{20... | collective-permute-start | bytes 15728648 | tf_op jit(solution)/shard_map/ppermute | solution.py:19
  116.2 58.1 %copy-start.2 = (f32[256]{0:T(256)S(1)}, f32[256]{0:T(256)}, u32[]{:S(2)}) copy-start(f32[256]{0:T(256)} %param.13) | copy-start | bytes 3076
  116.2 58.1 %copy-start.3 = (f32[256]{0:T(256)S(1)}, f32[256]{0:T(256)}, u32[]{:S(2)}) copy-start(f32[256]{0:T(256)} %param.12) | copy-start | bytes 3076
  146.6 2.1 copy-start
  165.7 18.5 %all-to-all-start = ((f32[16,9,128]{2,1,0:T(8,128)}), f32[16,9,128]{2,1,0:T(8,128)S(1)}, u32[]{:S(2)}, u32[]{:S(2)}) async-start(f32[16,9,128]{2,1,0:T(8,128)} %broadcast_in_dim.26), calls=%async_computation | async-start | bytes 262144 | tf_op jit(solution)/shard_map/all_to_all | solution.py:217
  202.6 7.4 %collective-permute-start.10 = (bf16[2560,256]{1,0:T(8,128)(2,1)S(1)}, bf16[2560,256]{1,0:T(8,128)(2,1)S(1)}, u32[]{:S(2)}, u32[]{:S(2)}) collective-permute-start(bf16[2560,256]{1,0:T(8,128)(2,1)S(1)} %get-tuple-element.18), channel_id=1, source_target_pairs={{0,16},{16,0},{1,17},{17,1},{2,18},{18,2},{3,19},{19,3},{4,20},{20... | collective-permute-start | bytes 3932168 | tf_op jit(solution)/shard_map/ppermute | solution.py:19
Sparse Core Ops, SparseCore 0:
  91.3 55.2 all-gather.1

commit v2 on v1

v2 whole, which is shorter than its diff:
```python
import functools

import jax
import jax.numpy as jnp
from jax import lax
from jax.experimental import pallas as pl
from jax.experimental.pallas import tpu as pltpu
from jax.sharding import Mesh, PartitionSpec as P

HEADS = 32
HD = 128
EPS = 1e-06
BF = jnp.bfloat16
F32 = jnp.float32
Y = ("yh", "yl")
MIB = 1024 * 1024


def shift(value, axis, by, size):
    return lax.ppermute(value, axis, [(i, (i + by) % size) for i in range(size)])


def weight_ring(own, other):
    up, down = shift(own, Y, 1, 8), shift(own, Y, -1, 8)
    parts = [(own, 0, 4, 0, 0, 0), (other, 0, 4, 0, 1, 0), (up, 0, 4, 1, 0, 0), (down, 0, 4, 7, 0, 0)]
    up = shift(jnp.concatenate([up, other]), Y, 1, 8)
    down = shift(jnp.concatenate([other, down]), Y, -1, 8)
    parts += [(up, 0, 4, 2, 0, 0), (up, 4, 4, 1, 1, 0), (down, 0, 4, 7, 1, 0), (down, 4, 4, 6, 0, 0)]
    up, down = shift(up, Y, 1, 8), shift(down, Y, -1, 8)
    parts += [(up, 0, 4, 3, 0, 0), (up, 4, 4, 2, 1, 0), (down, 0, 4, 6, 1, 0), (down, 4, 4, 5, 0, 0)]
    up, down = shift(up[2:], Y, 1, 8), shift(down[:6], Y, -1, 8)
    parts += [(up, 0, 2, 4, 0, 2), (up, 2, 4, 3, 1, 0), (down, 0, 4, 5, 1, 0), (down, 4, 2, 4, 0, 0)]
    up, down = shift(up[4:], Y, 1, 8), shift(down[:2], Y, -1, 8)
    parts += [(up, 0, 2, 4, 1, 2), (down, 0, 2, 4, 1, 0)]
    return parts


def project_kernel(place, x_hbm, *refs, layout, which, wide, rows):
    count = max(entry[0] for entry in layout) + 1
    pieces = refs[:count]
    out, x, w, sem = refs[count:]
    length = out.shape[0]
    y, zl = place[0], place[1]
    groups = sem.shape[0]
    span = x.shape[0] // groups
    spots = {}
    for _, _, _, back, step, _ in layout:
        spots.setdefault((back, step), len(spots))
    for (back, step), spot in spots.items():
        source = lax.rem(y + 8 - back, 8) * 2 + lax.rem(zl + step, 2)
        at = pl.ds(spot * rows, rows)
        group = spot * rows // span
        pltpu.make_async_copy(
            x_hbm.at[pl.ds(pl.multiple_of(source * rows, rows), rows), pl.ds(which * length, length)],
            x.at[at, :],
            sem.at[group, 0],
        ).start()
        for piece, first, entries, b, s, weight in layout:
            if (b, s) == (back, step):
                pltpu.make_async_copy(
                    pieces[piece].at[pl.ds(first, entries)], w.at[pl.ds(weight, entries), at, :], sem.at[group, 1]
                ).start()
    for g in range(groups):
        at = pl.ds(g * span, span)
        pltpu.make_async_copy(x.at[at, :], x.at[at, :], sem.at[g, 0]).wait()
        pltpu.make_async_copy(w.at[:, at, :], w.at[:, at, :], sem.at[g, 1]).wait()
        for i in range(4):
            part = lax.dot_general(x[at, :], w[i, at, :], (((0,), (0,)), ((), ())), preferred_element_type=F32)
            cols = slice(i * wide, (i + 1) * wide)
            out[:, cols] = part if g == 0 else out[:, cols] + part


def project(place, x, parts, which, wide):
    depth, length = x.shape[0], x.shape[1] // 2
    arrays = []
    layout = []
    for array, *rest in parts:
        known = [i for i, other in enumerate(arrays) if other is array]
        if not known:
            arrays.append(array)
        layout.append((known[0] if known else len(arrays) - 1, *rest))
    return pl.pallas_call(
        functools.partial(project_kernel, layout=tuple(layout), which=which, wide=wide, rows=depth // 16),
        in_specs=[pl.BlockSpec(memory_space=pltpu.SMEM)]
        + [pl.BlockSpec(memory_space=pl.ANY)] * (1 + len(arrays)),
        out_shape=jax.ShapeDtypeStruct((length, 4 * wide), F32),
        scratch_shapes=[
            pltpu.VMEM((depth, length), BF),
            pltpu.VMEM((4, depth, wide), BF),
            pltpu.SemaphoreType.DMA((4, 2)),
        ],
        compiler_params=pltpu.CompilerParams(vmem_limit_bytes=44 * MIB),
        cost_estimate=pl.CostEstimate(
            flops=2 * length * depth * 4 * wide, bytes_accessed=2 * depth * (length + 4 * wide), transcendentals=0
        ),
        name="project",
    )(place, x, *arrays)


def merge_kernel(one, two, qkd, value, stats, *, wide):
    whole = [one[:, i * wide : (i + 1) * wide] + two[:, i * wide : (i + 1) * wide] for i in range(4)]
    for i in range(3):
        qkd[:, i * wide : (i + 1) * wide] = whole[i]
    value[...] = whole[3].astype(BF)
    q, key, dq = whole[:3]
    lane = lax.broadcasted_iota(jnp.int32, (q.shape[0], 128), 1)
    sums = [jnp.sum(t, axis=1, keepdims=True) for t in (q * q, key * key, q * dq)]
    packed = jnp.where(lane == 0, sums[0], jnp.where(lane == 1, sums[1], jnp.where(lane == 2, sums[2], 0.0)))
    stats[...] = packed.T[:8]


def merge(one, two, wide):
    length = one.shape[0]
    return pl.pallas_call(
        functools.partial(merge_kernel, wide=wide),
        out_shape=[
            jax.ShapeDtypeStruct((length, 3 * wide), F32),
            jax.ShapeDtypeStruct((length, wide), BF),
            jax.ShapeDtypeStruct((8, length), F32),
        ],
        compiler_params=pltpu.CompilerParams(vmem_limit_bytes=16 * MIB),
        name="merge",
    )(one, two)


def columns(sums):
    full = jnp.concatenate([sums, jnp.zeros((128 - sums.shape[0], sums.shape[1]), F32)], axis=0)
    return full.T


def attend_kernel(sums, qkd, value, gains, weighted, stats, *, wide, total):
    length = qkd.shape[0]
    scale = 1.0 / HD**0.5
    cols = columns(sums[...])
    rq = lax.rsqrt(cols[:, 0:1] / total + EPS)
    rk = lax.rsqrt(cols[:, 1:2] / total + EPS)
    tq = cols[:, 2:3] / total
    causal = lax.broadcasted_iota(jnp.int32, (length, length), 1) <= lax.broadcasted_iota(
        jnp.int32, (length, length), 0
    )
    nt = (((1,), (1,)), ((), ()))
    back = jnp.zeros((length, 1), F32)
    for h in range(wide // HD):
        at = slice(h * HD, (h + 1) * HD)
        q = qkd[:, h * HD : (h + 1) * HD]
        key = qkd[:, wide + h * HD : wide + (h + 1) * HD]
        dq = qkd[:, 2 * wide + h * HD : 2 * wide + (h + 1) * HD]
        v = value[:, at]
        gq, gk = gains[0:1, at], gains[1:2, at]
        qn = (gq * q * rq).astype(BF)
        kn = (gk * key * rk).astype(BF)
        dqn = (gq * rq * (dq - q * rq * rq * tq)).astype(BF)
        scores = lax.dot_general(qn, kn, nt, preferred_element_type=F32) * scale
        scores = jnp.where(causal, scores, -jnp.inf)
        expo = jnp.exp(scores - jnp.max(scores, axis=1, keepdims=True))
        probs = expo / jnp.sum(expo, axis=1, keepdims=True)
        ds = lax.dot_general(dqn, kn, nt, preferred_element_type=F32) * scale
        dpb = (probs * (ds - jnp.sum(probs * ds, axis=1, keepdims=True))).astype(BF)
        upper = jnp.dot(dpb, v, preferred_element_type=F32).astype(BF)
        gp = lax.dot_general(upper, v, nt, preferred_element_type=F32)
        gs = (probs * (gp - jnp.sum(probs * gp, axis=1, keepdims=True))).astype(BF)
        w = gq * (jnp.dot(gs, kn, preferred_element_type=F32) * scale)
        weighted[:, at] = w
        back += jnp.sum(q * w, axis=1, keepdims=True)
    lane = lax.broadcasted_iota(jnp.int32, (length, 128), 1)
    stats[...] = jnp.where(lane == 0, back, 0.0).T[:8]


def attend(sums, qkd, value, gains, wide, total):
    length = qkd.shape[0]
    return pl.pallas_call(
        functools.partial(attend_kernel, wide=wide, total=total),
        out_shape=[
            jax.ShapeDtypeStruct((length, wide), F32),
            jax.ShapeDtypeStruct((8, length), F32),
        ],
        compiler_params=pltpu.CompilerParams(vmem_limit_bytes=16 * MIB),
        name="attend",
    )(sums, qkd, value, gains)


def grad_kernel(sums, back, qkd, weighted, gq, *, wide, total):
    rq = lax.rsqrt(columns(sums[...])[:, 0:1] / total + EPS)
    tb = columns(back[...])[:, 0:1] / total
    gq[...] = (rq * weighted[...] - qkd[:, :wide] * rq * rq * rq * tb).astype(BF)


def grad(sums, back, qkd, weighted, total):
    length, wide = weighted.shape
    return pl.pallas_call(
        functools.partial(grad_kernel, wide=wide, total=total),
        out_shape=jax.ShapeDtypeStruct((length, wide), BF),
        name="grad",
    )(sums, back, qkd, weighted)


def outer_kernel(place, x, near, gq, gq_core, gq_near, gq_near_core, term):
    length = gq.shape[0]
    for i in range(x.shape[0]):
        total = jnp.dot(x[i, 0, :, :length], gq[...], preferred_element_type=F32)
        total += jnp.dot(x[i, 0, :, length:], gq_core[...], preferred_element_type=F32)
        total += jnp.dot(near[i, :, :length], gq_near[...], preferred_element_type=F32)
        total += jnp.dot(near[i, :, length:], gq_near_core[...], preferred_element_type=F32)
        term[i] = total.astype(BF)


def outer(place, x, near, grads):
    _, _, rows, tokens = x.shape
    length, wide = grads[0].shape
    steps = 2
    block = 4 // steps
    return pl.pallas_call(
        outer_kernel,
        grid_spec=pltpu.PrefetchScalarGridSpec(
            num_scalar_prefetch=1,
            grid=(steps,),
            in_specs=[
                pl.BlockSpec((block, 1, rows, tokens), lambda k, place: (k, lax.rem(place[0], 2), 0, 0)),
                pl.BlockSpec((block, rows, tokens), lambda k, place: (k, 0, 0)),
            ]
            + [pl.BlockSpec((length, wide), lambda k, place: (0, 0))] * 4,
            out_specs=pl.BlockSpec((block, rows, wide), lambda k, place: (k, 0, 0)),
        ),
        out_shape=jax.ShapeDtypeStruct((4, rows, wide), BF),
        compiler_params=pltpu.CompilerParams(vmem_limit_bytes=20 * MIB),
        cost_estimate=pl.CostEstimate(
            flops=16 * rows * tokens * wide, bytes_accessed=16 * rows * tokens, transcendentals=0
        ),
        name="outer",
    )(place, x, near, *grads)


def sum_over_heads(stats, count):
    n = stats.shape[1]
    mine = stats[:count].reshape(1, count * n // 128, 128)
    got = lax.all_to_all(jnp.broadcast_to(mine, (16,) + mine.shape[1:]), ("x", "zh"), 0, 0, tiled=True)
    return jnp.sum(got, axis=0).reshape(count, n)


def on_device(inputs, w_query, w_key, w_value, tangent, gain_query, gain_key):
    wide = w_query.shape[1]
    total = HEADS * HD
    place = jnp.stack([lax.axis_index(Y), lax.axis_index("zl")]).astype(jnp.int32)
    core = lax.axis_index("c")
    tie = lax.optimization_barrier

    halves = inputs[0].T.reshape(2, inputs.shape[2] // 2, inputs.shape[1])
    kept = lax.dynamic_index_in_dim(halves, core, 0, keepdims=False)
    given = lax.dynamic_index_in_dim(halves, 1 - core, 0, keepdims=False)
    x = jnp.concatenate([kept, shift(given, "c", 1, 2)], axis=1)
    x = lax.all_gather(x, ("x", "zh"), axis=0, tiled=True)

    weights = jnp.stack([w_query, w_key, tangent, w_value])
    parts = weight_ring(weights, shift(weights, "zl", 1, 2))
    x, *last = tie((x, parts[-1][0], parts[-2][0]))
    parts[-1], parts[-2] = (last[0], *parts[-1][1:]), (last[1], *parts[-2][1:])

    theirs = project(place, x, parts, 1, wide)
    x, theirs = tie((x, theirs))
    fine = x.reshape(4, 2, x.shape[0] // 8, x.shape[1])
    theirs = shift(theirs, "c", 1, 2)
    near = shift(lax.dynamic_index_in_dim(fine, 1 - lax.axis_index("yl"), 1, keepdims=False), "yl", 1, 2)
    qkd, value, stats = merge(project(place, x, parts, 0, wide), theirs, wide)
    sums = sum_over_heads(stats, 3)
    weighted, stats = attend(sums, qkd, value, jnp.stack([gain_query, gain_key]), wide, total)
    back = sum_over_heads(stats, 1)
    gq = grad(sums, back, qkd, weighted, total)

    gq_near = shift(gq, "yl", 1, 2)
    gq_core = shift(gq, "c", 1, 2)
    term = outer(place, fine, near, (gq, gq_core, gq_near, shift(gq_near, "c", 1, 2)))
    got = lax.all_to_all(term.reshape(8, -1, wide), ("yh", "zl"), 0, 0, tiled=True)
    return jnp.sum(got.astype(F32), axis=0)


def solution(mesh):
    fine = Mesh(mesh.devices.reshape(4, 2, 2, 2, 4, 4), ("yh", "yl", "zl", "c", "x", "zh"))
    dp, tensor = ("yh", "yl", "zl", "c"), ("x", "zh")
    return jax.shard_map(
        on_device,
        mesh=fine,
        in_specs=(
            P(dp, None, tensor),
            P(dp, tensor),
            P(dp, tensor),
            P(dp, tensor),
            P(dp, tensor),
            P(tensor),
            P(tensor),
        ),
        out_specs=P(dp, tensor),
        check_vma=False,
    )
```

time: 260 us -> 214 us (0.82)
  blocking collectives: 77.9 us -> 36.1 us
  starting transfers between devices: 56.5 us -> 68.7 us
  waiting for transfers between devices: 66.8 us -> 55 us
  local copies, waits for them, and re-layouts: 19 us -> 15.5 us
    all_gather x1 -> x0, blocking collectives: 26.1 us -> none  [on_device(): xt = lax.all_gather(inputs[0].T, 'zh', axis=0, tiled=True)]
    all_gather x1, waiting for transfers between devices: 30.3 us -> 6.01 us  [on_device(): x = lax.all_gather(x, ('x', 'zh'), axis=0, tiled=True)]
    all_to_all x1, blocking collectives: 40.3 us -> 24.3 us  [on_device(): lax.all_to_all(term.reshape(8, -1, wide), ('yh', 'zl'), 0, 0, tiled=True)]
    ppermute x11 -> x17, waiting for transfers between devices: 26.8 us -> 38.7 us  [shift(): lax.ppermute(value, axis, [(i, (i + by) % size) for i in range(size)])]
    ppermute x11 -> x17, starting transfers between devices: 47.9 us -> 59.8 us  [shift(): lax.ppermute(value, axis, [(i, (i + by) % size) for i in range(size)])]
    unnamed x20 -> x33, local copies, waits for them, and re-layouts: 15.8 us -> 9.2 us
    squeeze x0 -> x2, local copies, waits for them, and re-layouts: none -> 4.1 us  [the longest x1 3.12 us: on_device(): lax.dynamic_index_in_dim(fine, 1 - lax.axis_index('yl'), 1, keepdims=False)]
    pallas_call x2 -> x5, Pallas kernels: 20.7 us -> 18.3 us  [the longest x2 10.6 us: project(): pl.pallas_call(functools.partial(project_kernel, layout=tuple(layout), wh...]
  transfers between devices with their start and end apart: 13 -> 19, of which waited for: 7 -> 11; matrix products, arithmetic and copies ran while one was open for 4% -> 3% of each run, Pallas kernels for 0% -> 5%
where the time goes in v2:
time: 214 us; the launch traced here: 213 us
  starting transfers between devices  68.7 us (32%)
  waiting for transfers between devices  55 us (26%)
  blocking collectives  36.1 us (17%)
  Pallas kernels  20.6 us (10%)
  local copies, waits for them, and re-layouts  15.5 us (7%)
  between operations  13.8 us (6%)
  other arithmetic  2.76 us (1%)
    ppermute x17, starting transfers between devices, shift(): lax.ppermute(value, axis, [(i, (i + by) % size) for i in range(size)])  59.8 us
    ppermute x17, waiting for transfers between devices, shift(): lax.ppermute(value, axis, [(i, (i + by) % size) for i in range(size)])  38.7 us
    all_to_all x1, blocking collectives, on_device(): lax.all_to_all(term.reshape(8, -1, wide), ('yh', 'zl'), 0, 0, tiled=True)  24.3 us
    all_to_all x1, blocking collectives, sum_over_heads(): lax.all_to_all(jnp.broadcast_to(mine, (16,) + mine.shape[1:]), ('x', 'zh'...  11.9 us
    pallas_call x2, Pallas kernels, project(): pl.pallas_call(functools.partial(project_kernel, layout=tuple(layout), wh...  10.6 us
    all_to_all x1, waiting for transfers between devices, sum_over_heads(): lax.all_to_all(jnp.broadcast_to(mine, (16,) + mine.shape[1:]), ('x', 'zh'...  10.3 us
    unnamed x33, local copies, waits for them, and re-layouts  9.2 us
    all_to_all x1, starting transfers between devices, sum_over_heads(): lax.all_to_all(jnp.broadcast_to(mine, (16,) + mine.shape[1:]), ('x', 'zh'...  8.94 us
  transfers between devices with their start and end apart: 19, of which 11 were waited for; matrix products, arithmetic and copies ran while one was open for 3% of the time, Pallas kernels for 5%

profile of v2, /device:TPU:1, one launch (start us, length us, event | category | flops | bytes accessed | tf_op | source)
XLA Modules:
  0.0 212.6 jit_solution(433630419670776608)
XLA Ops:
  6.5 1.0 dynamic-slice_bitcast_fusion.2
  7.5 8.8 %collective-permute-start = (bf16[160,384]{1,0:T(8,128)(2,1)S(1)}, bf16[160,384]{1,0:T(8,128)(2,1)S(1)}, u32[]{:S(2)}, u32[]{:S(2)}) collective-permute-start(bf16[160,384]{1,0:T(8,128)(2,1)S(1)} %get-tuple-element.28), channel_id=1, source_target_pairs={{0,16},{16,0},{1,17},{17,1},{2,18},{18,2},{3,19},{19,3},{4,20},{20... | collective-permute-start | bytes 368648 | tf_op jit(solution)/shard_map/ppermute | solution.py:20
  16.3 1.0 collective-permute-done
  18.0 1.1 pad_maximum_fusion.2.refs_0_
  19.1 1.9 collective-permute-start.1
  21.0 1.9 collective-permute-start.2
  22.9 3.4 %collective-permute-start.7 = (bf16[4,160,256]{2,1,0:T(8,128)(2,1)S(1)}, bf16[4,160,256]{2,1,0:T(8,128)(2,1)S(1)}, u32[]{:S(2)}, u32[]{:S(2)}) collective-permute-start(bf16[4,160,256]{2,1,0:T(8,128)(2,1)S(1)} %pad_maximum_fusion.2.refs_0_), channel_id=1, source_target_pairs={{0,64},{64,128},{128,192},{192,256},{256,320},{320,384},{384,448},... | collective-permute-start | bytes 983048 | tf_op jit(solution)/shard_map/ppermute | solution.py:20
  26.3 3.6 %collective-permute-done.1.refs_1_ = bf16[4,160,256]{2,1,0:T(8,128)(2,1)S(1)} collective-permute-done((bf16[4,160,256]{2,1,0:T(8,128)(2,1)S(1)}, bf16[4,160,256]{2,1,0:T(8,128)(2,1)S(1)}, u32[]{:S(2)}, u32[]{:S(2)}) %collective-permute-start.1) | collective-permute-done | bytes 327712 | tf_op jit(solution)/shard_map/ppermute | solution.py:20
  29.9 1.9 collective-permute-done.2.refs_3_
  31.8 2.6 %collective-permute-done.7.refs_2_ = bf16[4,160,256]{2,1,0:T(8,128)(2,1)S(1)} collective-permute-done((bf16[4,160,256]{2,1,0:T(8,128)(2,1)S(1)}, bf16[4,160,256]{2,1,0:T(8,128)(2,1)S(1)}, u32[]{:S(2)}, u32[]{:S(2)}) %collective-permute-start.7) | collective-permute-done | bytes 327712 | tf_op jit(solution)/shard_map/ppermute | solution.py:20
  34.6 2.3 %collective-permute-start.8 = (bf16[8,160,256]{2,1,0:T(8,128)(2,1)S(1)}, bf16[8,160,256]{2,1,0:T(8,128)(2,1)S(1)}, u32[]{:S(2)}, u32[]{:S(2)}) collective-permute-start(bf16[8,160,256]{2,1,0:T(8,128)(2,1)S(1)} %get-tuple-element.25), channel_id=1, source_target_pairs={{0,64},{64,128},{128,192},{192,256},{256,320},{320,384},{384,448},... | collective-permute-start | bytes 1966088 | tf_op jit(solution)/shard_map/ppermute | solution.py:20
  36.9 4.2 %collective-permute-start.3 = (bf16[8,160,256]{2,1,0:T(8,128)(2,1)S(1)}, bf16[8,160,256]{2,1,0:T(8,128)(2,1)S(1)}, u32[]{:S(2)}, u32[]{:S(2)}) collective-permute-start(bf16[8,160,256]{2,1,0:T(8,128)(2,1)S(1)} %get-tuple-element.26), channel_id=1, source_target_pairs={{0,448},{64,0},{128,64},{192,128},{256,192},{320,256},{384,320},{4... | collective-permute-start | bytes 1966088 | tf_op jit(solution)/shard_map/ppermute | solution.py:20
  41.1 11.1 %collective-permute-done.8.refs_4_ = bf16[8,160,256]{2,1,0:T(8,128)(2,1)S(1)} collective-permute-done((bf16[8,160,256]{2,1,0:T(8,128)(2,1)S(1)}, bf16[8,160,256]{2,1,0:T(8,128)(2,1)S(1)}, u32[]{:S(2)}, u32[]{:S(2)}) %collective-permute-start.8) | collective-permute-done | bytes 655392 | tf_op jit(solution)/shard_map/ppermute | solution.py:20
  52.2 1.9 collective-permute-start.9
  54.1 0.8 copy-done.5
  55.0 4.6 %collective-permute-start.4 = (bf16[8,160,256]{2,1,0:T(8,128)(2,1)S(1)}, bf16[8,160,256]{2,1,0:T(8,128)(2,1)S(1)}, u32[]{:S(2)}, u32[]{:S(2)}) collective-permute-start(bf16[8,160,256]{2,1,0:T(8,128)(2,1)S(1)} %collective-permute-done.3.refs_5_), channel_id=1, source_target_pairs={{0,448},{64,0},{128,64},{192,128},{256,192},{320,256},{384,320},{4... | collective-permute-start | bytes 1966088 | tf_op jit(solution)/shard_map/ppermute | solution.py:20
  59.5 9.5 %collective-permute-done.9.refs_6_ = bf16[8,160,256]{2,1,0:T(8,128)(2,1)S(1)} collective-permute-done((bf16[8,160,256]{2,1,0:T(8,128)(2,1)S(1)}, bf16[8,160,256]{2,1,0:T(8,128)(2,1)S(1)}, u32[]{:S(2)}, u32[]{:S(2)}) %collective-permute-start.9) | collective-permute-done | bytes 655392 | tf_op jit(solution)/shard_map/ppermute | solution.py:20
  69.1 1.9 collective-permute-start.10
  71.0 5.1 %collective-permute-start.5 = (bf16[6,160,256]{2,1,0:T(8,128)(2,1)S(1)}, bf16[6,160,256]{2,1,0:T(8,128)(2,1)S(1)}, u32[]{:S(2)}, u32[]{:S(2)}) collective-permute-start(bf16[6,160,256]{2,1,0:T(8,128)(2,1)S(1)} %slice.24), channel_id=1, source_target_pairs={{0,448},{64,0},{128,64},{192,128},{256,192},{320,256},{384,320},{4... | collective-permute-start | bytes 1474568 | tf_op jit(solution)/shard_map/ppermute | solution.py:20
  76.1 5.4 %collective-permute-done.10.refs_8_ = bf16[6,160,256]{2,1,0:T(8,128)(2,1)S(1)} collective-permute-done((bf16[6,160,256]{2,1,0:T(8,128)(2,1)S(1)}, bf16[6,160,256]{2,1,0:T(8,128)(2,1)S(1)}, u32[]{:S(2)}, u32[]{:S(2)}) %collective-permute-start.10) | collective-permute-done | bytes 491552 | tf_op jit(solution)/shard_map/ppermute | solution.py:20
  82.2 1.9 collective-permute-start.11
  84.8 0.8 copy-done.2
  85.7 4.6 %collective-permute-start.6 = (bf16[2,160,256]{2,1,0:T(8,128)(2,1)}, bf16[2,160,256]{2,1,0:T(8,128)(2,1)S(1)}, u32[]{:S(2)}, u32[]{:S(2)}) collective-permute-start(bf16[2,160,256]{2,1,0:T(8,128)(2,1)} %slice.25), channel_id=1, source_target_pairs={{0,448},{64,0},{128,64},{192,128},{256,192},{320,256},{384,320},{4... | collective-permute-start | bytes 491528 | tf_op jit(solution)/shard_map/ppermute | solution.py:20
  90.3 2.5 %collective-permute-done.6.refs_11_ = bf16[2,160,256]{2,1,0:T(8,128)(2,1)S(1)} collective-permute-done((bf16[2,160,256]{2,1,0:T(8,128)(2,1)}, bf16[2,160,256]{2,1,0:T(8,128)(2,1)S(1)}, u32[]{:S(2)}, u32[]{:S(2)}) %collective-permute-start.6) | collective-permute-done | bytes 163872 | tf_op jit(solution)/shard_map/ppermute | solution.py:20
  92.8 6.0 %all-gather.2.cloned.1.call-done.x_hbm = bf16[2560,768]{1,0:T(8,128)(2,1)} async-done(((bf16[160,768]{1,0:T(8,128)(2,1)}), bf16[2560,768]{1,0:T(8,128)(2,1)}) %all-gather.2.cloned.1.call-update) | async-done | bytes 3932176 | tf_op jit(solution)/shard_map/all_gather | solution.py:251
  98.8 1.0 copy-done.3
  99.8 1.1 copy-done.6
  100.9 1.1 copy-done.9
  102.0 5.9 %project.2 = f32[384,1024]{1,0:T(8,128)} custom-call(s32[2]{0:T(128)S(1)} %pad_add_fusion.place, bf16[2560,768]{1,0:T(8,128)(2,1)} %all-gather.2.cloned.1.call-done.x_hbm, bf16[4,160,256]{2,1,0:T(8,128)(2,1)S(1)} %pad_maximum_fusion.2.refs_0_, bf16[4,160,256]{2,1,0:T(8,128)(2,1)S(1)} %collective-permute-done.1.refs_1_, ...), custom_call_target="tpu_custom_call" | custom-call | flops 2013265920 | bytes 7208960 | tf_op jit(solution)/shard_map/project/pallas_call | solution.py:82
  107.9 2.6 %collective-permute-start.13 = (f32[384,1024]{1,0:T(8,128)}, f32[384,1024]{1,0:T(8,128)}, u32[]{:S(2)}, u32[]{:S(2)}) collective-permute-start(f32[384,1024]{1,0:T(8,128)} %project.2), channel_id=1, source_target_pairs={{0,16},{16,0},{1,17},{17,1},{2,18},{18,2},{3,19},{19,3},{4,20},{20... | collective-permute-start | bytes 4718600 | tf_op jit(solution)/shard_map/ppermute | solution.py:20
  110.6 3.1 %dynamic-slice_bitcast_fusion = bf16[4,320,768]{2,1,0:T(8,128)(2,1)} fusion(bf16[4,2,320,768]{3,2,1,0:T(8,128)(2,1)} %bitcast.27, s32[]{:T(128)S(6)} %select_n.13), kind=kLoop, calls=%fused_computation | loop fusion | bytes 3932164 | tf_op jit(solution)/shard_map/jit(dynamic_index_in_dim)/squeeze | solution.py:262
  113.7 3.1 %collective-permute-start.12 = (bf16[4,320,768]{2,1,0:T(8,128)(2,1)}, bf16[4,320,768]{2,1,0:T(8,128)(2,1)}, u32[]{:S(2)}, u32[]{:S(2)}) collective-permute-start(bf16[4,320,768]{2,1,0:T(8,128)(2,1)} %dynamic-slice_bitcast_fusion), channel_id=1, source_target_pairs={{0,64},{64,0},{1,65},{65,1},{2,66},{66,2},{3,67},{67,3},{4,68},{68... | collective-permute-start | bytes 5898248 | tf_op jit(solution)/shard_map/ppermute | solution.py:20
  116.8 4.7 %project.3.one = f32[384,1024]{1,0:T(8,128)S(1)} custom-call(s32[2]{0:T(128)S(1)} %pad_add_fusion.place, bf16[2560,768]{1,0:T(8,128)(2,1)} %all-gather.2.cloned.1.call-done.x_hbm, bf16[4,160,256]{2,1,0:T(8,128)(2,1)S(1)} %pad_maximum_fusion.2.refs_0_, bf16[4,160,256]{2,1,0:T(8,128)(2,1)S(1)} %collective-permute-done.1.refs_1_, ...), custom_call_target="tpu_custom_call" | custom-call | flops 2013265920 | bytes 7208960 | tf_op jit(solution)/shard_map/project/pallas_call | solution.py:82
  121.6 1.8 merge.1
  123.4 0.8 broadcast_in_dim.15
  124.2 8.9 %all-to-all-start = ((f32[16,9,128]{2,1,0:T(8,128)}), f32[16,9,128]{2,1,0:T(8,128)S(1)}, u32[]{:S(2)}, u32[]{:S(2)}) async-start(f32[16,9,128]{2,1,0:T(8,128)} %broadcast_in_dim.15), calls=%async_computation | async-start | bytes 262144 | tf_op jit(solution)/shard_map/all_to_all | solution.py:236
  133.1 10.3 %all-to-all-done = f32[16,9,128]{2,1,0:T(8,128)S(1)} async-done(((f32[16,9,128]{2,1,0:T(8,128)}), f32[16,9,128]{2,1,0:T(8,128)S(1)}, u32[]{:S(2)}, u32[]{:S(2)}) %all-to-all-start) | async-done | bytes 73760 | tf_op jit(solution)/shard_map/all_to_all | solution.py:236
  143.5 2.3 %attend.1 = (f32[384,256]{1,0:T(8,128)S(1)}, f32[8,384]{1,0:T(8,128)S(1)}) custom-call(f32[3,384]{1,0:T(4,128)S(1)} %reshape.21.sums, f32[384,768]{1,0:T(8,128)S(1)} %get-tuple-element.21.qkd, bf16[384,256]{1,0:T(8,128)(2,1)S(1)} %get-tuple-element.22.value, f32[2,256]{1,0:T(2,128)S(1)} %pad_maximum_fusion.4.gains), custom_call_target="tpu_custom_call" | custom-call | tf_op jit(solution)/shard_map/attend/pallas_call | solution.py:171
  146.6 11.9 %all_to_all.15 = f32[16,3,128]{2,1,0:T(4,128)S(1)} all-to-all(f32[16,3,128]{2,1,0:T(4,128)S(1)} %broadcast_in_dim.17), channel_id=1, replica_groups=mesh['yh'=4,'yl'=2,'zl'=2,'c'=2,'x'=4,'zh'=4] {'x','zh'}, dimensions={0} | all-to-all | bytes 49152 | tf_op jit(solution)/shard_map/all_to_all | solution.py:236
  159.0 2.4 %grad.1.gq = bf16[384,256]{1,0:T(8,128)(2,1)} custom-call(f32[3,384]{1,0:T(4,128)} %copy-done.13, f32[1,384]{1,0:T(1,128)} %bitcast.37, f32[384,768]{1,0:T(8,128)} %copy-done.1, f32[384,256]{1,0:T(8,128)} %copy-done.12), custom_call_target="tpu_custom_call" | custom-call | tf_op jit(solution)/shard_map/grad/pallas_call | solution.py:190
  161.4 2.9 %collective-permute-start.15 = (bf16[384,256]{1,0:T(8,128)(2,1)}, bf16[384,256]{1,0:T(8,128)(2,1)S(1)}, u32[]{:S(2)}, u32[]{:S(2)}) collective-permute-start(bf16[384,256]{1,0:T(8,128)(2,1)} %grad.1.gq), channel_id=1, source_target_pairs={{0,64},{64,0},{1,65},{65,1},{2,66},{66,2},{3,67},{67,3},{4,68},{68... | collective-permute-start | bytes 589832 | tf_op jit(solution)/shard_map/ppermute | solution.py:20
  164.3 4.8 %collective-permute-start.14 = (bf16[384,256]{1,0:T(8,128)(2,1)}, bf16[384,256]{1,0:T(8,128)(2,1)S(1)}, u32[]{:S(2)}, u32[]{:S(2)}) collective-permute-start(bf16[384,256]{1,0:T(8,128)(2,1)} %grad.1.gq), channel_id=1, source_target_pairs={{0,16},{16,0},{1,17},{17,1},{2,18},{18,2},{3,19},{19,3},{4,20},{20... | collective-permute-start | bytes 589832 | tf_op jit(solution)/shard_map/ppermute | solution.py:20
  169.1 4.0 %collective-permute-start.16 = (bf16[384,256]{1,0:T(8,128)(2,1)S(1)}, bf16[384,256]{1,0:T(8,128)(2,1)S(1)}, u32[]{:S(2)}, u32[]{:S(2)}) collective-permute-start(bf16[384,256]{1,0:T(8,128)(2,1)S(1)} %collective-permute-done.15.gq_near), channel_id=1, source_target_pairs={{0,16},{16,0},{1,17},{17,1},{2,18},{18,2},{3,19},{19,3},{4,20},{20... | collective-permute-start | bytes 589832 | tf_op jit(solution)/shard_map/ppermute | solution.py:20
  173.1 1.0 collective-permute-done.16.gq_near_core
  174.1 2.1 copy-done
  176.2 0.9 copy-done.11
  177.2 3.5 %outer.1 = bf16[4,320,256]{2,1,0:T(8,128)(2,1)S(1)} custom-call(s32[2]{0:T(128)S(1)} %pad_add_fusion.place, bf16[4,2,320,768]{3,2,1,0:T(8,128)(2,1)S(1)} %bitcast.28, bf16[4,320,768]{2,1,0:T(8,128)(2,1)} %collective-permute-done.12.near, bf16[384,256]{1,0:T(8,128)(2,1)S(1)} %copy-done.11, bf16[384,256]{1,0:T(8,128)(2,1)S(1)} %collective-permute-done.14.gq_core, ...), custom_call_target="tpu_custom_call" | custom-call | flops 1006632960 | bytes 3932160 | tf_op jit(solution)/shard_map/outer/pallas_call | solution.py:212
  180.7 24.3 %all_to_all.16 = bf16[8,160,256]{2,1,0:T(8,128)(2,1)S(1)} all-to-all(bf16[8,160,256]{2,1,0:T(8,128)(2,1)S(1)} %bitcast.29), channel_id=1, replica_groups=mesh['yh'=4,'yl'=2,'zl'=2,'c'=2,'x'=4,'zh'=4] {'yh','zl'}, dimensions={0} | all-to-all | bytes 1310720 | tf_op jit(solution)/shard_map/all_to_all | solution.py:272
  (52 shorter events, 4.6 us)
Async XLA Ops:
  6.5 92.3 %all-gather.2.cloned.1.call-start = ((), (), s32[]{:S(2)}) async-start(), calls=%async_computation.3 | async-start | bytes 4177920 | tf_op jit(solution)/shard_map/all_gather | solution.py:251
  7.5 9.7 %collective-permute-start = (bf16[160,384]{1,0:T(8,128)(2,1)S(1)}, bf16[160,384]{1,0:T(8,128)(2,1)S(1)}, u32[]{:S(2)}, u32[]{:S(2)}) collective-permute-start(bf16[160,384]{1,0:T(8,128)(2,1)S(1)} %get-tuple-element.28), channel_id=1, source_target_pairs={{0,16},{16,0},{1,17},{17,1},{2,18},{18,2},{3,19},{19,3},{4,20},{20... | collective-permute-start | bytes 368648 | tf_op jit(solution)/shard_map/ppermute | solution.py:20
  19.1 10.8 %collective-permute-start.1 = (bf16[4,160,256]{2,1,0:T(8,128)(2,1)S(1)}, bf16[4,160,256]{2,1,0:T(8,128)(2,1)S(1)}, u32[]{:S(2)}, u32[]{:S(2)}) collective-permute-start(bf16[4,160,256]{2,1,0:T(8,128)(2,1)S(1)} %pad_maximum_fusion.2.refs_0_), channel_id=1, source_target_pairs={{0,32},{32,0},{1,33},{33,1},{2,34},{34,2},{3,35},{35,3},{4,36},{36... | collective-permute-start | bytes 983048 | tf_op jit(solution)/shard_map/ppermute | solution.py:20
  21.0 10.8 %collective-permute-start.2 = (bf16[4,160,256]{2,1,0:T(8,128)(2,1)S(1)}, bf16[4,160,256]{2,1,0:T(8,128)(2,1)S(1)}, u32[]{:S(2)}, u32[]{:S(2)}) collective-permute-start(bf16[4,160,256]{2,1,0:T(8,128)(2,1)S(1)} %pad_maximum_fusion.2.refs_0_), channel_id=1, source_target_pairs={{0,448},{64,0},{128,64},{192,128},{256,192},{320,256},{384,320},{4... | collective-permute-start | bytes 983048 | tf_op jit(solution)/shard_map/ppermute | solution.py:20
  22.9 11.5 %collective-permute-start.7 = (bf16[4,160,256]{2,1,0:T(8,128)(2,1)S(1)}, bf16[4,160,256]{2,1,0:T(8,128)(2,1)S(1)}, u32[]{:S(2)}, u32[]{:S(2)}) collective-permute-start(bf16[4,160,256]{2,1,0:T(8,128)(2,1)S(1)} %pad_maximum_fusion.2.refs_0_), channel_id=1, source_target_pairs={{0,64},{64,128},{128,192},{192,256},{256,320},{320,384},{384,448},... | collective-permute-start | bytes 983048 | tf_op jit(solution)/shard_map/ppermute | solution.py:20
  34.6 17.6 %collective-permute-start.8 = (bf16[8,160,256]{2,1,0:T(8,128)(2,1)S(1)}, bf16[8,160,256]{2,1,0:T(8,128)(2,1)S(1)}, u32[]{:S(2)}, u32[]{:S(2)}) collective-permute-start(bf16[8,160,256]{2,1,0:T(8,128)(2,1)S(1)} %get-tuple-element.25), channel_id=1, source_target_pairs={{0,64},{64,128},{128,192},{192,256},{256,320},{320,384},{384,448},... | collective-permute-start | bytes 1966088 | tf_op jit(solution)/shard_map/ppermute | solution.py:20
  36.9 18.0 %collective-permute-start.3 = (bf16[8,160,256]{2,1,0:T(8,128)(2,1)S(1)}, bf16[8,160,256]{2,1,0:T(8,128)(2,1)S(1)}, u32[]{:S(2)}, u32[]{:S(2)}) collective-permute-start(bf16[8,160,256]{2,1,0:T(8,128)(2,1)S(1)} %get-tuple-element.26), channel_id=1, source_target_pairs={{0,448},{64,0},{128,64},{192,128},{256,192},{320,256},{384,320},{4... | collective-permute-start | bytes 1966088 | tf_op jit(solution)/shard_map/ppermute | solution.py:20
  52.2 16.8 %collective-permute-start.9 = (bf16[8,160,256]{2,1,0:T(8,128)(2,1)S(1)}, bf16[8,160,256]{2,1,0:T(8,128)(2,1)S(1)}, u32[]{:S(2)}, u32[]{:S(2)}) collective-permute-start(bf16[8,160,256]{2,1,0:T(8,128)(2,1)S(1)} %collective-permute-done.8.refs_4_), channel_id=1, source_target_pairs={{0,64},{64,128},{128,192},{192,256},{256,320},{320,384},{384,448},... | collective-permute-start | bytes 1966088 | tf_op jit(solution)/shard_map/ppermute | solution.py:20
  54.1 0.8 copy-start.5
  55.0 29.9 %copy-start.8 = (bf16[8,160,256]{2,1,0:T(8,128)(2,1)}, bf16[8,160,256]{2,1,0:T(8,128)(2,1)S(1)}, u32[]{:S(2)}) copy-start(bf16[8,160,256]{2,1,0:T(8,128)(2,1)S(1)} %collective-permute-done.3.refs_5_) | copy-start | bytes 1966084
  55.0 16.0 %collective-permute-start.4 = (bf16[8,160,256]{2,1,0:T(8,128)(2,1)S(1)}, bf16[8,160,256]{2,1,0:T(8,128)(2,1)S(1)}, u32[]{:S(2)}, u32[]{:S(2)}) collective-permute-start(bf16[8,160,256]{2,1,0:T(8,128)(2,1)S(1)} %collective-permute-done.3.refs_5_), channel_id=1, source_target_pairs={{0,448},{64,0},{128,64},{192,128},{256,192},{320,256},{384,320},{4... | collective-permute-start | bytes 1966088 | tf_op jit(solution)/shard_map/ppermute | solution.py:20
  69.1 12.5 %collective-permute-start.10 = (bf16[6,160,256]{2,1,0:T(8,128)(2,1)S(1)}, bf16[6,160,256]{2,1,0:T(8,128)(2,1)S(1)}, u32[]{:S(2)}, u32[]{:S(2)}) collective-permute-start(bf16[6,160,256]{2,1,0:T(8,128)(2,1)S(1)} %slice.26), channel_id=1, source_target_pairs={{0,64},{64,128},{128,192},{192,256},{256,320},{320,384},{384,448},... | collective-permute-start | bytes 1474568 | tf_op jit(solution)/shard_map/ppermute | solution.py:20
  71.0 13.1 %collective-permute-start.5 = (bf16[6,160,256]{2,1,0:T(8,128)(2,1)S(1)}, bf16[6,160,256]{2,1,0:T(8,128)(2,1)S(1)}, u32[]{:S(2)}, u32[]{:S(2)}) collective-permute-start(bf16[6,160,256]{2,1,0:T(8,128)(2,1)S(1)} %slice.24), channel_id=1, source_target_pairs={{0,448},{64,0},{128,64},{192,128},{256,192},{320,256},{384,320},{4... | collective-permute-start | bytes 1474568 | tf_op jit(solution)/shard_map/ppermute | solution.py:20
  82.2 8.1 %collective-permute-start.11 = (bf16[2,160,256]{2,1,0:T(8,128)(2,1)}, bf16[2,160,256]{2,1,0:T(8,128)(2,1)S(1)}, u32[]{:S(2)}, u32[]{:S(2)}) collective-permute-start(bf16[2,160,256]{2,1,0:T(8,128)(2,1)} %slice.27), channel_id=1, source_target_pairs={{0,64},{64,128},{128,192},{192,256},{256,320},{320,384},{384,448},... | collective-permute-start | bytes 491528 | tf_op jit(solution)/shard_map/ppermute | solution.py:20
  84.8 0.8 copy-start.2
  85.7 7.1 %collective-permute-start.6 = (bf16[2,160,256]{2,1,0:T(8,128)(2,1)}, bf16[2,160,256]{2,1,0:T(8,128)(2,1)S(1)}, u32[]{:S(2)}, u32[]{:S(2)}) collective-permute-start(bf16[2,160,256]{2,1,0:T(8,128)(2,1)} %slice.25), channel_id=1, source_target_pairs={{0,448},{64,0},{128,64},{192,128},{256,192},{320,256},{384,320},{4... | collective-permute-start | bytes 491528 | tf_op jit(solution)/shard_map/ppermute | solution.py:20
  98.8 1.0 copy-start.3
  99.8 1.1 copy-start.6
  100.9 1.1 copy-start.9
  107.9 13.7 %collective-permute-start.13 = (f32[384,1024]{1,0:T(8,128)}, f32[384,1024]{1,0:T(8,128)}, u32[]{:S(2)}, u32[]{:S(2)}) collective-permute-start(f32[384,1024]{1,0:T(8,128)} %project.2), channel_id=1, source_target_pairs={{0,16},{16,0},{1,17},{17,1},{2,18},{18,2},{3,19},{19,3},{4,20},{20... | collective-permute-start | bytes 4718600 | tf_op jit(solution)/shard_map/ppermute | solution.py:20
  110.6 6.3 %copy-start.4 = (bf16[6,160,256]{2,1,0:T(8,128)(2,1)S(1)}, bf16[6,160,256]{2,1,0:T(8,128)(2,1)}, u32[]{:S(2)}) copy-start(bf16[6,160,256]{2,1,0:T(8,128)(2,1)} %copy-done.2) | copy-start | bytes 1474564
  110.6 6.3 %copy-start.7 = (bf16[8,160,256]{2,1,0:T(8,128)(2,1)S(1)}, bf16[8,160,256]{2,1,0:T(8,128)(2,1)}, u32[]{:S(2)}) copy-start(bf16[8,160,256]{2,1,0:T(8,128)(2,1)} %copy-done.5) | copy-start | bytes 1966084
  110.6 6.3 %copy-start.10 = (bf16[8,160,256]{2,1,0:T(8,128)(2,1)S(1)}, bf16[8,160,256]{2,1,0:T(8,128)(2,1)}, u32[]{:S(2)}) copy-start(bf16[8,160,256]{2,1,0:T(8,128)(2,1)} %copy-done.8) | copy-start | bytes 1966084
  113.7 59.4 %collective-permute-start.12 = (bf16[4,320,768]{2,1,0:T(8,128)(2,1)}, bf16[4,320,768]{2,1,0:T(8,128)(2,1)}, u32[]{:S(2)}, u32[]{:S(2)}) collective-permute-start(bf16[4,320,768]{2,1,0:T(8,128)(2,1)} %dynamic-slice_bitcast_fusion), channel_id=1, source_target_pairs={{0,64},{64,0},{1,65},{65,1},{2,66},{66,2},{3,67},{67,3},{4,68},{68... | collective-permute-start | bytes 5898248 | tf_op jit(solution)/shard_map/ppermute | solution.py:20
  121.5 11.6 %copy-start.14 = (f32[256]{0:T(256)S(1)}, f32[256]{0:T(256)}, u32[]{:S(2)}) copy-start(f32[256]{0:T(256)} %param.13) | copy-start | bytes 3076
  121.6 11.6 %copy-start.15 = (f32[256]{0:T(256)S(1)}, f32[256]{0:T(256)}, u32[]{:S(2)}) copy-start(f32[256]{0:T(256)} %param.12) | copy-start | bytes 3076
  123.4 35.6 %copy-start.1 = (f32[384,768]{1,0:T(8,128)}, f32[384,768]{1,0:T(8,128)S(1)}, u32[]{:S(2)}) copy-start(f32[384,768]{1,0:T(8,128)S(1)} %get-tuple-element.21.qkd) | copy-start | bytes 3538948
  124.2 19.3 %all-to-all-start = ((f32[16,9,128]{2,1,0:T(8,128)}), f32[16,9,128]{2,1,0:T(8,128)S(1)}, u32[]{:S(2)}, u32[]{:S(2)}) async-start(f32[16,9,128]{2,1,0:T(8,128)} %broadcast_in_dim.15), calls=%async_computation | async-start | bytes 262144 | tf_op jit(solution)/shard_map/all_to_all | solution.py:236
  143.5 15.5 %copy-start.13 = (f32[3,384]{1,0:T(4,128)}, f32[3,384]{1,0:T(4,128)S(1)}, u32[]{:S(2)}) copy-start(f32[3,384]{1,0:T(4,128)S(1)} %reshape.21.sums) | copy-start | bytes 13828
  145.8 0.8 copy-start.12
  161.4 7.7 %collective-permute-start.15 = (bf16[384,256]{1,0:T(8,128)(2,1)}, bf16[384,256]{1,0:T(8,128)(2,1)S(1)}, u32[]{:S(2)}, u32[]{:S(2)}) collective-permute-start(bf16[384,256]{1,0:T(8,128)(2,1)} %grad.1.gq), channel_id=1, source_target_pairs={{0,64},{64,0},{1,65},{65,1},{2,66},{66,2},{3,67},{67,3},{4,68},{68... | collective-permute-start | bytes 589832 | tf_op jit(solution)/shard_map/ppermute | solution.py:20
  164.3 8.8 %collective-permute-start.14 = (bf16[384,256]{1,0:T(8,128)(2,1)}, bf16[384,256]{1,0:T(8,128)(2,1)S(1)}, u32[]{:S(2)}, u32[]{:S(2)}) collective-permute-start(bf16[384,256]{1,0:T(8,128)(2,1)} %grad.1.gq), channel_id=1, source_target_pairs={{0,16},{16,0},{1,17},{17,1},{2,18},{18,2},{3,19},{19,3},{4,20},{20... | collective-permute-start | bytes 589832 | tf_op jit(solution)/shard_map/ppermute | solution.py:20
  169.1 5.0 %collective-permute-start.16 = (bf16[384,256]{1,0:T(8,128)(2,1)S(1)}, bf16[384,256]{1,0:T(8,128)(2,1)S(1)}, u32[]{:S(2)}, u32[]{:S(2)}) collective-permute-start(bf16[384,256]{1,0:T(8,128)(2,1)S(1)} %collective-permute-done.15.gq_near), channel_id=1, source_target_pairs={{0,16},{16,0},{1,17},{17,1},{2,18},{18,2},{3,19},{19,3},{4,20},{20... | collective-permute-start | bytes 589832 | tf_op jit(solution)/shard_map/ppermute | solution.py:20
  174.1 2.1 copy-start
  176.2 0.9 copy-start.11
Sparse Core Ops, SparseCore 0:
  18.1 80.6 all-gather.1

commit v3 on v2

v3 whole, which is shorter than its diff:
```python
import functools

import jax
import jax.numpy as jnp
from jax import lax
from jax.experimental import pallas as pl
from jax.experimental.pallas import tpu as pltpu
from jax.sharding import Mesh, PartitionSpec as P

HEADS = 32
HD = 128
EPS = 1e-06
BF = jnp.bfloat16
F32 = jnp.float32
Y = ("yh", "yl")
MIB = 1024 * 1024


def shift(value, axis, by, size):
    return lax.ppermute(value, axis, [(i, (i + by) % size) for i in range(size)])


def weight_ring(own, other):
    up, down = shift(own, Y, 1, 8), shift(own, Y, -1, 8)
    parts = [(own, 0, 4, 0, 0, 0), (other, 0, 4, 0, 1, 0), (up, 0, 4, 1, 0, 0), (down, 0, 4, 7, 0, 0)]
    up = shift(jnp.concatenate([up, other]), Y, 1, 8)
    down = shift(jnp.concatenate([other, down]), Y, -1, 8)
    parts += [(up, 0, 4, 2, 0, 0), (up, 4, 4, 1, 1, 0), (down, 0, 4, 7, 1, 0), (down, 4, 4, 6, 0, 0)]
    up, down = shift(up, Y, 1, 8), shift(down, Y, -1, 8)
    parts += [(up, 0, 4, 3, 0, 0), (up, 4, 4, 2, 1, 0), (down, 0, 4, 6, 1, 0), (down, 4, 4, 5, 0, 0)]
    up, down = shift(up[2:], Y, 1, 8), shift(down[:6], Y, -1, 8)
    parts += [(up, 0, 2, 4, 0, 2), (up, 2, 4, 3, 1, 0), (down, 0, 4, 5, 1, 0), (down, 4, 2, 4, 0, 0)]
    up, down = shift(up[4:], Y, 1, 8), shift(down[:2], Y, -1, 8)
    parts += [(up, 0, 2, 4, 1, 2), (down, 0, 2, 4, 1, 0)]
    return parts


def project_kernel(place, x_hbm, *refs, layout, wide, rows):
    count = max(entry[0] for entry in layout) + 1
    pieces = refs[:count]
    own, theirs, near, x, w, sem, out_sem = refs[count:]
    length = own.shape[0]
    y, zl = place[0], place[1]
    groups = sem.shape[0]
    span = x.shape[0] // groups
    spots = {}
    for _, _, _, back, step, _ in layout:
        spots.setdefault((back, step), len(spots))

    def source(back, step):
        return lax.rem(y + 8 - back, 8), lax.rem(zl + step, 2)

    def block(index):
        return pl.ds(pl.multiple_of(index * rows, rows), rows)

    for (back, step), spot in spots.items():
        far_y, far_zl = source(back, step)
        at = pl.ds(spot * rows, rows)
        group = spot * rows // span
        index = (lax.rem(far_y, 2) * 2 + far_zl) * 4 + lax.div(far_y, 2)
        pltpu.make_async_copy(x_hbm.at[block(index), :], x.at[at, :], sem.at[group, 0]).start()
        for piece, first, entries, b, s, weight in layout:
            if (b, s) == (back, step):
                pltpu.make_async_copy(
                    pieces[piece].at[pl.ds(first, entries)], w.at[pl.ds(weight, entries), at, :], sem.at[group, 1]
                ).start()
    for g in range(groups):
        at = pl.ds(g * span, span)
        pltpu.make_async_copy(x.at[at, :], x.at[at, :], sem.at[g, 0]).wait()
        for (back, step), spot in spots.items():
            if back % 2 and spot * rows // span == g:
                far_y, far_zl = source(back, step)
                pltpu.make_async_copy(
                    x.at[pl.ds(spot * rows, rows), :], near.at[block(far_zl * 4 + lax.div(far_y, 2)), :], out_sem
                ).start()
        pltpu.make_async_copy(w.at[:, at, :], w.at[:, at, :], sem.at[g, 1]).wait()
        for i in range(4):
            part = lax.dot_general(x[at, :], w[i, at, :], (((0,), (0,)), ((), ())), preferred_element_type=F32)
            cols = slice(i * wide, (i + 1) * wide)
            own[:, cols] = part[:length] if g == 0 else own[:, cols] + part[:length]
            theirs[:, cols] = part[length:] if g == 0 else theirs[:, cols] + part[length:]
    pltpu.make_async_copy(near, near, out_sem).wait()


def project(place, x, parts, wide):
    depth, length = x.shape[0], x.shape[1] // 2
    arrays = []
    layout = []
    for array, *rest in parts:
        known = [i for i, other in enumerate(arrays) if other is array]
        if not known:
            arrays.append(array)
        layout.append((known[0] if known else len(arrays) - 1, *rest))
    return pl.pallas_call(
        functools.partial(project_kernel, layout=tuple(layout), wide=wide, rows=depth // 16),
        in_specs=[pl.BlockSpec(memory_space=pltpu.SMEM)]
        + [pl.BlockSpec(memory_space=pl.ANY)] * (1 + len(arrays)),
        out_specs=[
            pl.BlockSpec(memory_space=pltpu.VMEM),
            pl.BlockSpec(memory_space=pltpu.VMEM),
            pl.BlockSpec(memory_space=pl.ANY),
        ],
        out_shape=[
            jax.ShapeDtypeStruct((length, 4 * wide), F32),
            jax.ShapeDtypeStruct((length, 4 * wide), F32),
            jax.ShapeDtypeStruct((depth // 2, 2 * length), BF),
        ],
        scratch_shapes=[
            pltpu.VMEM(x.shape, BF),
            pltpu.VMEM((4, depth, wide), BF),
            pltpu.SemaphoreType.DMA((2, 2)),
            pltpu.SemaphoreType.DMA,
        ],
        compiler_params=pltpu.CompilerParams(vmem_limit_bytes=62 * MIB),
        cost_estimate=pl.CostEstimate(
            flops=16 * length * depth * wide, bytes_accessed=4 * depth * (length + 2 * wide), transcendentals=0
        ),
        name="project",
    )(place, x, *arrays)


def pack(columns):
    n = columns[0].shape[0]
    lane = lax.broadcasted_iota(jnp.int32, (n, 128), 1)
    full = jnp.zeros((n, 128), F32)
    for i, column in enumerate(columns):
        full = jnp.where(lane == i, column, full)
    full = full.T
    rows = [full[i : i + 1, j : j + 128] for i in range(len(columns)) for j in range(0, n, 128)]
    return jnp.broadcast_to(jnp.concatenate(rows, axis=0)[None], (16, len(rows), 128))


def unpack(got, count):
    total = jnp.sum(got, axis=0)
    rows = total.shape[0]
    full = jnp.concatenate([total, jnp.zeros((128 - rows, 128), F32)], axis=0).T
    each = rows // count
    return [
        jnp.concatenate([full[:, i * each + j : i * each + j + 1] for j in range(each)], axis=0) for i in range(count)
    ]


def merge_kernel(one, two, qkd, value, stats, *, wide):
    whole = [one[:, i * wide : (i + 1) * wide] + two[:, i * wide : (i + 1) * wide] for i in range(4)]
    for i in range(3):
        qkd[:, i * wide : (i + 1) * wide] = whole[i]
    value[...] = whole[3].astype(BF)
    q, key, dq = whole[:3]
    stats[...] = pack([jnp.sum(t, axis=1, keepdims=True) for t in (q * q, key * key, q * dq)])


def merge(one, two, wide):
    length = one.shape[0]
    return pl.pallas_call(
        functools.partial(merge_kernel, wide=wide),
        out_shape=[
            jax.ShapeDtypeStruct((length, 3 * wide), F32),
            jax.ShapeDtypeStruct((length, wide), BF),
            jax.ShapeDtypeStruct((16, 3 * length // 128, 128), F32),
        ],
        compiler_params=pltpu.CompilerParams(vmem_limit_bytes=16 * MIB),
        name="merge",
    )(one, two)


def attend_kernel(sums, qkd, value, gains, weighted, stats, *, wide, total):
    length = qkd.shape[0]
    scale = 1.0 / HD**0.5
    rq, rk, tq = unpack(sums[...], 3)
    rq = lax.rsqrt(rq / total + EPS)
    rk = lax.rsqrt(rk / total + EPS)
    tq = tq / total
    causal = lax.broadcasted_iota(jnp.int32, (length, length), 1) <= lax.broadcasted_iota(
        jnp.int32, (length, length), 0
    )
    nt = (((1,), (1,)), ((), ()))
    back = jnp.zeros((length, 1), F32)
    for h in range(wide // HD):
        at = slice(h * HD, (h + 1) * HD)
        q = qkd[:, h * HD : (h + 1) * HD]
        key = qkd[:, wide + h * HD : wide + (h + 1) * HD]
        dq = qkd[:, 2 * wide + h * HD : 2 * wide + (h + 1) * HD]
        v = value[:, at]
        gq, gk = gains[0:1, at], gains[1:2, at]
        qn = (gq * q * rq).astype(BF)
        kn = (gk * key * rk).astype(BF)
        dqn = (gq * rq * (dq - q * rq * rq * tq)).astype(BF)
        scores = lax.dot_general(qn, kn, nt, preferred_element_type=F32) * scale
        scores = jnp.where(causal, scores, -jnp.inf)
        expo = jnp.exp(scores - jnp.max(scores, axis=1, keepdims=True))
        probs = expo / jnp.sum(expo, axis=1, keepdims=True)
        ds = lax.dot_general(dqn, kn, nt, preferred_element_type=F32) * scale
        dpb = (probs * (ds - jnp.sum(probs * ds, axis=1, keepdims=True))).astype(BF)
        upper = jnp.dot(dpb, v, preferred_element_type=F32).astype(BF)
        gp = lax.dot_general(upper, v, nt, preferred_element_type=F32)
        gs = (probs * (gp - jnp.sum(probs * gp, axis=1, keepdims=True))).astype(BF)
        w = gq * (jnp.dot(gs, kn, preferred_element_type=F32) * scale)
        weighted[:, at] = w
        back += jnp.sum(q * w, axis=1, keepdims=True)
    stats[...] = pack([back])


def attend(sums, qkd, value, gains, wide, total):
    length = qkd.shape[0]
    return pl.pallas_call(
        functools.partial(attend_kernel, wide=wide, total=total),
        out_shape=[
            jax.ShapeDtypeStruct((length, wide), F32),
            jax.ShapeDtypeStruct((16, length // 128, 128), F32),
        ],
        compiler_params=pltpu.CompilerParams(vmem_limit_bytes=16 * MIB),
        name="attend",
    )(sums, qkd, value, gains)


def grad_kernel(sums, back, q, weighted, gq, *, total):
    rq = lax.rsqrt(unpack(sums[...], 3)[0] / total + EPS)
    tb = unpack(back[...], 1)[0] / total
    gq[...] = (rq * weighted[...] - q[...] * rq * rq * rq * tb).astype(BF)


def grad(sums, back, qkd, weighted, total):
    length, wide = weighted.shape
    return pl.pallas_call(
        functools.partial(grad_kernel, total=total),
        grid=(1,),
        in_specs=[
            pl.BlockSpec(sums.shape, lambda k: (0, 0, 0)),
            pl.BlockSpec(back.shape, lambda k: (0, 0, 0)),
            pl.BlockSpec((length, wide), lambda k: (0, 0)),
            pl.BlockSpec((length, wide), lambda k: (0, 0)),
        ],
        out_specs=pl.BlockSpec((length, wide), lambda k: (0, 0)),
        out_shape=jax.ShapeDtypeStruct((length, wide), BF),
        name="grad",
    )(sums, back, qkd, weighted)


def outer_kernel(place, x, near, gq, gq_core, gq_near, gq_near_core, term):
    length = gq.shape[0]
    total = jnp.dot(x[0, :, :length], gq[...], preferred_element_type=F32)
    total += jnp.dot(x[0, :, length:], gq_core[...], preferred_element_type=F32)
    total += jnp.dot(near[:, :length], gq_near[...], preferred_element_type=F32)
    total += jnp.dot(near[:, length:], gq_near_core[...], preferred_element_type=F32)
    term[...] = total.astype(BF)


def outer(place, x, near, grads):
    rows, tokens = near.shape
    length, wide = grads[0].shape
    steps = 2
    block = rows // steps
    return pl.pallas_call(
        outer_kernel,
        grid_spec=pltpu.PrefetchScalarGridSpec(
            num_scalar_prefetch=1,
            grid=(steps,),
            in_specs=[
                pl.BlockSpec((1, block, tokens), lambda k, place: (lax.rem(place[0], 2), k, 0)),
                pl.BlockSpec((block, tokens), lambda k, place: (k, 0)),
            ]
            + [pl.BlockSpec((length, wide), lambda k, place: (0, 0))] * 4,
            out_specs=pl.BlockSpec((block, wide), lambda k, place: (k, 0)),
        ),
        out_shape=jax.ShapeDtypeStruct((rows, wide), BF),
        compiler_params=pltpu.CompilerParams(vmem_limit_bytes=62 * MIB),
        cost_estimate=pl.CostEstimate(flops=4 * rows * tokens * wide, bytes_accessed=4 * rows * tokens, transcendentals=0),
        name="outer",
    )(place, x.reshape(2, rows, tokens), near, *grads)


def to_all(value, axes):
    return lax.all_to_all(value, axes, 0, 0, tiled=True)


def on_device(inputs, w_query, w_key, w_value, tangent, gain_query, gain_key):
    wide = w_query.shape[1]
    total = HEADS * HD
    place = jnp.stack([lax.axis_index(Y), lax.axis_index("zl")]).astype(jnp.int32)
    core = lax.axis_index("c")
    tie = lax.optimization_barrier

    halves = inputs[0].T.reshape(2, inputs.shape[2] // 2, inputs.shape[1])
    kept = lax.dynamic_index_in_dim(halves, core, 0, keepdims=False)
    given = lax.dynamic_index_in_dim(halves, 1 - core, 0, keepdims=False)
    x = jnp.concatenate([kept, shift(given, "c", 1, 2)], axis=1)
    x = lax.all_gather(x, ("zh", "x"), axis=0, tiled=True)

    weights = jnp.stack([w_query, w_key, tangent, w_value])
    parts = weight_ring(weights, shift(weights, "zl", 1, 2))
    x, *last = tie((x, parts[-1][0], parts[-2][0]))
    parts[-1], parts[-2] = (last[0], *parts[-1][1:]), (last[1], *parts[-2][1:])

    own, theirs, near = project(place, x, parts, wide)
    theirs = shift(theirs, "c", 1, 2)
    near = shift(near, "yl", 1, 2)
    qkd, value, stats = merge(own, theirs, wide)
    gains, stats = tie((jnp.stack([gain_query, gain_key]), stats))
    sums = to_all(stats, ("x", "zh"))
    weighted, stats = attend(sums, qkd, value, gains, wide, total)
    gq = grad(sums, to_all(stats, ("x", "zh")), qkd, weighted, total)

    gq_near = shift(gq, "yl", 1, 2)
    gq_core = shift(gq, "c", 1, 2)
    term = outer(place, x, near, (gq, gq_core, gq_near, shift(gq_near, "c", 1, 2)))
    got = to_all(term.reshape(8, -1, wide), ("zl", "yh"))
    return jnp.sum(got.astype(F32), axis=0)


def solution(mesh):
    fine = Mesh(mesh.devices.reshape(4, 2, 2, 2, 4, 4), ("yh", "yl", "zl", "c", "x", "zh"))
    dp, tensor = ("yh", "yl", "zl", "c"), ("x", "zh")
    return jax.shard_map(
        on_device,
        mesh=fine,
        in_specs=(
            P(dp, None, tensor),
            P(dp, tensor),
            P(dp, tensor),
            P(dp, tensor),
            P(dp, tensor),
            P(tensor),
            P(tensor),
        ),
        out_specs=P(dp, tensor),
        check_vma=False,
    )
```

time: 214 us -> 205 us (0.958)
  blocking collectives: 36.1 us -> 56 us
  local copies, waits for them, and re-layouts: 15.5 us -> 4.67 us
  starting transfers between devices: 68.7 us -> 58.4 us
  waiting for transfers between devices: 55 us -> 48.3 us
    all_to_all x2 -> x3, blocking collectives: 36.1 us -> 56 us  [to_all(): return lax.all_to_all(value, axes, 0, 0, tiled=True)]
    all_to_all x1 -> x0, waiting for transfers between devices: 10.3 us -> none  [sum_over_heads(): lax.all_to_all(jnp.broadcast_to(mine, (16,) + mine.shape[1:]), ('x', 'zh'...]
    all_to_all x1 -> x0, starting transfers between devices: 8.94 us -> none  [sum_over_heads(): lax.all_to_all(jnp.broadcast_to(mine, (16,) + mine.shape[1:]), ('x', 'zh'...]
    unnamed x33 -> x44, local copies, waits for them, and re-layouts: 9.2 us -> 3.59 us
    squeeze x1 -> x0, local copies, waits for them, and re-layouts: 3.12 us -> none  [on_device(): lax.dynamic_index_in_dim(fine, 1 - lax.axis_index('yl'), 1, keepdims=False)]
    pallas_call x3 -> x2, Pallas kernels: 13 us -> 11.6 us  [the longest x1 9.28 us: project(): pl.pallas_call(functools.partial(project_kernel, layout=tuple(layout), wi...]
  transfers between devices with their start and end apart: 19 -> 18, of which waited for: 11 -> 13; matrix products, arithmetic and copies ran while one was open for 3% -> 1% of each run, Pallas kernels for 5% -> 2%
where the time goes in v3:
time: 205 us; the launch traced here: 204 us
  starting transfers between devices  58.4 us (28%)
  blocking collectives  56 us (27%)
  waiting for transfers between devices  48.3 us (24%)
  Pallas kernels  19.1 us (9%)
  between operations  13.8 us (7%)
  local copies, waits for them, and re-layouts  4.67 us (2%)
  other arithmetic  3.23 us (2%)
    ppermute x17, starting transfers between devices, shift(): lax.ppermute(value, axis, [(i, (i + by) % size) for i in range(size)])  58.4 us
    all_to_all x3, blocking collectives, to_all(): return lax.all_to_all(value, axes, 0, 0, tiled=True)  56 us
    ppermute x17, waiting for transfers between devices, shift(): lax.ppermute(value, axis, [(i, (i + by) % size) for i in range(size)])  40.6 us
    pallas_call x1, Pallas kernels, project(): pl.pallas_call(functools.partial(project_kernel, layout=tuple(layout), wi...  9.28 us
    all_gather x1, waiting for transfers between devices, on_device(): x = lax.all_gather(x, ('zh', 'x'), axis=0, tiled=True)  7.7 us
    pallas_call x1, Pallas kernels, outer(): pl.pallas_call(outer_kernel, grid_spec=pltpu.PrefetchScalarGridSpec(num_s...  4.81 us
  transfers between devices with their start and end apart: 18, of which 13 were waited for; matrix products, arithmetic and copies ran while one was open for 1% of the time, Pallas kernels for 2%

profile of v3, /device:TPU:1, one launch (start us, length us, event | category | flops | bytes accessed | tf_op | source)
XLA Modules:
  0.0 203.6 jit_solution(6545503092360067744)
XLA Ops:
  6.5 1.0 dynamic-slice_bitcast_fusion.1
  7.5 8.8 %collective-permute-start = (bf16[160,384]{1,0:T(8,128)(2,1)S(1)}, bf16[160,384]{1,0:T(8,128)(2,1)S(1)}, u32[]{:S(2)}, u32[]{:S(2)}) collective-permute-start(bf16[160,384]{1,0:T(8,128)(2,1)S(1)} %get-tuple-element.34), channel_id=1, source_target_pairs={{0,16},{16,0},{1,17},{17,1},{2,18},{18,2},{3,19},{19,3},{4,20},{20... | collective-permute-start | bytes 368648 | tf_op jit(solution)/shard_map/ppermute | solution.py:20
  16.3 1.0 collective-permute-done
  17.3 0.7 pad_maximum_fusion.3
  18.0 1.1 pad_maximum_fusion.2.refs_0_
  19.1 1.9 collective-permute-start.1
  21.0 1.9 collective-permute-start.2
  22.9 3.4 %collective-permute-start.7 = (bf16[4,160,256]{2,1,0:T(8,128)(2,1)S(1)}, bf16[4,160,256]{2,1,0:T(8,128)(2,1)S(1)}, u32[]{:S(2)}, u32[]{:S(2)}) collective-permute-start(bf16[4,160,256]{2,1,0:T(8,128)(2,1)S(1)} %pad_maximum_fusion.2.refs_0_), channel_id=1, source_target_pairs={{0,64},{64,128},{128,192},{192,256},{256,320},{320,384},{384,448},... | collective-permute-start | bytes 983048 | tf_op jit(solution)/shard_map/ppermute | solution.py:20
  26.3 3.6 %collective-permute-done.1.refs_1_ = bf16[4,160,256]{2,1,0:T(8,128)(2,1)S(1)} collective-permute-done((bf16[4,160,256]{2,1,0:T(8,128)(2,1)S(1)}, bf16[4,160,256]{2,1,0:T(8,128)(2,1)S(1)}, u32[]{:S(2)}, u32[]{:S(2)}) %collective-permute-start.1) | collective-permute-done | bytes 327712 | tf_op jit(solution)/shard_map/ppermute | solution.py:20
  29.9 1.9 collective-permute-done.2.refs_3_
  31.9 2.6 %collective-permute-done.7.refs_2_ = bf16[4,160,256]{2,1,0:T(8,128)(2,1)S(1)} collective-permute-done((bf16[4,160,256]{2,1,0:T(8,128)(2,1)S(1)}, bf16[4,160,256]{2,1,0:T(8,128)(2,1)S(1)}, u32[]{:S(2)}, u32[]{:S(2)}) %collective-permute-start.7) | collective-permute-done | bytes 327712 | tf_op jit(solution)/shard_map/ppermute | solution.py:20
  34.5 0.1 pad_maximum_fusion.1
  34.6 2.3 %collective-permute-start.8 = (bf16[8,160,256]{2,1,0:T(8,128)(2,1)S(1)}, bf16[8,160,256]{2,1,0:T(8,128)(2,1)S(1)}, u32[]{:S(2)}, u32[]{:S(2)}) collective-permute-start(bf16[8,160,256]{2,1,0:T(8,128)(2,1)S(1)} %get-tuple-element.31), channel_id=1, source_target_pairs={{0,64},{64,128},{128,192},{192,256},{256,320},{320,384},{384,448},... | collective-permute-start | bytes 1966088 | tf_op jit(solution)/shard_map/ppermute | solution.py:20
  37.0 4.2 %collective-permute-start.3 = (bf16[8,160,256]{2,1,0:T(8,128)(2,1)S(1)}, bf16[8,160,256]{2,1,0:T(8,128)(2,1)S(1)}, u32[]{:S(2)}, u32[]{:S(2)}) collective-permute-start(bf16[8,160,256]{2,1,0:T(8,128)(2,1)S(1)} %get-tuple-element.32), channel_id=1, source_target_pairs={{0,448},{64,0},{128,64},{192,128},{256,192},{320,256},{384,320},{4... | collective-permute-start | bytes 1966088 | tf_op jit(solution)/shard_map/ppermute | solution.py:20
  41.1 11.1 %collective-permute-done.8.refs_4_ = bf16[8,160,256]{2,1,0:T(8,128)(2,1)S(1)} collective-permute-done((bf16[8,160,256]{2,1,0:T(8,128)(2,1)S(1)}, bf16[8,160,256]{2,1,0:T(8,128)(2,1)S(1)}, u32[]{:S(2)}, u32[]{:S(2)}) %collective-permute-start.8) | collective-permute-done | bytes 655392 | tf_op jit(solution)/shard_map/ppermute | solution.py:20
  52.2 1.9 collective-permute-start.9
  54.2 4.6 %collective-permute-start.4 = (bf16[8,160,256]{2,1,0:T(8,128)(2,1)S(1)}, bf16[8,160,256]{2,1,0:T(8,128)(2,1)S(1)}, u32[]{:S(2)}, u32[]{:S(2)}) collective-permute-start(bf16[8,160,256]{2,1,0:T(8,128)(2,1)S(1)} %collective-permute-done.3.refs_5_), channel_id=1, source_target_pairs={{0,448},{64,0},{128,64},{192,128},{256,192},{320,256},{384,320},{4... | collective-permute-start | bytes 1966088 | tf_op jit(solution)/shard_map/ppermute | solution.py:20
  58.8 10.3 %collective-permute-done.9.refs_6_ = bf16[8,160,256]{2,1,0:T(8,128)(2,1)S(1)} collective-permute-done((bf16[8,160,256]{2,1,0:T(8,128)(2,1)S(1)}, bf16[8,160,256]{2,1,0:T(8,128)(2,1)S(1)}, u32[]{:S(2)}, u32[]{:S(2)}) %collective-permute-start.9) | collective-permute-done | bytes 655392 | tf_op jit(solution)/shard_map/ppermute | solution.py:20
  69.1 1.9 collective-permute-start.10
  71.1 4.6 %collective-permute-start.5 = (bf16[6,160,256]{2,1,0:T(8,128)(2,1)S(1)}, bf16[6,160,256]{2,1,0:T(8,128)(2,1)S(1)}, u32[]{:S(2)}, u32[]{:S(2)}) collective-permute-start(bf16[6,160,256]{2,1,0:T(8,128)(2,1)S(1)} %slice.16), channel_id=1, source_target_pairs={{0,448},{64,0},{128,64},{192,128},{256,192},{320,256},{384,320},{4... | collective-permute-start | bytes 1474568 | tf_op jit(solution)/shard_map/ppermute | solution.py:20
  75.7 5.9 %collective-permute-done.10.refs_8_ = bf16[6,160,256]{2,1,0:T(8,128)(2,1)S(1)} collective-permute-done((bf16[6,160,256]{2,1,0:T(8,128)(2,1)S(1)}, bf16[6,160,256]{2,1,0:T(8,128)(2,1)S(1)}, u32[]{:S(2)}, u32[]{:S(2)}) %collective-permute-start.10) | collective-permute-done | bytes 491552 | tf_op jit(solution)/shard_map/ppermute | solution.py:20
  81.6 1.9 collective-permute-start.11
  83.6 4.6 %collective-permute-start.6 = (bf16[2,160,256]{2,1,0:T(8,128)(2,1)S(1)}, bf16[2,160,256]{2,1,0:T(8,128)(2,1)S(1)}, u32[]{:S(2)}, u32[]{:S(2)}) collective-permute-start(bf16[2,160,256]{2,1,0:T(8,128)(2,1)S(1)} %slice.17), channel_id=1, source_target_pairs={{0,448},{64,0},{128,64},{192,128},{256,192},{320,256},{384,320},{4... | collective-permute-start | bytes 491528 | tf_op jit(solution)/shard_map/ppermute | solution.py:20
  88.2 0.6 pad_add_fusion.place
  88.8 0.5 collective-permute-done.11.refs_10_
  89.3 1.1 collective-permute-done.6.refs_11_
  90.4 0.7 copy-done.21
  91.1 7.7 %all-gather.2.cloned.1.call-done.x_hbm = bf16[2560,768]{1,0:T(8,128)(2,1)} async-done(((bf16[160,768]{1,0:T(8,128)(2,1)}), bf16[2560,768]{1,0:T(8,128)(2,1)}) %all-gather.2.cloned.1.call-update) | async-done | bytes 3932176 | tf_op jit(solution)/shard_map/all_gather | solution.py:287
  98.8 9.3 %project.1 = (f32[384,1024]{1,0:T(8,128)}, f32[384,1024]{1,0:T(8,128)}, bf16[1280,768]{1,0:T(8,128)(2,1)}) custom-call(s32[2]{0:T(128)} %pad_add_fusion.place, bf16[2560,768]{1,0:T(8,128)(2,1)} %all-gather.2.cloned.1.call-done.x_hbm, bf16[4,160,256]{2,1,0:T(8,128)(2,1)} %copy-done.10, bf16[4,160,256]{2,1,0:T(8,128)(2,1)} %copy-done.7, ...), custom_call_target="tpu_custom_call" | custom-call | flops 4026531840 | bytes 9175040 | tf_op jit(solution)/shard_map/project/pallas_call | solution.py:94
  108.1 2.6 %collective-permute-start.13 = (f32[384,1024]{1,0:T(8,128)}, f32[384,1024]{1,0:T(8,128)S(1)}, u32[]{:S(2)}, u32[]{:S(2)}) collective-permute-start(f32[384,1024]{1,0:T(8,128)} %get-tuple-element.23), channel_id=1, source_target_pairs={{0,16},{16,0},{1,17},{17,1},{2,18},{18,2},{3,19},{19,3},{4,20},{20... | collective-permute-start | bytes 4718600 | tf_op jit(solution)/shard_map/ppermute | solution.py:20
  110.7 3.1 %collective-permute-start.12 = (bf16[1280,768]{1,0:T(8,128)(2,1)}, bf16[1280,768]{1,0:T(8,128)(2,1)S(1)}, u32[]{:S(2)}, u32[]{:S(2)}) collective-permute-start(bf16[1280,768]{1,0:T(8,128)(2,1)} %get-tuple-element.21), channel_id=1, source_target_pairs={{0,64},{64,0},{1,65},{65,1},{2,66},{66,2},{3,67},{67,3},{4,68},{68... | collective-permute-start | bytes 5898248 | tf_op jit(solution)/shard_map/ppermute | solution.py:20
  113.9 0.1 collective-permute-done.13.two
  114.0 1.4 copy-done.1
  115.4 0.4 merge.1
  115.7 18.7 %all_to_all.15.sums = f32[16,9,128]{2,1,0:T(8,128)S(1)} all-to-all(f32[16,9,128]{2,1,0:T(8,128)S(1)} %get-tuple-element.25), channel_id=1, replica_groups=mesh['yh'=4,'yl'=2,'zl'=2,'c'=2,'x'=4,'zh'=4] {'x','zh'}, dimensions={0} | all-to-all | bytes 147456 | tf_op jit(solution)/shard_map/all_to_all | solution.py:273
  134.4 2.4 %attend.1 = (f32[384,256]{1,0:T(8,128)S(1)}, f32[16,3,128]{2,1,0:T(4,128)S(1)}) custom-call(f32[16,9,128]{2,1,0:T(8,128)S(1)} %all_to_all.15.sums, f32[384,768]{1,0:T(8,128)S(1)} %get-tuple-element.26.qkd.q, bf16[384,256]{1,0:T(8,128)(2,1)S(1)} %get-tuple-element.27.value, f32[2,256]{1,0:T(2,128)S(1)} %pad_maximum_fusion.4.gains), custom_call_target="tpu_custom_call" | custom-call | tf_op jit(solution)/shard_map/attend/pallas_call | solution.py:205
  136.8 0.8 copy-done.3
  137.5 12.1 %all_to_all.16.back = f32[16,3,128]{2,1,0:T(4,128)} all-to-all(f32[16,3,128]{2,1,0:T(4,128)S(1)} %get-tuple-element.29), channel_id=1, replica_groups=mesh['yh'=4,'yl'=2,'zl'=2,'c'=2,'x'=4,'zh'=4] {'x','zh'}, dimensions={0} | all-to-all | bytes 49152 | tf_op jit(solution)/shard_map/all_to_all | solution.py:273
  149.6 2.4 %grad.1.gq = bf16[384,256]{1,0:T(8,128)(2,1)} custom-call(f32[16,9,128]{2,1,0:T(8,128)} %copy-done.2, f32[16,3,128]{2,1,0:T(4,128)} %all_to_all.16.back, f32[384,768]{1,0:T(8,128)} %copy-done, f32[384,256]{1,0:T(8,128)} %copy-done.3), custom_call_target="tpu_custom_call" | custom-call | tf_op jit(solution)/shard_map/grad/pallas_call | solution.py:224
  152.0 2.1 %collective-permute-start.15 = (bf16[384,256]{1,0:T(8,128)(2,1)}, bf16[384,256]{1,0:T(8,128)(2,1)S(1)}, u32[]{:S(2)}, u32[]{:S(2)}) collective-permute-start(bf16[384,256]{1,0:T(8,128)(2,1)} %grad.1.gq), channel_id=1, source_target_pairs={{0,64},{64,0},{1,65},{65,1},{2,66},{66,2},{3,67},{67,3},{4,68},{68... | collective-permute-start | bytes 589832 | tf_op jit(solution)/shard_map/ppermute | solution.py:20
  154.1 4.5 %collective-permute-start.14 = (bf16[384,256]{1,0:T(8,128)(2,1)}, bf16[384,256]{1,0:T(8,128)(2,1)S(1)}, u32[]{:S(2)}, u32[]{:S(2)}) collective-permute-start(bf16[384,256]{1,0:T(8,128)(2,1)} %grad.1.gq), channel_id=1, source_target_pairs={{0,16},{16,0},{1,17},{17,1},{2,18},{18,2},{3,19},{19,3},{4,20},{20... | collective-permute-start | bytes 589832 | tf_op jit(solution)/shard_map/ppermute | solution.py:20
  158.6 1.4 collective-permute-done.15.gq_near
  160.0 4.1 %collective-permute-start.16 = (bf16[384,256]{1,0:T(8,128)(2,1)S(1)}, bf16[384,256]{1,0:T(8,128)(2,1)S(1)}, u32[]{:S(2)}, u32[]{:S(2)}) collective-permute-start(bf16[384,256]{1,0:T(8,128)(2,1)S(1)} %collective-permute-done.15.gq_near), channel_id=1, source_target_pairs={{0,16},{16,0},{1,17},{17,1},{2,18},{18,2},{3,19},{19,3},{4,20},{20... | collective-permute-start | bytes 589832 | tf_op jit(solution)/shard_map/ppermute | solution.py:20
  164.2 1.0 collective-permute-done.16.gq_near_core
  165.2 0.7 copy-done.13
  165.9 4.8 %outer.1 = bf16[1280,256]{1,0:T(8,128)(2,1)} custom-call(s32[2]{0:T(128)} %pad_add_fusion.place, bf16[2,1280,768]{2,1,0:T(8,128)(2,1)} %bitcast.19, bf16[1280,768]{1,0:T(8,128)(2,1)} %copy-done.4, bf16[384,256]{1,0:T(8,128)(2,1)} %grad.1.gq, bf16[384,256]{1,0:T(8,128)(2,1)} %copy-done.12, bf16[384,256]{1,0:T(8,128)(2,1)} %copy-done.11, ...), custom_call_target="tpu_custom_call" | custom-call | flops 1006632960 | bytes 3932160 | tf_op jit(solution)/shard_map/outer/pallas_call | solution.py:253
  170.7 25.2 %all_to_all.17 = bf16[8,160,256]{2,1,0:T(8,128)(2,1)S(1)} all-to-all(bf16[8,160,256]{2,1,0:T(8,128)(2,1)} %bitcast.20), channel_id=1, replica_groups=mesh['yh'=4,'yl'=2,'zl'=2,'c'=2,'x'=4,'zh'=4] {'zl','yh'}, dimensions={0} | all-to-all | bytes 1310720 | tf_op jit(solution)/shard_map/all_to_all | solution.py:273
  196.0 0.8 convert_reduce_fusion
  (52 shorter events, 0.2 us)
Async XLA Ops:
  6.5 92.3 %all-gather.2.cloned.1.call-start = ((), (), s32[]{:S(2)}) async-start(), calls=%async_computation.3 | async-start | bytes 4177920 | tf_op jit(solution)/shard_map/all_gather | solution.py:287
  7.5 9.7 %collective-permute-start = (bf16[160,384]{1,0:T(8,128)(2,1)S(1)}, bf16[160,384]{1,0:T(8,128)(2,1)S(1)}, u32[]{:S(2)}, u32[]{:S(2)}) collective-permute-start(bf16[160,384]{1,0:T(8,128)(2,1)S(1)} %get-tuple-element.34), channel_id=1, source_target_pairs={{0,16},{16,0},{1,17},{17,1},{2,18},{18,2},{3,19},{19,3},{4,20},{20... | collective-permute-start | bytes 368648 | tf_op jit(solution)/shard_map/ppermute | solution.py:20
  19.1 12.8 %copy-start.10 = (bf16[4,160,256]{2,1,0:T(8,128)(2,1)}, bf16[4,160,256]{2,1,0:T(8,128)(2,1)S(1)}, u32[]{:S(2)}) copy-start(bf16[4,160,256]{2,1,0:T(8,128)(2,1)S(1)} %pad_maximum_fusion.2.refs_0_) | copy-start | bytes 983044
  19.1 10.8 %collective-permute-start.1 = (bf16[4,160,256]{2,1,0:T(8,128)(2,1)S(1)}, bf16[4,160,256]{2,1,0:T(8,128)(2,1)S(1)}, u32[]{:S(2)}, u32[]{:S(2)}) collective-permute-start(bf16[4,160,256]{2,1,0:T(8,128)(2,1)S(1)} %pad_maximum_fusion.2.refs_0_), channel_id=1, source_target_pairs={{0,32},{32,0},{1,33},{33,1},{2,34},{34,2},{3,35},{35,3},{4,36},{36... | collective-permute-start | bytes 983048 | tf_op jit(solution)/shard_map/ppermute | solution.py:20
  21.0 10.8 %collective-permute-start.2 = (bf16[4,160,256]{2,1,0:T(8,128)(2,1)S(1)}, bf16[4,160,256]{2,1,0:T(8,128)(2,1)S(1)}, u32[]{:S(2)}, u32[]{:S(2)}) collective-permute-start(bf16[4,160,256]{2,1,0:T(8,128)(2,1)S(1)} %pad_maximum_fusion.2.refs_0_), channel_id=1, source_target_pairs={{0,448},{64,0},{128,64},{192,128},{256,192},{320,256},{384,320},{4... | collective-permute-start | bytes 983048 | tf_op jit(solution)/shard_map/ppermute | solution.py:20
  22.9 11.5 %collective-permute-start.7 = (bf16[4,160,256]{2,1,0:T(8,128)(2,1)S(1)}, bf16[4,160,256]{2,1,0:T(8,128)(2,1)S(1)}, u32[]{:S(2)}, u32[]{:S(2)}) collective-permute-start(bf16[4,160,256]{2,1,0:T(8,128)(2,1)S(1)} %pad_maximum_fusion.2.refs_0_), channel_id=1, source_target_pairs={{0,64},{64,128},{128,192},{192,256},{256,320},{320,384},{384,448},... | collective-permute-start | bytes 983048 | tf_op jit(solution)/shard_map/ppermute | solution.py:20
  29.9 39.2 %copy-start.7 = (bf16[4,160,256]{2,1,0:T(8,128)(2,1)}, bf16[4,160,256]{2,1,0:T(8,128)(2,1)S(1)}, u32[]{:S(2)}) copy-start(bf16[4,160,256]{2,1,0:T(8,128)(2,1)S(1)} %collective-permute-done.1.refs_1_) | copy-start | bytes 983044
  31.9 37.2 %copy-start.8 = (bf16[4,160,256]{2,1,0:T(8,128)(2,1)}, bf16[4,160,256]{2,1,0:T(8,128)(2,1)S(1)}, u32[]{:S(2)}) copy-start(bf16[4,160,256]{2,1,0:T(8,128)(2,1)S(1)} %collective-permute-done.2.refs_3_) | copy-start | bytes 983044
  34.5 34.6 %copy-start.9 = (bf16[4,160,256]{2,1,0:T(8,128)(2,1)}, bf16[4,160,256]{2,1,0:T(8,128)(2,1)S(1)}, u32[]{:S(2)}) copy-start(bf16[4,160,256]{2,1,0:T(8,128)(2,1)S(1)} %collective-permute-done.7.refs_2_) | copy-start | bytes 983044
  34.6 17.6 %collective-permute-start.8 = (bf16[8,160,256]{2,1,0:T(8,128)(2,1)S(1)}, bf16[8,160,256]{2,1,0:T(8,128)(2,1)S(1)}, u32[]{:S(2)}, u32[]{:S(2)}) collective-permute-start(bf16[8,160,256]{2,1,0:T(8,128)(2,1)S(1)} %get-tuple-element.31), channel_id=1, source_target_pairs={{0,64},{64,128},{128,192},{192,256},{256,320},{320,384},{384,448},... | collective-permute-start | bytes 1966088 | tf_op jit(solution)/shard_map/ppermute | solution.py:20
  37.0 17.2 %collective-permute-start.3 = (bf16[8,160,256]{2,1,0:T(8,128)(2,1)S(1)}, bf16[8,160,256]{2,1,0:T(8,128)(2,1)S(1)}, u32[]{:S(2)}, u32[]{:S(2)}) collective-permute-start(bf16[8,160,256]{2,1,0:T(8,128)(2,1)S(1)} %get-tuple-element.32), channel_id=1, source_target_pairs={{0,448},{64,0},{128,64},{192,128},{256,192},{320,256},{384,320},{4... | collective-permute-start | bytes 1966088 | tf_op jit(solution)/shard_map/ppermute | solution.py:20
  52.2 6.5 %copy-start.18 = (bf16[8,160,256]{2,1,0:T(8,128)(2,1)}, bf16[8,160,256]{2,1,0:T(8,128)(2,1)S(1)}, u32[]{:S(2)}) copy-start(bf16[8,160,256]{2,1,0:T(8,128)(2,1)S(1)} %collective-permute-done.8.refs_4_) | copy-start | bytes 1966084
  52.2 16.8 %collective-permute-start.9 = (bf16[8,160,256]{2,1,0:T(8,128)(2,1)S(1)}, bf16[8,160,256]{2,1,0:T(8,128)(2,1)S(1)}, u32[]{:S(2)}, u32[]{:S(2)}) collective-permute-start(bf16[8,160,256]{2,1,0:T(8,128)(2,1)S(1)} %collective-permute-done.8.refs_4_), channel_id=1, source_target_pairs={{0,64},{64,128},{128,192},{192,256},{256,320},{320,384},{384,448},... | collective-permute-start | bytes 1966088 | tf_op jit(solution)/shard_map/ppermute | solution.py:20
  54.2 16.9 %copy-start.19 = (bf16[8,160,256]{2,1,0:T(8,128)(2,1)}, bf16[8,160,256]{2,1,0:T(8,128)(2,1)S(1)}, u32[]{:S(2)}) copy-start(bf16[8,160,256]{2,1,0:T(8,128)(2,1)S(1)} %collective-permute-done.3.refs_5_) | copy-start | bytes 1966084
  54.2 16.9 %collective-permute-start.4 = (bf16[8,160,256]{2,1,0:T(8,128)(2,1)S(1)}, bf16[8,160,256]{2,1,0:T(8,128)(2,1)S(1)}, u32[]{:S(2)}, u32[]{:S(2)}) collective-permute-start(bf16[8,160,256]{2,1,0:T(8,128)(2,1)S(1)} %collective-permute-done.3.refs_5_), channel_id=1, source_target_pairs={{0,448},{64,0},{128,64},{192,128},{256,192},{320,256},{384,320},{4... | collective-permute-start | bytes 1966088 | tf_op jit(solution)/shard_map/ppermute | solution.py:20
  69.0 29.8 %copy-start.5 = (bf16[8,160,256]{2,1,0:T(8,128)(2,1)}, bf16[8,160,256]{2,1,0:T(8,128)(2,1)S(1)}, u32[]{:S(2)}) copy-start(bf16[8,160,256]{2,1,0:T(8,128)(2,1)S(1)} %collective-permute-done.9.refs_6_) | copy-start | bytes 1966084
  69.1 12.5 %collective-permute-start.10 = (bf16[6,160,256]{2,1,0:T(8,128)(2,1)S(1)}, bf16[6,160,256]{2,1,0:T(8,128)(2,1)S(1)}, u32[]{:S(2)}, u32[]{:S(2)}) collective-permute-start(bf16[6,160,256]{2,1,0:T(8,128)(2,1)S(1)} %slice.18), channel_id=1, source_target_pairs={{0,64},{64,128},{128,192},{192,256},{256,320},{320,384},{384,448},... | collective-permute-start | bytes 1474568 | tf_op jit(solution)/shard_map/ppermute | solution.py:20
  71.1 27.7 %copy-start.6 = (bf16[8,160,256]{2,1,0:T(8,128)(2,1)}, bf16[8,160,256]{2,1,0:T(8,128)(2,1)S(1)}, u32[]{:S(2)}) copy-start(bf16[8,160,256]{2,1,0:T(8,128)(2,1)S(1)} %collective-permute-done.4.refs_7_) | copy-start | bytes 1966084
  71.1 12.4 %collective-permute-start.5 = (bf16[6,160,256]{2,1,0:T(8,128)(2,1)S(1)}, bf16[6,160,256]{2,1,0:T(8,128)(2,1)S(1)}, u32[]{:S(2)}, u32[]{:S(2)}) collective-permute-start(bf16[6,160,256]{2,1,0:T(8,128)(2,1)S(1)} %slice.16), channel_id=1, source_target_pairs={{0,448},{64,0},{128,64},{192,128},{256,192},{320,256},{384,320},{4... | collective-permute-start | bytes 1474568 | tf_op jit(solution)/shard_map/ppermute | solution.py:20
  81.6 1.9 copy-start.14
  81.6 7.7 %collective-permute-start.11 = (bf16[2,160,256]{2,1,0:T(8,128)(2,1)S(1)}, bf16[2,160,256]{2,1,0:T(8,128)(2,1)S(1)}, u32[]{:S(2)}, u32[]{:S(2)}) collective-permute-start(bf16[2,160,256]{2,1,0:T(8,128)(2,1)S(1)} %slice.19), channel_id=1, source_target_pairs={{0,64},{64,128},{128,192},{192,256},{256,320},{320,384},{384,448},... | collective-permute-start | bytes 491528 | tf_op jit(solution)/shard_map/ppermute | solution.py:20
  83.6 15.2 %copy-start.15 = (bf16[6,160,256]{2,1,0:T(8,128)(2,1)}, bf16[6,160,256]{2,1,0:T(8,128)(2,1)S(1)}, u32[]{:S(2)}) copy-start(bf16[6,160,256]{2,1,0:T(8,128)(2,1)S(1)} %collective-permute-done.5.refs_9_) | copy-start | bytes 1474564
  83.6 6.8 %collective-permute-start.6 = (bf16[2,160,256]{2,1,0:T(8,128)(2,1)S(1)}, bf16[2,160,256]{2,1,0:T(8,128)(2,1)S(1)}, u32[]{:S(2)}, u32[]{:S(2)}) collective-permute-start(bf16[2,160,256]{2,1,0:T(8,128)(2,1)S(1)} %slice.17), channel_id=1, source_target_pairs={{0,448},{64,0},{128,64},{192,128},{256,192},{320,256},{384,320},{4... | collective-permute-start | bytes 491528 | tf_op jit(solution)/shard_map/ppermute | solution.py:20
  88.8 25.1 %copy-start.16 = (f32[256]{0:T(256)S(1)}, f32[256]{0:T(256)}, u32[]{:S(2)}) copy-start(f32[256]{0:T(256)} %param.13) | copy-start | bytes 3076
  88.8 25.1 %copy-start.17 = (f32[256]{0:T(256)S(1)}, f32[256]{0:T(256)}, u32[]{:S(2)}) copy-start(f32[256]{0:T(256)} %param.12) | copy-start | bytes 3076
  89.3 9.5 %copy-start.20 = (bf16[2,160,256]{2,1,0:T(8,128)(2,1)}, bf16[2,160,256]{2,1,0:T(8,128)(2,1)S(1)}, u32[]{:S(2)}) copy-start(bf16[2,160,256]{2,1,0:T(8,128)(2,1)S(1)} %collective-permute-done.11.refs_10_) | copy-start | bytes 491524
  90.4 0.7 copy-start.21
  108.1 5.9 %collective-permute-start.13 = (f32[384,1024]{1,0:T(8,128)}, f32[384,1024]{1,0:T(8,128)S(1)}, u32[]{:S(2)}, u32[]{:S(2)}) collective-permute-start(f32[384,1024]{1,0:T(8,128)} %get-tuple-element.23), channel_id=1, source_target_pairs={{0,16},{16,0},{1,17},{17,1},{2,18},{18,2},{3,19},{19,3},{4,20},{20... | collective-permute-start | bytes 4718600 | tf_op jit(solution)/shard_map/ppermute | solution.py:20
  110.7 53.5 %collective-permute-start.12 = (bf16[1280,768]{1,0:T(8,128)(2,1)}, bf16[1280,768]{1,0:T(8,128)(2,1)S(1)}, u32[]{:S(2)}, u32[]{:S(2)}) collective-permute-start(bf16[1280,768]{1,0:T(8,128)(2,1)} %get-tuple-element.21), channel_id=1, source_target_pairs={{0,64},{64,0},{1,65},{65,1},{2,66},{66,2},{3,67},{67,3},{4,68},{68... | collective-permute-start | bytes 5898248 | tf_op jit(solution)/shard_map/ppermute | solution.py:20
  114.0 1.4 copy-start.1
  115.7 33.9 %copy-start = (f32[384,768]{1,0:T(8,128)}, f32[384,768]{1,0:T(8,128)S(1)}, u32[]{:S(2)}) copy-start(f32[384,768]{1,0:T(8,128)S(1)} %get-tuple-element.26.qkd.q) | copy-start | bytes 3538948
  134.4 15.2 %copy-start.2 = (f32[16,9,128]{2,1,0:T(8,128)}, f32[16,9,128]{2,1,0:T(8,128)S(1)}, u32[]{:S(2)}) copy-start(f32[16,9,128]{2,1,0:T(8,128)S(1)} %all_to_all.15.sums) | copy-start | bytes 221188
  136.8 0.8 copy-start.3
  152.0 8.0 %collective-permute-start.15 = (bf16[384,256]{1,0:T(8,128)(2,1)}, bf16[384,256]{1,0:T(8,128)(2,1)S(1)}, u32[]{:S(2)}, u32[]{:S(2)}) collective-permute-start(bf16[384,256]{1,0:T(8,128)(2,1)} %grad.1.gq), channel_id=1, source_target_pairs={{0,64},{64,0},{1,65},{65,1},{2,66},{66,2},{3,67},{67,3},{4,68},{68... | collective-permute-start | bytes 589832 | tf_op jit(solution)/shard_map/ppermute | solution.py:20
  154.1 10.1 %collective-permute-start.14 = (bf16[384,256]{1,0:T(8,128)(2,1)}, bf16[384,256]{1,0:T(8,128)(2,1)S(1)}, u32[]{:S(2)}, u32[]{:S(2)}) collective-permute-start(bf16[384,256]{1,0:T(8,128)(2,1)} %grad.1.gq), channel_id=1, source_target_pairs={{0,16},{16,0},{1,17},{17,1},{2,18},{18,2},{3,19},{19,3},{4,20},{20... | collective-permute-start | bytes 589832 | tf_op jit(solution)/shard_map/ppermute | solution.py:20
  160.0 4.2 %copy-start.11 = (bf16[384,256]{1,0:T(8,128)(2,1)}, bf16[384,256]{1,0:T(8,128)(2,1)S(1)}, u32[]{:S(2)}) copy-start(bf16[384,256]{1,0:T(8,128)(2,1)S(1)} %collective-permute-done.15.gq_near) | copy-start | bytes 589828
  160.0 5.2 %collective-permute-start.16 = (bf16[384,256]{1,0:T(8,128)(2,1)S(1)}, bf16[384,256]{1,0:T(8,128)(2,1)S(1)}, u32[]{:S(2)}, u32[]{:S(2)}) collective-permute-start(bf16[384,256]{1,0:T(8,128)(2,1)S(1)} %collective-permute-done.15.gq_near), channel_id=1, source_target_pairs={{0,16},{16,0},{1,17},{17,1},{2,18},{18,2},{3,19},{19,3},{4,20},{20... | collective-permute-start | bytes 589832 | tf_op jit(solution)/shard_map/ppermute | solution.py:20
  164.2 1.0 copy-start.12
  164.2 1.7 copy-start.4
  165.2 0.7 copy-start.13
Sparse Core Ops, SparseCore 0:
  18.1 80.6 all-gather.1

commit v4 on v3

--- a/solution.py
+++ b/solution.py
@@ -236,37 +236,25 @@
     )(sums, back, qkd, weighted)
 
 
-def outer_kernel(place, x, near, gq, gq_core, gq_near, gq_near_core, term):
+def outer_kernel(x, near, gq, gq_core, gq_near, gq_near_core, term):
     length = gq.shape[0]
-    total = jnp.dot(x[0, :, :length], gq[...], preferred_element_type=F32)
-    total += jnp.dot(x[0, :, length:], gq_core[...], preferred_element_type=F32)
+    total = jnp.dot(x[:, :length], gq[...], preferred_element_type=F32)
+    total += jnp.dot(x[:, length:], gq_core[...], preferred_element_type=F32)
     total += jnp.dot(near[:, :length], gq_near[...], preferred_element_type=F32)
     total += jnp.dot(near[:, length:], gq_near_core[...], preferred_element_type=F32)
     term[...] = total.astype(BF)
 
 
-def outer(place, x, near, grads):
+def outer(x, near, grads):
     rows, tokens = near.shape
-    length, wide = grads[0].shape
-    steps = 2
-    block = rows // steps
+    wide = grads[0].shape[1]
     return pl.pallas_call(
         outer_kernel,
-        grid_spec=pltpu.PrefetchScalarGridSpec(
-            num_scalar_prefetch=1,
-            grid=(steps,),
-            in_specs=[
-                pl.BlockSpec((1, block, tokens), lambda k, place: (lax.rem(place[0], 2), k, 0)),
-                pl.BlockSpec((block, tokens), lambda k, place: (k, 0)),
-            ]
-            + [pl.BlockSpec((length, wide), lambda k, place: (0, 0))] * 4,
-            out_specs=pl.BlockSpec((block, wide), lambda k, place: (k, 0)),
-        ),
         out_shape=jax.ShapeDtypeStruct((rows, wide), BF),
-        compiler_params=pltpu.CompilerParams(vmem_limit_bytes=62 * MIB),
+        compiler_params=pltpu.CompilerParams(vmem_limit_bytes=16 * MIB),
         cost_estimate=pl.CostEstimate(flops=4 * rows * tokens * wide, bytes_accessed=4 * rows * tokens, transcendentals=0),
         name="outer",
-    )(place, x.reshape(2, rows, tokens), near, *grads)
+    )(x, near, *grads)
 
 
 def to_all(value, axes):
@@ -302,7 +290,9 @@
 
     gq_near = shift(gq, "yl", 1, 2)
     gq_core = shift(gq, "c", 1, 2)
-    term = outer(place, x, near, (gq, gq_core, gq_near, shift(gq_near, "c", 1, 2)))
+    halves, gq = tie((x.reshape(2, -1, x.shape[1]), gq))
+    mine = lax.dynamic_index_in_dim(halves, lax.axis_index("yl"), 0, keepdims=False)
+    term = outer(mine, near, (gq, gq_core, gq_near, shift(gq_near, "c", 1, 2)))
     got = to_all(term.reshape(8, -1, wide), ("zl", "yh"))
     return jnp.sum(got.astype(F32), axis=0)
 

time: 205 us -> 202 us (0.985)
  Pallas kernels: 19.1 us -> 15.9 us
    pallas_call x1, Pallas kernels: 4.81 us -> 1.53 us  [outer(): pl.pallas_call(outer_kernel, out_shape=jax.ShapeDtypeStruct((rows, wide),...]
  transfers between devices with their start and end apart: 18 -> 18, of which waited for: 13 -> 12; matrix products, arithmetic and copies ran while one was open for 1% -> 2% of each run, Pallas kernels for 2% -> 3%
where the time goes in v4:
time: 202 us; the launch traced here: 200 us
  starting transfers between devices  58.4 us (29%)
  blocking collectives  55.8 us (28%)
  waiting for transfers between devices  47.3 us (23%)
  Pallas kernels  15.9 us (8%)
  between operations  13.8 us (7%)
  local copies, waits for them, and re-layouts  5.64 us (3%)
  other arithmetic  3.28 us (2%)
    ppermute x17, starting transfers between devices, shift(): lax.ppermute(value, axis, [(i, (i + by) % size) for i in range(size)])  58.4 us
    all_to_all x3, blocking collectives, to_all(): return lax.all_to_all(value, axes, 0, 0, tiled=True)  55.8 us
    ppermute x17, waiting for transfers between devices, shift(): lax.ppermute(value, axis, [(i, (i + by) % size) for i in range(size)])  39.6 us
    pallas_call x1, Pallas kernels, project(): pl.pallas_call(functools.partial(project_kernel, layout=tuple(layout), wi...  9.24 us
    all_gather x1, waiting for transfers between devices, on_device(): x = lax.all_gather(x, ('zh', 'x'), axis=0, tiled=True)  7.73 us
  transfers between devices with their start and end apart: 18, of which 12 were waited for; matrix products, arithmetic and copies ran while one was open for 2% of the time, Pallas kernels for 3%

profile of v4, /device:TPU:1, one launch (start us, length us, event | category | flops | bytes accessed | tf_op | source)
XLA Modules:
  0.0 200.1 jit_solution(15320397273775286602)
XLA Ops:
  6.5 1.0 dynamic-slice_bitcast_fusion.2
  7.5 8.8 %collective-permute-start = (bf16[160,384]{1,0:T(8,128)(2,1)S(1)}, bf16[160,384]{1,0:T(8,128)(2,1)S(1)}, u32[]{:S(2)}, u32[]{:S(2)}) collective-permute-start(bf16[160,384]{1,0:T(8,128)(2,1)S(1)} %get-tuple-element.38), channel_id=1, source_target_pairs={{0,16},{16,0},{1,17},{17,1},{2,18},{18,2},{3,19},{19,3},{4,20},{20... | collective-permute-start | bytes 368648 | tf_op jit(solution)/shard_map/ppermute | solution.py:20
  16.3 1.0 collective-permute-done
  17.3 0.7 pad_maximum_fusion.3
  18.0 0.0 all-gather.2.cloned.1.call-update
  18.0 1.1 pad_maximum_fusion.2.refs_0_
  19.1 1.9 collective-permute-start.1
  21.0 1.9 collective-permute-start.2
  23.0 3.4 %collective-permute-start.7 = (bf16[4,160,256]{2,1,0:T(8,128)(2,1)S(1)}, bf16[4,160,256]{2,1,0:T(8,128)(2,1)S(1)}, u32[]{:S(2)}, u32[]{:S(2)}) collective-permute-start(bf16[4,160,256]{2,1,0:T(8,128)(2,1)S(1)} %pad_maximum_fusion.2.refs_0_), channel_id=1, source_target_pairs={{0,64},{64,128},{128,192},{192,256},{256,320},{320,384},{384,448},... | collective-permute-start | bytes 983048 | tf_op jit(solution)/shard_map/ppermute | solution.py:20
  26.3 3.6 %collective-permute-done.1.refs_1_ = bf16[4,160,256]{2,1,0:T(8,128)(2,1)S(1)} collective-permute-done((bf16[4,160,256]{2,1,0:T(8,128)(2,1)S(1)}, bf16[4,160,256]{2,1,0:T(8,128)(2,1)S(1)}, u32[]{:S(2)}, u32[]{:S(2)}) %collective-permute-start.1) | collective-permute-done | bytes 327712 | tf_op jit(solution)/shard_map/ppermute | solution.py:20
  29.9 1.9 collective-permute-done.2.refs_3_
  31.9 2.6 %collective-permute-done.7.refs_2_ = bf16[4,160,256]{2,1,0:T(8,128)(2,1)S(1)} collective-permute-done((bf16[4,160,256]{2,1,0:T(8,128)(2,1)S(1)}, bf16[4,160,256]{2,1,0:T(8,128)(2,1)S(1)}, u32[]{:S(2)}, u32[]{:S(2)}) %collective-permute-start.7) | collective-permute-done | bytes 327712 | tf_op jit(solution)/shard_map/ppermute | solution.py:20
  34.5 0.1 pad_maximum_fusion.1
  34.6 2.3 %collective-permute-start.8 = (bf16[8,160,256]{2,1,0:T(8,128)(2,1)S(1)}, bf16[8,160,256]{2,1,0:T(8,128)(2,1)S(1)}, u32[]{:S(2)}, u32[]{:S(2)}) collective-permute-start(bf16[8,160,256]{2,1,0:T(8,128)(2,1)S(1)} %get-tuple-element.35), channel_id=1, source_target_pairs={{0,64},{64,128},{128,192},{192,256},{256,320},{320,384},{384,448},... | collective-permute-start | bytes 1966088 | tf_op jit(solution)/shard_map/ppermute | solution.py:20
  37.0 4.2 %collective-permute-start.3 = (bf16[8,160,256]{2,1,0:T(8,128)(2,1)S(1)}, bf16[8,160,256]{2,1,0:T(8,128)(2,1)S(1)}, u32[]{:S(2)}, u32[]{:S(2)}) collective-permute-start(bf16[8,160,256]{2,1,0:T(8,128)(2,1)S(1)} %get-tuple-element.36), channel_id=1, source_target_pairs={{0,448},{64,0},{128,64},{192,128},{256,192},{320,256},{384,320},{4... | collective-permute-start | bytes 1966088 | tf_op jit(solution)/shard_map/ppermute | solution.py:20
  41.1 11.1 %collective-permute-done.8.refs_4_ = bf16[8,160,256]{2,1,0:T(8,128)(2,1)S(1)} collective-permute-done((bf16[8,160,256]{2,1,0:T(8,128)(2,1)S(1)}, bf16[8,160,256]{2,1,0:T(8,128)(2,1)S(1)}, u32[]{:S(2)}, u32[]{:S(2)}) %collective-permute-start.8) | collective-permute-done | bytes 655392 | tf_op jit(solution)/shard_map/ppermute | solution.py:20
  52.3 1.9 collective-permute-start.9
  54.2 4.6 %collective-permute-start.4 = (bf16[8,160,256]{2,1,0:T(8,128)(2,1)S(1)}, bf16[8,160,256]{2,1,0:T(8,128)(2,1)S(1)}, u32[]{:S(2)}, u32[]{:S(2)}) collective-permute-start(bf16[8,160,256]{2,1,0:T(8,128)(2,1)S(1)} %collective-permute-done.3.refs_5_), channel_id=1, source_target_pairs={{0,448},{64,0},{128,64},{192,128},{256,192},{320,256},{384,320},{4... | collective-permute-start | bytes 1966088 | tf_op jit(solution)/shard_map/ppermute | solution.py:20
  58.8 10.3 %collective-permute-done.9.refs_6_ = bf16[8,160,256]{2,1,0:T(8,128)(2,1)S(1)} collective-permute-done((bf16[8,160,256]{2,1,0:T(8,128)(2,1)S(1)}, bf16[8,160,256]{2,1,0:T(8,128)(2,1)S(1)}, u32[]{:S(2)}, u32[]{:S(2)}) %collective-permute-start.9) | collective-permute-done | bytes 655392 | tf_op jit(solution)/shard_map/ppermute | solution.py:20
  69.1 1.9 collective-permute-start.10
  71.1 4.6 %collective-permute-start.5 = (bf16[6,160,256]{2,1,0:T(8,128)(2,1)S(1)}, bf16[6,160,256]{2,1,0:T(8,128)(2,1)S(1)}, u32[]{:S(2)}, u32[]{:S(2)}) collective-permute-start(bf16[6,160,256]{2,1,0:T(8,128)(2,1)S(1)} %slice.16), channel_id=1, source_target_pairs={{0,448},{64,0},{128,64},{192,128},{256,192},{320,256},{384,320},{4... | collective-permute-start | bytes 1474568 | tf_op jit(solution)/shard_map/ppermute | solution.py:20
  75.7 5.9 %collective-permute-done.10.refs_8_ = bf16[6,160,256]{2,1,0:T(8,128)(2,1)S(1)} collective-permute-done((bf16[6,160,256]{2,1,0:T(8,128)(2,1)S(1)}, bf16[6,160,256]{2,1,0:T(8,128)(2,1)S(1)}, u32[]{:S(2)}, u32[]{:S(2)}) %collective-permute-start.10) | collective-permute-done | bytes 491552 | tf_op jit(solution)/shard_map/ppermute | solution.py:20
  81.6 1.9 collective-permute-start.11
  83.6 4.6 %collective-permute-start.6 = (bf16[2,160,256]{2,1,0:T(8,128)(2,1)S(1)}, bf16[2,160,256]{2,1,0:T(8,128)(2,1)S(1)}, u32[]{:S(2)}, u32[]{:S(2)}) collective-permute-start(bf16[2,160,256]{2,1,0:T(8,128)(2,1)S(1)} %slice.17), channel_id=1, source_target_pairs={{0,448},{64,0},{128,64},{192,128},{256,192},{320,256},{384,320},{4... | collective-permute-start | bytes 491528 | tf_op jit(solution)/shard_map/ppermute | solution.py:20
  88.2 0.6 pad_add_fusion.place
  88.8 0.5 collective-permute-done.11.refs_10_
  89.3 1.1 collective-permute-done.6.refs_11_
  90.4 0.6 copy-done.18
  91.1 7.7 %all-gather.2.cloned.1.call-done.x_hbm = bf16[2560,768]{1,0:T(8,128)(2,1)} async-done(((bf16[160,768]{1,0:T(8,128)(2,1)}), bf16[2560,768]{1,0:T(8,128)(2,1)}) %all-gather.2.cloned.1.call-update) | async-done | bytes 3932176 | tf_op jit(solution)/shard_map/all_gather | solution.py:275
  98.8 9.2 %project.1 = (f32[384,1024]{1,0:T(8,128)}, f32[384,1024]{1,0:T(8,128)}, bf16[1280,768]{1,0:T(8,128)(2,1)}) custom-call(s32[2]{0:T(128)} %pad_add_fusion.place, bf16[2560,768]{1,0:T(8,128)(2,1)} %all-gather.2.cloned.1.call-done.x_hbm, bf16[4,160,256]{2,1,0:T(8,128)(2,1)} %copy-done.10, bf16[4,160,256]{2,1,0:T(8,128)(2,1)} %copy-done.7, ...), custom_call_target="tpu_custom_call" | custom-call | flops 4026531840 | bytes 9175040 | tf_op jit(solution)/shard_map/project/pallas_call | solution.py:94
  108.1 2.6 %collective-permute-start.12 = (f32[384,1024]{1,0:T(8,128)}, f32[384,1024]{1,0:T(8,128)S(1)}, u32[]{:S(2)}, u32[]{:S(2)}) collective-permute-start(f32[384,1024]{1,0:T(8,128)} %get-tuple-element.24), channel_id=1, source_target_pairs={{0,16},{16,0},{1,17},{17,1},{2,18},{18,2},{3,19},{19,3},{4,20},{20... | collective-permute-start | bytes 4718600 | tf_op jit(solution)/shard_map/ppermute | solution.py:20
  110.7 3.1 %collective-permute-start.13 = (bf16[1280,768]{1,0:T(8,128)(2,1)}, bf16[1280,768]{1,0:T(8,128)(2,1)S(1)}, u32[]{:S(2)}, u32[]{:S(2)}) collective-permute-start(bf16[1280,768]{1,0:T(8,128)(2,1)} %get-tuple-element.33), channel_id=1, source_target_pairs={{0,64},{64,0},{1,65},{65,1},{2,66},{66,2},{3,67},{67,3},{4,68},{68... | collective-permute-start | bytes 5898248 | tf_op jit(solution)/shard_map/ppermute | solution.py:20
  113.9 0.1 collective-permute-done.12.two
  113.9 1.4 copy-done.1
  115.3 0.4 merge.1
  115.7 18.7 %all_to_all.15.sums = f32[16,9,128]{2,1,0:T(8,128)S(1)} all-to-all(f32[16,9,128]{2,1,0:T(8,128)S(1)} %get-tuple-element.26), channel_id=1, replica_groups=mesh['yh'=4,'yl'=2,'zl'=2,'c'=2,'x'=4,'zh'=4] {'x','zh'}, dimensions={0} | all-to-all | bytes 147456 | tf_op jit(solution)/shard_map/all_to_all | solution.py:261
  134.4 2.4 %attend.1 = (f32[384,256]{1,0:T(8,128)S(1)}, f32[16,3,128]{2,1,0:T(4,128)S(1)}) custom-call(f32[16,9,128]{2,1,0:T(8,128)S(1)} %all_to_all.15.sums, f32[384,768]{1,0:T(8,128)S(1)} %get-tuple-element.27.qkd.q, bf16[384,256]{1,0:T(8,128)(2,1)S(1)} %get-tuple-element.28.value, f32[2,256]{1,0:T(2,128)S(1)} %pad_maximum_fusion.4.gains), custom_call_target="tpu_custom_call" | custom-call | tf_op jit(solution)/shard_map/attend/pallas_call | solution.py:205
  136.8 0.8 copy-done.4
  137.5 12.1 %all_to_all.16.back = f32[16,3,128]{2,1,0:T(4,128)} all-to-all(f32[16,3,128]{2,1,0:T(4,128)S(1)} %get-tuple-element.30), channel_id=1, replica_groups=mesh['yh'=4,'yl'=2,'zl'=2,'c'=2,'x'=4,'zh'=4] {'x','zh'}, dimensions={0} | all-to-all | bytes 49152 | tf_op jit(solution)/shard_map/all_to_all | solution.py:261
  149.6 2.3 %grad.1.gq = bf16[384,256]{1,0:T(8,128)(2,1)} custom-call(f32[16,9,128]{2,1,0:T(8,128)} %copy-done.2, f32[16,3,128]{2,1,0:T(4,128)} %all_to_all.16.back, f32[384,768]{1,0:T(8,128)} %copy-done, f32[384,256]{1,0:T(8,128)} %copy-done.4), custom_call_target="tpu_custom_call" | custom-call | tf_op jit(solution)/shard_map/grad/pallas_call | solution.py:224
  152.0 2.1 %collective-permute-start.15 = (bf16[384,256]{1,0:T(8,128)(2,1)}, bf16[384,256]{1,0:T(8,128)(2,1)S(1)}, u32[]{:S(2)}, u32[]{:S(2)}) collective-permute-start(bf16[384,256]{1,0:T(8,128)(2,1)} %grad.1.gq), channel_id=1, source_target_pairs={{0,64},{64,0},{1,65},{65,1},{2,66},{66,2},{3,67},{67,3},{4,68},{68... | collective-permute-start | bytes 589832 | tf_op jit(solution)/shard_map/ppermute | solution.py:20
  154.0 4.5 %collective-permute-start.14 = (bf16[384,256]{1,0:T(8,128)(2,1)}, bf16[384,256]{1,0:T(8,128)(2,1)S(1)}, u32[]{:S(2)}, u32[]{:S(2)}) collective-permute-start(bf16[384,256]{1,0:T(8,128)(2,1)} %grad.1.gq), channel_id=1, source_target_pairs={{0,16},{16,0},{1,17},{17,1},{2,18},{18,2},{3,19},{19,3},{4,20},{20... | collective-permute-start | bytes 589832 | tf_op jit(solution)/shard_map/ppermute | solution.py:20
  158.6 1.5 collective-permute-done.15.gq_near
  160.0 4.1 %collective-permute-start.16 = (bf16[384,256]{1,0:T(8,128)(2,1)S(1)}, bf16[384,256]{1,0:T(8,128)(2,1)S(1)}, u32[]{:S(2)}, u32[]{:S(2)}) collective-permute-start(bf16[384,256]{1,0:T(8,128)(2,1)S(1)} %collective-permute-done.15.gq_near), channel_id=1, source_target_pairs={{0,16},{16,0},{1,17},{17,1},{2,18},{18,2},{3,19},{19,3},{4,20},{20... | collective-permute-start | bytes 589832 | tf_op jit(solution)/shard_map/ppermute | solution.py:20
  164.2 1.7 dynamic-slice_bitcast_fusion.x
  165.9 1.5 outer.1
  167.4 25.1 %all_to_all.17 = bf16[8,160,256]{2,1,0:T(8,128)(2,1)S(1)} all-to-all(bf16[8,160,256]{2,1,0:T(8,128)(2,1)S(1)} %bitcast.21), channel_id=1, replica_groups=mesh['yh'=4,'yl'=2,'zl'=2,'c'=2,'x'=4,'zh'=4] {'zl','yh'}, dimensions={0} | all-to-all | bytes 1310720 | tf_op jit(solution)/shard_map/all_to_all | solution.py:261
  192.5 0.8 convert_reduce_fusion
  (47 shorter events, 0.2 us)
Async XLA Ops:
  6.5 92.3 %all-gather.2.cloned.1.call-start = ((), (), s32[]{:S(2)}) async-start(), calls=%async_computation.3 | async-start | bytes 4177920 | tf_op jit(solution)/shard_map/all_gather | solution.py:275
  7.5 9.7 %collective-permute-start = (bf16[160,384]{1,0:T(8,128)(2,1)S(1)}, bf16[160,384]{1,0:T(8,128)(2,1)S(1)}, u32[]{:S(2)}, u32[]{:S(2)}) collective-permute-start(bf16[160,384]{1,0:T(8,128)(2,1)S(1)} %get-tuple-element.38), channel_id=1, source_target_pairs={{0,16},{16,0},{1,17},{17,1},{2,18},{18,2},{3,19},{19,3},{4,20},{20... | collective-permute-start | bytes 368648 | tf_op jit(solution)/shard_map/ppermute | solution.py:20
  19.1 12.8 %copy-start.10 = (bf16[4,160,256]{2,1,0:T(8,128)(2,1)}, bf16[4,160,256]{2,1,0:T(8,128)(2,1)S(1)}, u32[]{:S(2)}) copy-start(bf16[4,160,256]{2,1,0:T(8,128)(2,1)S(1)} %pad_maximum_fusion.2.refs_0_) | copy-start | bytes 983044
  19.1 10.8 %collective-permute-start.1 = (bf16[4,160,256]{2,1,0:T(8,128)(2,1)S(1)}, bf16[4,160,256]{2,1,0:T(8,128)(2,1)S(1)}, u32[]{:S(2)}, u32[]{:S(2)}) collective-permute-start(bf16[4,160,256]{2,1,0:T(8,128)(2,1)S(1)} %pad_maximum_fusion.2.refs_0_), channel_id=1, source_target_pairs={{0,32},{32,0},{1,33},{33,1},{2,34},{34,2},{3,35},{35,3},{4,36},{36... | collective-permute-start | bytes 983048 | tf_op jit(solution)/shard_map/ppermute | solution.py:20
  21.0 10.8 %collective-permute-start.2 = (bf16[4,160,256]{2,1,0:T(8,128)(2,1)S(1)}, bf16[4,160,256]{2,1,0:T(8,128)(2,1)S(1)}, u32[]{:S(2)}, u32[]{:S(2)}) collective-permute-start(bf16[4,160,256]{2,1,0:T(8,128)(2,1)S(1)} %pad_maximum_fusion.2.refs_0_), channel_id=1, source_target_pairs={{0,448},{64,0},{128,64},{192,128},{256,192},{320,256},{384,320},{4... | collective-permute-start | bytes 983048 | tf_op jit(solution)/shard_map/ppermute | solution.py:20
  23.0 11.5 %collective-permute-start.7 = (bf16[4,160,256]{2,1,0:T(8,128)(2,1)S(1)}, bf16[4,160,256]{2,1,0:T(8,128)(2,1)S(1)}, u32[]{:S(2)}, u32[]{:S(2)}) collective-permute-start(bf16[4,160,256]{2,1,0:T(8,128)(2,1)S(1)} %pad_maximum_fusion.2.refs_0_), channel_id=1, source_target_pairs={{0,64},{64,128},{128,192},{192,256},{256,320},{320,384},{384,448},... | collective-permute-start | bytes 983048 | tf_op jit(solution)/shard_map/ppermute | solution.py:20
  29.9 41.2 %copy-start.7 = (bf16[4,160,256]{2,1,0:T(8,128)(2,1)}, bf16[4,160,256]{2,1,0:T(8,128)(2,1)S(1)}, u32[]{:S(2)}) copy-start(bf16[4,160,256]{2,1,0:T(8,128)(2,1)S(1)} %collective-permute-done.1.refs_1_) | copy-start | bytes 983044
  31.9 39.2 %copy-start.8 = (bf16[4,160,256]{2,1,0:T(8,128)(2,1)}, bf16[4,160,256]{2,1,0:T(8,128)(2,1)S(1)}, u32[]{:S(2)}) copy-start(bf16[4,160,256]{2,1,0:T(8,128)(2,1)S(1)} %collective-permute-done.2.refs_3_) | copy-start | bytes 983044
  34.5 36.6 %copy-start.9 = (bf16[4,160,256]{2,1,0:T(8,128)(2,1)}, bf16[4,160,256]{2,1,0:T(8,128)(2,1)S(1)}, u32[]{:S(2)}) copy-start(bf16[4,160,256]{2,1,0:T(8,128)(2,1)S(1)} %collective-permute-done.7.refs_2_) | copy-start | bytes 983044
  34.6 17.6 %collective-permute-start.8 = (bf16[8,160,256]{2,1,0:T(8,128)(2,1)S(1)}, bf16[8,160,256]{2,1,0:T(8,128)(2,1)S(1)}, u32[]{:S(2)}, u32[]{:S(2)}) collective-permute-start(bf16[8,160,256]{2,1,0:T(8,128)(2,1)S(1)} %get-tuple-element.35), channel_id=1, source_target_pairs={{0,64},{64,128},{128,192},{192,256},{256,320},{320,384},{384,448},... | collective-permute-start | bytes 1966088 | tf_op jit(solution)/shard_map/ppermute | solution.py:20
  37.0 17.2 %collective-permute-start.3 = (bf16[8,160,256]{2,1,0:T(8,128)(2,1)S(1)}, bf16[8,160,256]{2,1,0:T(8,128)(2,1)S(1)}, u32[]{:S(2)}, u32[]{:S(2)}) collective-permute-start(bf16[8,160,256]{2,1,0:T(8,128)(2,1)S(1)} %get-tuple-element.36), channel_id=1, source_target_pairs={{0,448},{64,0},{128,64},{192,128},{256,192},{320,256},{384,320},{4... | collective-permute-start | bytes 1966088 | tf_op jit(solution)/shard_map/ppermute | solution.py:20
  52.3 46.6 %copy-start.15 = (bf16[8,160,256]{2,1,0:T(8,128)(2,1)}, bf16[8,160,256]{2,1,0:T(8,128)(2,1)S(1)}, u32[]{:S(2)}) copy-start(bf16[8,160,256]{2,1,0:T(8,128)(2,1)S(1)} %collective-permute-done.8.refs_4_) | copy-start | bytes 1966084
  52.3 16.8 %collective-permute-start.9 = (bf16[8,160,256]{2,1,0:T(8,128)(2,1)S(1)}, bf16[8,160,256]{2,1,0:T(8,128)(2,1)S(1)}, u32[]{:S(2)}, u32[]{:S(2)}) collective-permute-start(bf16[8,160,256]{2,1,0:T(8,128)(2,1)S(1)} %collective-permute-done.8.refs_4_), channel_id=1, source_target_pairs={{0,64},{64,128},{128,192},{192,256},{256,320},{320,384},{384,448},... | collective-permute-start | bytes 1966088 | tf_op jit(solution)/shard_map/ppermute | solution.py:20
  54.2 29.4 %copy-start.16 = (bf16[8,160,256]{2,1,0:T(8,128)(2,1)}, bf16[8,160,256]{2,1,0:T(8,128)(2,1)S(1)}, u32[]{:S(2)}) copy-start(bf16[8,160,256]{2,1,0:T(8,128)(2,1)S(1)} %collective-permute-done.3.refs_5_) | copy-start | bytes 1966084
  54.2 16.8 %collective-permute-start.4 = (bf16[8,160,256]{2,1,0:T(8,128)(2,1)S(1)}, bf16[8,160,256]{2,1,0:T(8,128)(2,1)S(1)}, u32[]{:S(2)}, u32[]{:S(2)}) collective-permute-start(bf16[8,160,256]{2,1,0:T(8,128)(2,1)S(1)} %collective-permute-done.3.refs_5_), channel_id=1, source_target_pairs={{0,448},{64,0},{128,64},{192,128},{256,192},{320,256},{384,320},{4... | collective-permute-start | bytes 1966088 | tf_op jit(solution)/shard_map/ppermute | solution.py:20
  69.1 29.8 %copy-start.5 = (bf16[8,160,256]{2,1,0:T(8,128)(2,1)}, bf16[8,160,256]{2,1,0:T(8,128)(2,1)S(1)}, u32[]{:S(2)}) copy-start(bf16[8,160,256]{2,1,0:T(8,128)(2,1)S(1)} %collective-permute-done.9.refs_6_) | copy-start | bytes 1966084
  69.1 12.5 %collective-permute-start.10 = (bf16[6,160,256]{2,1,0:T(8,128)(2,1)S(1)}, bf16[6,160,256]{2,1,0:T(8,128)(2,1)S(1)}, u32[]{:S(2)}, u32[]{:S(2)}) collective-permute-start(bf16[6,160,256]{2,1,0:T(8,128)(2,1)S(1)} %slice.18), channel_id=1, source_target_pairs={{0,64},{64,128},{128,192},{192,256},{256,320},{320,384},{384,448},... | collective-permute-start | bytes 1474568 | tf_op jit(solution)/shard_map/ppermute | solution.py:20
  71.0 27.8 %copy-start.6 = (bf16[8,160,256]{2,1,0:T(8,128)(2,1)}, bf16[8,160,256]{2,1,0:T(8,128)(2,1)S(1)}, u32[]{:S(2)}) copy-start(bf16[8,160,256]{2,1,0:T(8,128)(2,1)S(1)} %collective-permute-done.4.refs_7_) | copy-start | bytes 1966084
  71.1 12.4 %collective-permute-start.5 = (bf16[6,160,256]{2,1,0:T(8,128)(2,1)S(1)}, bf16[6,160,256]{2,1,0:T(8,128)(2,1)S(1)}, u32[]{:S(2)}, u32[]{:S(2)}) collective-permute-start(bf16[6,160,256]{2,1,0:T(8,128)(2,1)S(1)} %slice.16), channel_id=1, source_target_pairs={{0,448},{64,0},{128,64},{192,128},{256,192},{320,256},{384,320},{4... | collective-permute-start | bytes 1474568 | tf_op jit(solution)/shard_map/ppermute | solution.py:20
  81.6 1.9 copy-start.11
  81.6 7.7 %collective-permute-start.11 = (bf16[2,160,256]{2,1,0:T(8,128)(2,1)S(1)}, bf16[2,160,256]{2,1,0:T(8,128)(2,1)S(1)}, u32[]{:S(2)}, u32[]{:S(2)}) collective-permute-start(bf16[2,160,256]{2,1,0:T(8,128)(2,1)S(1)} %slice.19), channel_id=1, source_target_pairs={{0,64},{64,128},{128,192},{192,256},{256,320},{320,384},{384,448},... | collective-permute-start | bytes 491528 | tf_op jit(solution)/shard_map/ppermute | solution.py:20
  83.6 6.9 %copy-start.12 = (bf16[6,160,256]{2,1,0:T(8,128)(2,1)}, bf16[6,160,256]{2,1,0:T(8,128)(2,1)S(1)}, u32[]{:S(2)}) copy-start(bf16[6,160,256]{2,1,0:T(8,128)(2,1)S(1)} %collective-permute-done.5.refs_9_) | copy-start | bytes 1474564
  83.6 6.8 %collective-permute-start.6 = (bf16[2,160,256]{2,1,0:T(8,128)(2,1)S(1)}, bf16[2,160,256]{2,1,0:T(8,128)(2,1)S(1)}, u32[]{:S(2)}, u32[]{:S(2)}) collective-permute-start(bf16[2,160,256]{2,1,0:T(8,128)(2,1)S(1)} %slice.17), channel_id=1, source_target_pairs={{0,448},{64,0},{128,64},{192,128},{256,192},{320,256},{384,320},{4... | collective-permute-start | bytes 491528 | tf_op jit(solution)/shard_map/ppermute | solution.py:20
  88.8 25.0 %copy-start.13 = (f32[256]{0:T(256)S(1)}, f32[256]{0:T(256)}, u32[]{:S(2)}) copy-start(f32[256]{0:T(256)} %param.13) | copy-start | bytes 3076
  88.8 25.0 %copy-start.14 = (f32[256]{0:T(256)S(1)}, f32[256]{0:T(256)}, u32[]{:S(2)}) copy-start(f32[256]{0:T(256)} %param.12) | copy-start | bytes 3076
  89.3 1.1 copy-start.17
  90.4 0.7 copy-start.18
  108.1 5.9 %collective-permute-start.12 = (f32[384,1024]{1,0:T(8,128)}, f32[384,1024]{1,0:T(8,128)S(1)}, u32[]{:S(2)}, u32[]{:S(2)}) collective-permute-start(f32[384,1024]{1,0:T(8,128)} %get-tuple-element.24), channel_id=1, source_target_pairs={{0,16},{16,0},{1,17},{17,1},{2,18},{18,2},{3,19},{19,3},{4,20},{20... | collective-permute-start | bytes 4718600 | tf_op jit(solution)/shard_map/ppermute | solution.py:20
  110.7 55.2 %collective-permute-start.13 = (bf16[1280,768]{1,0:T(8,128)(2,1)}, bf16[1280,768]{1,0:T(8,128)(2,1)S(1)}, u32[]{:S(2)}, u32[]{:S(2)}) collective-permute-start(bf16[1280,768]{1,0:T(8,128)(2,1)} %get-tuple-element.33), channel_id=1, source_target_pairs={{0,64},{64,0},{1,65},{65,1},{2,66},{66,2},{3,67},{67,3},{4,68},{68... | collective-permute-start | bytes 5898248 | tf_op jit(solution)/shard_map/ppermute | solution.py:20
  113.9 1.4 copy-start.1
  115.7 33.9 %copy-start = (f32[384,768]{1,0:T(8,128)}, f32[384,768]{1,0:T(8,128)S(1)}, u32[]{:S(2)}) copy-start(f32[384,768]{1,0:T(8,128)S(1)} %get-tuple-element.27.qkd.q) | copy-start | bytes 3538948
  134.4 15.2 %copy-start.2 = (f32[16,9,128]{2,1,0:T(8,128)}, f32[16,9,128]{2,1,0:T(8,128)S(1)}, u32[]{:S(2)}) copy-start(f32[16,9,128]{2,1,0:T(8,128)S(1)} %all_to_all.15.sums) | copy-start | bytes 221188
  136.8 0.8 copy-start.4
  152.0 8.1 %collective-permute-start.15 = (bf16[384,256]{1,0:T(8,128)(2,1)}, bf16[384,256]{1,0:T(8,128)(2,1)S(1)}, u32[]{:S(2)}, u32[]{:S(2)}) collective-permute-start(bf16[384,256]{1,0:T(8,128)(2,1)} %grad.1.gq), channel_id=1, source_target_pairs={{0,64},{64,0},{1,65},{65,1},{2,66},{66,2},{3,67},{67,3},{4,68},{68... | collective-permute-start | bytes 589832 | tf_op jit(solution)/shard_map/ppermute | solution.py:20
  154.0 11.8 %collective-permute-start.14 = (bf16[384,256]{1,0:T(8,128)(2,1)}, bf16[384,256]{1,0:T(8,128)(2,1)S(1)}, u32[]{:S(2)}, u32[]{:S(2)}) collective-permute-start(bf16[384,256]{1,0:T(8,128)(2,1)} %grad.1.gq), channel_id=1, source_target_pairs={{0,16},{16,0},{1,17},{17,1},{2,18},{18,2},{3,19},{19,3},{4,20},{20... | collective-permute-start | bytes 589832 | tf_op jit(solution)/shard_map/ppermute | solution.py:20
  158.6 7.3 %copy-start.3 = (bf16[384,256]{1,0:T(8,128)(2,1)S(1)}, bf16[384,256]{1,0:T(8,128)(2,1)}, u32[]{:S(2)}) copy-start(bf16[384,256]{1,0:T(8,128)(2,1)} %grad.1.gq) | copy-start | bytes 589828
  160.0 5.8 %collective-permute-start.16 = (bf16[384,256]{1,0:T(8,128)(2,1)S(1)}, bf16[384,256]{1,0:T(8,128)(2,1)S(1)}, u32[]{:S(2)}, u32[]{:S(2)}) collective-permute-start(bf16[384,256]{1,0:T(8,128)(2,1)S(1)} %collective-permute-done.15.gq_near), channel_id=1, source_target_pairs={{0,16},{16,0},{1,17},{17,1},{2,18},{18,2},{3,19},{19,3},{4,20},{20... | collective-permute-start | bytes 589832 | tf_op jit(solution)/shard_map/ppermute | solution.py:20
Sparse Core Ops, SparseCore 0:
  18.2 80.6 all-gather.1

commit v5 on v4

--- a/solution.py
+++ b/solution.py
@@ -126,14 +126,15 @@
     for i, column in enumerate(columns):
         full = jnp.where(lane == i, column, full)
     full = full.T
-    rows = [full[i : i + 1, j : j + 128] for i in range(len(columns)) for j in range(0, n, 128)]
-    return jnp.broadcast_to(jnp.concatenate(rows, axis=0)[None], (16, len(rows), 128))
+    row = jnp.concatenate([full[i : i + 1] for i in range(len(columns))], axis=1)
+    return jnp.broadcast_to(row[None], (16, 1, row.shape[1]))
 
 
 def unpack(got, count):
     total = jnp.sum(got, axis=0)
-    rows = total.shape[0]
-    full = jnp.concatenate([total, jnp.zeros((128 - rows, 128), F32)], axis=0).T
+    rows = total.shape[1] // 128
+    pieces = [total[:, j * 128 : (j + 1) * 128] for j in range(rows)]
+    full = jnp.concatenate([*pieces, jnp.zeros((128 - rows, 128), F32)], axis=0).T
     each = rows // count
     return [
         jnp.concatenate([full[:, i * each + j : i * each + j + 1] for j in range(each)], axis=0) for i in range(count)
@@ -156,7 +157,7 @@
         out_shape=[
             jax.ShapeDtypeStruct((length, 3 * wide), F32),
             jax.ShapeDtypeStruct((length, wide), BF),
-            jax.ShapeDtypeStruct((16, 3 * length // 128, 128), F32),
+            jax.ShapeDtypeStruct((16, 1, 3 * length), F32),
         ],
         compiler_params=pltpu.CompilerParams(vmem_limit_bytes=16 * MIB),
         name="merge",
@@ -206,7 +207,7 @@
         functools.partial(attend_kernel, wide=wide, total=total),
         out_shape=[
             jax.ShapeDtypeStruct((length, wide), F32),
-            jax.ShapeDtypeStruct((16, length // 128, 128), F32),
+            jax.ShapeDtypeStruct((16, 1, length), F32),
         ],
         compiler_params=pltpu.CompilerParams(vmem_limit_bytes=16 * MIB),
         name="attend",

time: 202 us -> 202 us (level)
  no operation moved by 1% of the time
where the time goes in v5:
time: 202 us; the launch traced here: 200 us
  starting transfers between devices  57.9 us (29%)
  blocking collectives  54.6 us (27%)
  waiting for transfers between devices  49 us (24%)
  Pallas kernels  15.9 us (8%)
  between operations  13.8 us (7%)
  local copies, waits for them, and re-layouts  5.63 us (3%)
  other arithmetic  3.28 us (2%)
    ppermute x17, starting transfers between devices, shift(): lax.ppermute(value, axis, [(i, (i + by) % size) for i in range(size)])  57.9 us
    all_to_all x3, blocking collectives, to_all(): return lax.all_to_all(value, axes, 0, 0, tiled=True)  54.6 us
    ppermute x17, waiting for transfers between devices, shift(): lax.ppermute(value, axis, [(i, (i + by) % size) for i in range(size)])  41.2 us
    pallas_call x1, Pallas kernels, project(): pl.pallas_call(functools.partial(project_kernel, layout=tuple(layout), wi...  9.24 us
    all_gather x1, waiting for transfers between devices, on_device(): x = lax.all_gather(x, ('zh', 'x'), axis=0, tiled=True)  7.73 us
  transfers between devices with their start and end apart: 18, of which 12 were waited for; matrix products, arithmetic and copies ran while one was open for 2% of the time, Pallas kernels for 3%

profile of v5, /device:TPU:1, one launch (start us, length us, event | category | flops | bytes accessed | tf_op | source)
XLA Modules:
  0.0 200.1 jit_solution(2065132415693629665)
XLA Ops:
  6.5 1.0 dynamic-slice_bitcast_fusion.2
  7.5 8.8 %collective-permute-start = (bf16[160,384]{1,0:T(8,128)(2,1)S(1)}, bf16[160,384]{1,0:T(8,128)(2,1)S(1)}, u32[]{:S(2)}, u32[]{:S(2)}) collective-permute-start(bf16[160,384]{1,0:T(8,128)(2,1)S(1)} %get-tuple-element.38), channel_id=1, source_target_pairs={{0,16},{16,0},{1,17},{17,1},{2,18},{18,2},{3,19},{19,3},{4,20},{20... | collective-permute-start | bytes 368648 | tf_op jit(solution)/shard_map/ppermute | solution.py:20
  16.3 1.0 collective-permute-done
  17.3 0.7 pad_maximum_fusion.3
  18.0 0.0 all-gather.2.cloned.1.call-update
  18.0 1.1 pad_maximum_fusion.2.refs_0_
  19.1 1.9 collective-permute-start.1
  21.0 1.9 collective-permute-start.2
  23.0 3.4 %collective-permute-start.7 = (bf16[4,160,256]{2,1,0:T(8,128)(2,1)S(1)}, bf16[4,160,256]{2,1,0:T(8,128)(2,1)S(1)}, u32[]{:S(2)}, u32[]{:S(2)}) collective-permute-start(bf16[4,160,256]{2,1,0:T(8,128)(2,1)S(1)} %pad_maximum_fusion.2.refs_0_), channel_id=1, source_target_pairs={{0,64},{64,128},{128,192},{192,256},{256,320},{320,384},{384,448},... | collective-permute-start | bytes 983048 | tf_op jit(solution)/shard_map/ppermute | solution.py:20
  26.3 3.6 %collective-permute-done.1.refs_1_ = bf16[4,160,256]{2,1,0:T(8,128)(2,1)S(1)} collective-permute-done((bf16[4,160,256]{2,1,0:T(8,128)(2,1)S(1)}, bf16[4,160,256]{2,1,0:T(8,128)(2,1)S(1)}, u32[]{:S(2)}, u32[]{:S(2)}) %collective-permute-start.1) | collective-permute-done | bytes 327712 | tf_op jit(solution)/shard_map/ppermute | solution.py:20
  29.9 1.9 collective-permute-done.2.refs_3_
  31.9 2.6 %collective-permute-done.7.refs_2_ = bf16[4,160,256]{2,1,0:T(8,128)(2,1)S(1)} collective-permute-done((bf16[4,160,256]{2,1,0:T(8,128)(2,1)S(1)}, bf16[4,160,256]{2,1,0:T(8,128)(2,1)S(1)}, u32[]{:S(2)}, u32[]{:S(2)}) %collective-permute-start.7) | collective-permute-done | bytes 327712 | tf_op jit(solution)/shard_map/ppermute | solution.py:20
  34.5 0.1 pad_maximum_fusion.1
  34.6 2.3 %collective-permute-start.8 = (bf16[8,160,256]{2,1,0:T(8,128)(2,1)S(1)}, bf16[8,160,256]{2,1,0:T(8,128)(2,1)S(1)}, u32[]{:S(2)}, u32[]{:S(2)}) collective-permute-start(bf16[8,160,256]{2,1,0:T(8,128)(2,1)S(1)} %get-tuple-element.35), channel_id=1, source_target_pairs={{0,64},{64,128},{128,192},{192,256},{256,320},{320,384},{384,448},... | collective-permute-start | bytes 1966088 | tf_op jit(solution)/shard_map/ppermute | solution.py:20
  37.0 4.2 %collective-permute-start.3 = (bf16[8,160,256]{2,1,0:T(8,128)(2,1)S(1)}, bf16[8,160,256]{2,1,0:T(8,128)(2,1)S(1)}, u32[]{:S(2)}, u32[]{:S(2)}) collective-permute-start(bf16[8,160,256]{2,1,0:T(8,128)(2,1)S(1)} %get-tuple-element.36), channel_id=1, source_target_pairs={{0,448},{64,0},{128,64},{192,128},{256,192},{320,256},{384,320},{4... | collective-permute-start | bytes 1966088 | tf_op jit(solution)/shard_map/ppermute | solution.py:20
  41.1 11.1 %collective-permute-done.8.refs_4_ = bf16[8,160,256]{2,1,0:T(8,128)(2,1)S(1)} collective-permute-done((bf16[8,160,256]{2,1,0:T(8,128)(2,1)S(1)}, bf16[8,160,256]{2,1,0:T(8,128)(2,1)S(1)}, u32[]{:S(2)}, u32[]{:S(2)}) %collective-permute-start.8) | collective-permute-done | bytes 655392 | tf_op jit(solution)/shard_map/ppermute | solution.py:20
  52.3 1.9 collective-permute-start.9
  54.2 4.6 %collective-permute-start.4 = (bf16[8,160,256]{2,1,0:T(8,128)(2,1)S(1)}, bf16[8,160,256]{2,1,0:T(8,128)(2,1)S(1)}, u32[]{:S(2)}, u32[]{:S(2)}) collective-permute-start(bf16[8,160,256]{2,1,0:T(8,128)(2,1)S(1)} %collective-permute-done.3.refs_5_), channel_id=1, source_target_pairs={{0,448},{64,0},{128,64},{192,128},{256,192},{320,256},{384,320},{4... | collective-permute-start | bytes 1966088 | tf_op jit(solution)/shard_map/ppermute | solution.py:20
  58.8 10.3 %collective-permute-done.9.refs_6_ = bf16[8,160,256]{2,1,0:T(8,128)(2,1)S(1)} collective-permute-done((bf16[8,160,256]{2,1,0:T(8,128)(2,1)S(1)}, bf16[8,160,256]{2,1,0:T(8,128)(2,1)S(1)}, u32[]{:S(2)}, u32[]{:S(2)}) %collective-permute-start.9) | collective-permute-done | bytes 655392 | tf_op jit(solution)/shard_map/ppermute | solution.py:20
  69.1 1.9 collective-permute-start.10
  71.1 4.6 %collective-permute-start.5 = (bf16[6,160,256]{2,1,0:T(8,128)(2,1)S(1)}, bf16[6,160,256]{2,1,0:T(8,128)(2,1)S(1)}, u32[]{:S(2)}, u32[]{:S(2)}) collective-permute-start(bf16[6,160,256]{2,1,0:T(8,128)(2,1)S(1)} %slice.16), channel_id=1, source_target_pairs={{0,448},{64,0},{128,64},{192,128},{256,192},{320,256},{384,320},{4... | collective-permute-start | bytes 1474568 | tf_op jit(solution)/shard_map/ppermute | solution.py:20
  75.7 5.9 %collective-permute-done.10.refs_8_ = bf16[6,160,256]{2,1,0:T(8,128)(2,1)S(1)} collective-permute-done((bf16[6,160,256]{2,1,0:T(8,128)(2,1)S(1)}, bf16[6,160,256]{2,1,0:T(8,128)(2,1)S(1)}, u32[]{:S(2)}, u32[]{:S(2)}) %collective-permute-start.10) | collective-permute-done | bytes 491552 | tf_op jit(solution)/shard_map/ppermute | solution.py:20
  81.6 1.9 collective-permute-start.11
  83.6 4.6 %collective-permute-start.6 = (bf16[2,160,256]{2,1,0:T(8,128)(2,1)S(1)}, bf16[2,160,256]{2,1,0:T(8,128)(2,1)S(1)}, u32[]{:S(2)}, u32[]{:S(2)}) collective-permute-start(bf16[2,160,256]{2,1,0:T(8,128)(2,1)S(1)} %slice.17), channel_id=1, source_target_pairs={{0,448},{64,0},{128,64},{192,128},{256,192},{320,256},{384,320},{4... | collective-permute-start | bytes 491528 | tf_op jit(solution)/shard_map/ppermute | solution.py:20
  88.2 0.6 pad_add_fusion.place
  88.8 0.5 collective-permute-done.11.refs_10_
  89.3 1.1 collective-permute-done.6.refs_11_
  90.4 0.6 copy-done.18
  91.1 7.7 %all-gather.2.cloned.1.call-done.x_hbm = bf16[2560,768]{1,0:T(8,128)(2,1)} async-done(((bf16[160,768]{1,0:T(8,128)(2,1)}), bf16[2560,768]{1,0:T(8,128)(2,1)}) %all-gather.2.cloned.1.call-update) | async-done | bytes 3932176 | tf_op jit(solution)/shard_map/all_gather | solution.py:276
  98.8 9.2 %project.1 = (f32[384,1024]{1,0:T(8,128)}, f32[384,1024]{1,0:T(8,128)}, bf16[1280,768]{1,0:T(8,128)(2,1)}) custom-call(s32[2]{0:T(128)} %pad_add_fusion.place, bf16[2560,768]{1,0:T(8,128)(2,1)} %all-gather.2.cloned.1.call-done.x_hbm, bf16[4,160,256]{2,1,0:T(8,128)(2,1)} %copy-done.10, bf16[4,160,256]{2,1,0:T(8,128)(2,1)} %copy-done.7, ...), custom_call_target="tpu_custom_call" | custom-call | flops 4026531840 | bytes 9175040 | tf_op jit(solution)/shard_map/project/pallas_call | solution.py:94
  108.1 2.6 %collective-permute-start.12 = (f32[384,1024]{1,0:T(8,128)}, f32[384,1024]{1,0:T(8,128)S(1)}, u32[]{:S(2)}, u32[]{:S(2)}) collective-permute-start(f32[384,1024]{1,0:T(8,128)} %get-tuple-element.24), channel_id=1, source_target_pairs={{0,16},{16,0},{1,17},{17,1},{2,18},{18,2},{3,19},{19,3},{4,20},{20... | collective-permute-start | bytes 4718600 | tf_op jit(solution)/shard_map/ppermute | solution.py:20
  110.7 3.1 %collective-permute-start.13 = (bf16[1280,768]{1,0:T(8,128)(2,1)}, bf16[1280,768]{1,0:T(8,128)(2,1)S(1)}, u32[]{:S(2)}, u32[]{:S(2)}) collective-permute-start(bf16[1280,768]{1,0:T(8,128)(2,1)} %get-tuple-element.33), channel_id=1, source_target_pairs={{0,64},{64,0},{1,65},{65,1},{2,66},{66,2},{3,67},{67,3},{4,68},{68... | collective-permute-start | bytes 5898248 | tf_op jit(solution)/shard_map/ppermute | solution.py:20
  113.9 0.1 collective-permute-done.12.two
  113.9 1.4 copy-done.1
  115.3 0.4 merge.1
  115.7 17.5 %all_to_all.15.sums = f32[16,1,1152]{2,1,0:T(1,128)S(1)} all-to-all(f32[16,1,1152]{2,1,0:T(1,128)S(1)} %get-tuple-element.26), channel_id=1, replica_groups=mesh['yh'=4,'yl'=2,'zl'=2,'c'=2,'x'=4,'zh'=4] {'x','zh'}, dimensions={0} | all-to-all | bytes 147456 | tf_op jit(solution)/shard_map/all_to_all | solution.py:262
  133.3 2.4 %attend.1 = (f32[384,256]{1,0:T(8,128)S(1)}, f32[16,1,384]{2,1,0:T(1,128)S(1)}) custom-call(f32[16,1,1152]{2,1,0:T(1,128)S(1)} %all_to_all.15.sums, f32[384,768]{1,0:T(8,128)S(1)} %get-tuple-element.27.qkd.q, bf16[384,256]{1,0:T(8,128)(2,1)S(1)} %get-tuple-element.28.value, f32[2,256]{1,0:T(2,128)S(1)} %pad_maximum_fusion.4.gains), custom_call_target="tpu_custom_call" | custom-call | tf_op jit(solution)/shard_map/attend/pallas_call | solution.py:206
  135.7 0.8 copy-done.4
  136.4 12.1 %all_to_all.16.back = f32[16,1,384]{2,1,0:T(1,128)} all-to-all(f32[16,1,384]{2,1,0:T(1,128)S(1)} %get-tuple-element.30), channel_id=1, replica_groups=mesh['yh'=4,'yl'=2,'zl'=2,'c'=2,'x'=4,'zh'=4] {'x','zh'}, dimensions={0} | all-to-all | bytes 49152 | tf_op jit(solution)/shard_map/all_to_all | solution.py:262
  148.5 2.3 %grad.1.gq = bf16[384,256]{1,0:T(8,128)(2,1)} custom-call(f32[16,1,1152]{2,1,0:T(1,128)} %copy-done.3, f32[16,1,384]{2,1,0:T(1,128)} %all_to_all.16.back, f32[384,768]{1,0:T(8,128)} %copy-done, f32[384,256]{1,0:T(8,128)} %copy-done.4), custom_call_target="tpu_custom_call" | custom-call | tf_op jit(solution)/shard_map/grad/pallas_call | solution.py:225
  150.8 2.1 %collective-permute-start.15 = (bf16[384,256]{1,0:T(8,128)(2,1)}, bf16[384,256]{1,0:T(8,128)(2,1)S(1)}, u32[]{:S(2)}, u32[]{:S(2)}) collective-permute-start(bf16[384,256]{1,0:T(8,128)(2,1)} %grad.1.gq), channel_id=1, source_target_pairs={{0,64},{64,0},{1,65},{65,1},{2,66},{66,2},{3,67},{67,3},{4,68},{68... | collective-permute-start | bytes 589832 | tf_op jit(solution)/shard_map/ppermute | solution.py:20
  152.9 4.7 %collective-permute-start.14 = (bf16[384,256]{1,0:T(8,128)(2,1)}, bf16[384,256]{1,0:T(8,128)(2,1)S(1)}, u32[]{:S(2)}, u32[]{:S(2)}) collective-permute-start(bf16[384,256]{1,0:T(8,128)(2,1)} %grad.1.gq), channel_id=1, source_target_pairs={{0,16},{16,0},{1,17},{17,1},{2,18},{18,2},{3,19},{19,3},{4,20},{20... | collective-permute-start | bytes 589832 | tf_op jit(solution)/shard_map/ppermute | solution.py:20
  157.6 3.1 %collective-permute-done.15.gq_near = bf16[384,256]{1,0:T(8,128)(2,1)S(1)} collective-permute-done((bf16[384,256]{1,0:T(8,128)(2,1)}, bf16[384,256]{1,0:T(8,128)(2,1)S(1)}, u32[]{:S(2)}, u32[]{:S(2)}) %collective-permute-start.15) | collective-permute-done | bytes 196640 | tf_op jit(solution)/shard_map/ppermute | solution.py:20
  160.8 3.4 %collective-permute-start.16 = (bf16[384,256]{1,0:T(8,128)(2,1)S(1)}, bf16[384,256]{1,0:T(8,128)(2,1)S(1)}, u32[]{:S(2)}, u32[]{:S(2)}) collective-permute-start(bf16[384,256]{1,0:T(8,128)(2,1)S(1)} %collective-permute-done.15.gq_near), channel_id=1, source_target_pairs={{0,16},{16,0},{1,17},{17,1},{2,18},{18,2},{3,19},{19,3},{4,20},{20... | collective-permute-start | bytes 589832 | tf_op jit(solution)/shard_map/ppermute | solution.py:20
  164.2 1.7 dynamic-slice_bitcast_fusion.x
  165.9 1.5 outer.1
  167.4 25.1 %all_to_all.17 = bf16[8,160,256]{2,1,0:T(8,128)(2,1)S(1)} all-to-all(bf16[8,160,256]{2,1,0:T(8,128)(2,1)S(1)} %bitcast.21), channel_id=1, replica_groups=mesh['yh'=4,'yl'=2,'zl'=2,'c'=2,'x'=4,'zh'=4] {'zl','yh'}, dimensions={0} | all-to-all | bytes 1310720 | tf_op jit(solution)/shard_map/all_to_all | solution.py:262
  192.5 0.8 convert_reduce_fusion
  (47 shorter events, 0.2 us)
Async XLA Ops:
  6.5 92.3 %all-gather.2.cloned.1.call-start = ((), (), s32[]{:S(2)}) async-start(), calls=%async_computation.3 | async-start | bytes 4177920 | tf_op jit(solution)/shard_map/all_gather | solution.py:276
  7.5 9.7 %collective-permute-start = (bf16[160,384]{1,0:T(8,128)(2,1)S(1)}, bf16[160,384]{1,0:T(8,128)(2,1)S(1)}, u32[]{:S(2)}, u32[]{:S(2)}) collective-permute-start(bf16[160,384]{1,0:T(8,128)(2,1)S(1)} %get-tuple-element.38), channel_id=1, source_target_pairs={{0,16},{16,0},{1,17},{17,1},{2,18},{18,2},{3,19},{19,3},{4,20},{20... | collective-permute-start | bytes 368648 | tf_op jit(solution)/shard_map/ppermute | solution.py:20
  19.1 12.8 %copy-start.10 = (bf16[4,160,256]{2,1,0:T(8,128)(2,1)}, bf16[4,160,256]{2,1,0:T(8,128)(2,1)S(1)}, u32[]{:S(2)}) copy-start(bf16[4,160,256]{2,1,0:T(8,128)(2,1)S(1)} %pad_maximum_fusion.2.refs_0_) | copy-start | bytes 983044
  19.1 10.8 %collective-permute-start.1 = (bf16[4,160,256]{2,1,0:T(8,128)(2,1)S(1)}, bf16[4,160,256]{2,1,0:T(8,128)(2,1)S(1)}, u32[]{:S(2)}, u32[]{:S(2)}) collective-permute-start(bf16[4,160,256]{2,1,0:T(8,128)(2,1)S(1)} %pad_maximum_fusion.2.refs_0_), channel_id=1, source_target_pairs={{0,32},{32,0},{1,33},{33,1},{2,34},{34,2},{3,35},{35,3},{4,36},{36... | collective-permute-start | bytes 983048 | tf_op jit(solution)/shard_map/ppermute | solution.py:20
  21.0 10.8 %collective-permute-start.2 = (bf16[4,160,256]{2,1,0:T(8,128)(2,1)S(1)}, bf16[4,160,256]{2,1,0:T(8,128)(2,1)S(1)}, u32[]{:S(2)}, u32[]{:S(2)}) collective-permute-start(bf16[4,160,256]{2,1,0:T(8,128)(2,1)S(1)} %pad_maximum_fusion.2.refs_0_), channel_id=1, source_target_pairs={{0,448},{64,0},{128,64},{192,128},{256,192},{320,256},{384,320},{4... | collective-permute-start | bytes 983048 | tf_op jit(solution)/shard_map/ppermute | solution.py:20
  23.0 11.5 %collective-permute-start.7 = (bf16[4,160,256]{2,1,0:T(8,128)(2,1)S(1)}, bf16[4,160,256]{2,1,0:T(8,128)(2,1)S(1)}, u32[]{:S(2)}, u32[]{:S(2)}) collective-permute-start(bf16[4,160,256]{2,1,0:T(8,128)(2,1)S(1)} %pad_maximum_fusion.2.refs_0_), channel_id=1, source_target_pairs={{0,64},{64,128},{128,192},{192,256},{256,320},{320,384},{384,448},... | collective-permute-start | bytes 983048 | tf_op jit(solution)/shard_map/ppermute | solution.py:20
  29.9 41.2 %copy-start.7 = (bf16[4,160,256]{2,1,0:T(8,128)(2,1)}, bf16[4,160,256]{2,1,0:T(8,128)(2,1)S(1)}, u32[]{:S(2)}) copy-start(bf16[4,160,256]{2,1,0:T(8,128)(2,1)S(1)} %collective-permute-done.1.refs_1_) | copy-start | bytes 983044
  31.9 39.2 %copy-start.8 = (bf16[4,160,256]{2,1,0:T(8,128)(2,1)}, bf16[4,160,256]{2,1,0:T(8,128)(2,1)S(1)}, u32[]{:S(2)}) copy-start(bf16[4,160,256]{2,1,0:T(8,128)(2,1)S(1)} %collective-permute-done.2.refs_3_) | copy-start | bytes 983044
  34.5 36.6 %copy-start.9 = (bf16[4,160,256]{2,1,0:T(8,128)(2,1)}, bf16[4,160,256]{2,1,0:T(8,128)(2,1)S(1)}, u32[]{:S(2)}) copy-start(bf16[4,160,256]{2,1,0:T(8,128)(2,1)S(1)} %collective-permute-done.7.refs_2_) | copy-start | bytes 983044
  34.6 17.6 %collective-permute-start.8 = (bf16[8,160,256]{2,1,0:T(8,128)(2,1)S(1)}, bf16[8,160,256]{2,1,0:T(8,128)(2,1)S(1)}, u32[]{:S(2)}, u32[]{:S(2)}) collective-permute-start(bf16[8,160,256]{2,1,0:T(8,128)(2,1)S(1)} %get-tuple-element.35), channel_id=1, source_target_pairs={{0,64},{64,128},{128,192},{192,256},{256,320},{320,384},{384,448},... | collective-permute-start | bytes 1966088 | tf_op jit(solution)/shard_map/ppermute | solution.py:20
  37.0 17.2 %collective-permute-start.3 = (bf16[8,160,256]{2,1,0:T(8,128)(2,1)S(1)}, bf16[8,160,256]{2,1,0:T(8,128)(2,1)S(1)}, u32[]{:S(2)}, u32[]{:S(2)}) collective-permute-start(bf16[8,160,256]{2,1,0:T(8,128)(2,1)S(1)} %get-tuple-element.36), channel_id=1, source_target_pairs={{0,448},{64,0},{128,64},{192,128},{256,192},{320,256},{384,320},{4... | collective-permute-start | bytes 1966088 | tf_op jit(solution)/shard_map/ppermute | solution.py:20
  52.3 46.6 %copy-start.15 = (bf16[8,160,256]{2,1,0:T(8,128)(2,1)}, bf16[8,160,256]{2,1,0:T(8,128)(2,1)S(1)}, u32[]{:S(2)}) copy-start(bf16[8,160,256]{2,1,0:T(8,128)(2,1)S(1)} %collective-permute-done.8.refs_4_) | copy-start | bytes 1966084
  52.3 16.8 %collective-permute-start.9 = (bf16[8,160,256]{2,1,0:T(8,128)(2,1)S(1)}, bf16[8,160,256]{2,1,0:T(8,128)(2,1)S(1)}, u32[]{:S(2)}, u32[]{:S(2)}) collective-permute-start(bf16[8,160,256]{2,1,0:T(8,128)(2,1)S(1)} %collective-permute-done.8.refs_4_), channel_id=1, source_target_pairs={{0,64},{64,128},{128,192},{192,256},{256,320},{320,384},{384,448},... | collective-permute-start | bytes 1966088 | tf_op jit(solution)/shard_map/ppermute | solution.py:20
  54.2 29.4 %copy-start.16 = (bf16[8,160,256]{2,1,0:T(8,128)(2,1)}, bf16[8,160,256]{2,1,0:T(8,128)(2,1)S(1)}, u32[]{:S(2)}) copy-start(bf16[8,160,256]{2,1,0:T(8,128)(2,1)S(1)} %collective-permute-done.3.refs_5_) | copy-start | bytes 1966084
  54.2 16.8 %collective-permute-start.4 = (bf16[8,160,256]{2,1,0:T(8,128)(2,1)S(1)}, bf16[8,160,256]{2,1,0:T(8,128)(2,1)S(1)}, u32[]{:S(2)}, u32[]{:S(2)}) collective-permute-start(bf16[8,160,256]{2,1,0:T(8,128)(2,1)S(1)} %collective-permute-done.3.refs_5_), channel_id=1, source_target_pairs={{0,448},{64,0},{128,64},{192,128},{256,192},{320,256},{384,320},{4... | collective-permute-start | bytes 1966088 | tf_op jit(solution)/shard_map/ppermute | solution.py:20
  69.1 29.8 %copy-start.5 = (bf16[8,160,256]{2,1,0:T(8,128)(2,1)}, bf16[8,160,256]{2,1,0:T(8,128)(2,1)S(1)}, u32[]{:S(2)}) copy-start(bf16[8,160,256]{2,1,0:T(8,128)(2,1)S(1)} %collective-permute-done.9.refs_6_) | copy-start | bytes 1966084
  69.1 12.5 %collective-permute-start.10 = (bf16[6,160,256]{2,1,0:T(8,128)(2,1)S(1)}, bf16[6,160,256]{2,1,0:T(8,128)(2,1)S(1)}, u32[]{:S(2)}, u32[]{:S(2)}) collective-permute-start(bf16[6,160,256]{2,1,0:T(8,128)(2,1)S(1)} %slice.18), channel_id=1, source_target_pairs={{0,64},{64,128},{128,192},{192,256},{256,320},{320,384},{384,448},... | collective-permute-start | bytes 1474568 | tf_op jit(solution)/shard_map/ppermute | solution.py:20
  71.0 27.8 %copy-start.6 = (bf16[8,160,256]{2,1,0:T(8,128)(2,1)}, bf16[8,160,256]{2,1,0:T(8,128)(2,1)S(1)}, u32[]{:S(2)}) copy-start(bf16[8,160,256]{2,1,0:T(8,128)(2,1)S(1)} %collective-permute-done.4.refs_7_) | copy-start | bytes 1966084
  71.1 12.4 %collective-permute-start.5 = (bf16[6,160,256]{2,1,0:T(8,128)(2,1)S(1)}, bf16[6,160,256]{2,1,0:T(8,128)(2,1)S(1)}, u32[]{:S(2)}, u32[]{:S(2)}) collective-permute-start(bf16[6,160,256]{2,1,0:T(8,128)(2,1)S(1)} %slice.16), channel_id=1, source_target_pairs={{0,448},{64,0},{128,64},{192,128},{256,192},{320,256},{384,320},{4... | collective-permute-start | bytes 1474568 | tf_op jit(solution)/shard_map/ppermute | solution.py:20
  81.6 1.9 copy-start.11
  81.6 7.7 %collective-permute-start.11 = (bf16[2,160,256]{2,1,0:T(8,128)(2,1)S(1)}, bf16[2,160,256]{2,1,0:T(8,128)(2,1)S(1)}, u32[]{:S(2)}, u32[]{:S(2)}) collective-permute-start(bf16[2,160,256]{2,1,0:T(8,128)(2,1)S(1)} %slice.19), channel_id=1, source_target_pairs={{0,64},{64,128},{128,192},{192,256},{256,320},{320,384},{384,448},... | collective-permute-start | bytes 491528 | tf_op jit(solution)/shard_map/ppermute | solution.py:20
  83.6 6.9 %copy-start.12 = (bf16[6,160,256]{2,1,0:T(8,128)(2,1)}, bf16[6,160,256]{2,1,0:T(8,128)(2,1)S(1)}, u32[]{:S(2)}) copy-start(bf16[6,160,256]{2,1,0:T(8,128)(2,1)S(1)} %collective-permute-done.5.refs_9_) | copy-start | bytes 1474564
  83.6 6.8 %collective-permute-start.6 = (bf16[2,160,256]{2,1,0:T(8,128)(2,1)S(1)}, bf16[2,160,256]{2,1,0:T(8,128)(2,1)S(1)}, u32[]{:S(2)}, u32[]{:S(2)}) collective-permute-start(bf16[2,160,256]{2,1,0:T(8,128)(2,1)S(1)} %slice.17), channel_id=1, source_target_pairs={{0,448},{64,0},{128,64},{192,128},{256,192},{320,256},{384,320},{4... | collective-permute-start | bytes 491528 | tf_op jit(solution)/shard_map/ppermute | solution.py:20
  88.8 25.0 %copy-start.13 = (f32[256]{0:T(256)S(1)}, f32[256]{0:T(256)}, u32[]{:S(2)}) copy-start(f32[256]{0:T(256)} %param.13) | copy-start | bytes 3076
  88.8 25.0 %copy-start.14 = (f32[256]{0:T(256)S(1)}, f32[256]{0:T(256)}, u32[]{:S(2)}) copy-start(f32[256]{0:T(256)} %param.12) | copy-start | bytes 3076
  89.3 1.1 copy-start.17
  90.4 0.7 copy-start.18
  108.1 5.9 %collective-permute-start.12 = (f32[384,1024]{1,0:T(8,128)}, f32[384,1024]{1,0:T(8,128)S(1)}, u32[]{:S(2)}, u32[]{:S(2)}) collective-permute-start(f32[384,1024]{1,0:T(8,128)} %get-tuple-element.24), channel_id=1, source_target_pairs={{0,16},{16,0},{1,17},{17,1},{2,18},{18,2},{3,19},{19,3},{4,20},{20... | collective-permute-start | bytes 4718600 | tf_op jit(solution)/shard_map/ppermute | solution.py:20
  110.7 55.2 %collective-permute-start.13 = (bf16[1280,768]{1,0:T(8,128)(2,1)}, bf16[1280,768]{1,0:T(8,128)(2,1)S(1)}, u32[]{:S(2)}, u32[]{:S(2)}) collective-permute-start(bf16[1280,768]{1,0:T(8,128)(2,1)} %get-tuple-element.33), channel_id=1, source_target_pairs={{0,64},{64,0},{1,65},{65,1},{2,66},{66,2},{3,67},{67,3},{4,68},{68... | collective-permute-start | bytes 5898248 | tf_op jit(solution)/shard_map/ppermute | solution.py:20
  113.9 1.4 copy-start.1
  115.7 32.7 %copy-start = (f32[384,768]{1,0:T(8,128)}, f32[384,768]{1,0:T(8,128)S(1)}, u32[]{:S(2)}) copy-start(f32[384,768]{1,0:T(8,128)S(1)} %get-tuple-element.27.qkd.q) | copy-start | bytes 3538948
  133.3 15.2 %copy-start.3 = (f32[16,1,1152]{2,1,0:T(1,128)}, f32[16,1,1152]{2,1,0:T(1,128)S(1)}, u32[]{:S(2)}) copy-start(f32[16,1,1152]{2,1,0:T(1,128)S(1)} %all_to_all.15.sums) | copy-start | bytes 221188
  135.7 0.8 copy-start.4
  150.8 10.0 %collective-permute-start.15 = (bf16[384,256]{1,0:T(8,128)(2,1)}, bf16[384,256]{1,0:T(8,128)(2,1)S(1)}, u32[]{:S(2)}, u32[]{:S(2)}) collective-permute-start(bf16[384,256]{1,0:T(8,128)(2,1)} %grad.1.gq), channel_id=1, source_target_pairs={{0,64},{64,0},{1,65},{65,1},{2,66},{66,2},{3,67},{67,3},{4,68},{68... | collective-permute-start | bytes 589832 | tf_op jit(solution)/shard_map/ppermute | solution.py:20
  152.9 12.9 %collective-permute-start.14 = (bf16[384,256]{1,0:T(8,128)(2,1)}, bf16[384,256]{1,0:T(8,128)(2,1)S(1)}, u32[]{:S(2)}, u32[]{:S(2)}) collective-permute-start(bf16[384,256]{1,0:T(8,128)(2,1)} %grad.1.gq), channel_id=1, source_target_pairs={{0,16},{16,0},{1,17},{17,1},{2,18},{18,2},{3,19},{19,3},{4,20},{20... | collective-permute-start | bytes 589832 | tf_op jit(solution)/shard_map/ppermute | solution.py:20
  157.6 8.2 %copy-start.2 = (bf16[384,256]{1,0:T(8,128)(2,1)S(1)}, bf16[384,256]{1,0:T(8,128)(2,1)}, u32[]{:S(2)}) copy-start(bf16[384,256]{1,0:T(8,128)(2,1)} %grad.1.gq) | copy-start | bytes 589828
  160.8 5.1 %collective-permute-start.16 = (bf16[384,256]{1,0:T(8,128)(2,1)S(1)}, bf16[384,256]{1,0:T(8,128)(2,1)S(1)}, u32[]{:S(2)}, u32[]{:S(2)}) collective-permute-start(bf16[384,256]{1,0:T(8,128)(2,1)S(1)} %collective-permute-done.15.gq_near), channel_id=1, source_target_pairs={{0,16},{16,0},{1,17},{17,1},{2,18},{18,2},{3,19},{19,3},{4,20},{20... | collective-permute-start | bytes 589832 | tf_op jit(solution)/shard_map/ppermute | solution.py:20
Sparse Core Ops, SparseCore 0:
  18.2 80.6 all-gather.1

commit v6 on v5

--- a/solution.py
+++ b/solution.py
@@ -38,7 +38,7 @@
 def project_kernel(place, x_hbm, *refs, layout, wide, rows):
     count = max(entry[0] for entry in layout) + 1
     pieces = refs[:count]
-    own, theirs, near, x, w, sem, out_sem = refs[count:]
+    own, theirs, up, down, x, w, sem, out_sem = refs[count:]
     length = own.shape[0]
     y, zl = place[0], place[1]
     groups = sem.shape[0]
@@ -69,9 +69,9 @@
         pltpu.make_async_copy(x.at[at, :], x.at[at, :], sem.at[g, 0]).wait()
         for (back, step), spot in spots.items():
             if back % 2 and spot * rows // span == g:
-                far_y, far_zl = source(back, step)
+                far_y, _ = source(back, step)
                 pltpu.make_async_copy(
-                    x.at[pl.ds(spot * rows, rows), :], near.at[block(far_zl * 4 + lax.div(far_y, 2)), :], out_sem
+                    x.at[pl.ds(spot * rows, rows), :], (up, down)[step].at[block(lax.div(far_y, 2)), :], out_sem.at[step]
                 ).start()
         pltpu.make_async_copy(w.at[:, at, :], w.at[:, at, :], sem.at[g, 1]).wait()
         for i in range(4):
@@ -79,7 +79,8 @@
             cols = slice(i * wide, (i + 1) * wide)
             own[:, cols] = part[:length] if g == 0 else own[:, cols] + part[:length]
             theirs[:, cols] = part[length:] if g == 0 else theirs[:, cols] + part[length:]
-    pltpu.make_async_copy(near, near, out_sem).wait()
+    pltpu.make_async_copy(up, up, out_sem.at[0]).wait()
+    pltpu.make_async_copy(down, down, out_sem.at[1]).wait()
 
 
 def project(place, x, parts, wide):
@@ -99,17 +100,19 @@
             pl.BlockSpec(memory_space=pltpu.VMEM),
             pl.BlockSpec(memory_space=pltpu.VMEM),
             pl.BlockSpec(memory_space=pl.ANY),
+            pl.BlockSpec(memory_space=pl.ANY),
         ],
         out_shape=[
             jax.ShapeDtypeStruct((length, 4 * wide), F32),
             jax.ShapeDtypeStruct((length, 4 * wide), F32),
-            jax.ShapeDtypeStruct((depth // 2, 2 * length), BF),
+            jax.ShapeDtypeStruct((depth // 4, 2 * length), BF),
+            jax.ShapeDtypeStruct((depth // 4, 2 * length), BF),
         ],
         scratch_shapes=[
             pltpu.VMEM(x.shape, BF),
             pltpu.VMEM((4, depth, wide), BF),
             pltpu.SemaphoreType.DMA((2, 2)),
-            pltpu.SemaphoreType.DMA,
+            pltpu.SemaphoreType.DMA((2,)),
         ],
         compiler_params=pltpu.CompilerParams(vmem_limit_bytes=62 * MIB),
         cost_estimate=pl.CostEstimate(
@@ -237,25 +240,29 @@
     )(sums, back, qkd, weighted)
 
 
-def outer_kernel(x, near, gq, gq_core, gq_near, gq_near_core, term):
-    length = gq.shape[0]
-    total = jnp.dot(x[:, :length], gq[...], preferred_element_type=F32)
-    total += jnp.dot(x[:, length:], gq_core[...], preferred_element_type=F32)
-    total += jnp.dot(near[:, :length], gq_near[...], preferred_element_type=F32)
-    total += jnp.dot(near[:, length:], gq_near_core[...], preferred_element_type=F32)
-    term[...] = total.astype(BF)
-
-
-def outer(x, near, grads):
-    rows, tokens = near.shape
-    wide = grads[0].shape[1]
+def outer_kernel(place, x, up, down, gq, gq_core, gq_up, gq_down, gq_cores, term):
+    length, half = gq.shape[0], up.shape[0]
+    for step, (near, gq_near) in enumerate(((up, gq_up), (down, gq_down))):
+        at = pl.ds(pl.multiple_of(lax.rem(place[1] + step, 2) * half, half), half)
+        total = jnp.dot(x[at, :length], gq[...], preferred_element_type=F32)
+        total += jnp.dot(x[at, length:], gq_core[...], preferred_element_type=F32)
+        total += jnp.dot(near[:, :length], gq_near[...], preferred_element_type=F32)
+        cores = gq_cores[step * length : (step + 1) * length, :]
+        total += jnp.dot(near[:, length:], cores, preferred_element_type=F32)
+        term[at, :] = total.astype(BF)
+
+
+def outer(place, x, *rest):
+    rows, tokens = x.shape
+    wide = rest[2].shape[1]
     return pl.pallas_call(
         outer_kernel,
+        in_specs=[pl.BlockSpec(memory_space=pltpu.SMEM)] + [pl.BlockSpec(memory_space=pltpu.VMEM)] * (1 + len(rest)),
         out_shape=jax.ShapeDtypeStruct((rows, wide), BF),
         compiler_params=pltpu.CompilerParams(vmem_limit_bytes=16 * MIB),
         cost_estimate=pl.CostEstimate(flops=4 * rows * tokens * wide, bytes_accessed=4 * rows * tokens, transcendentals=0),
         name="outer",
-    )(x, near, *grads)
+    )(place, x, *rest)
 
 
 def to_all(value, axes):
@@ -280,20 +287,21 @@
     x, *last = tie((x, parts[-1][0], parts[-2][0]))
     parts[-1], parts[-2] = (last[0], *parts[-1][1:]), (last[1], *parts[-2][1:])
 
-    own, theirs, near = project(place, x, parts, wide)
+    own, theirs, up, down = project(place, x, parts, wide)
     theirs = shift(theirs, "c", 1, 2)
-    near = shift(near, "yl", 1, 2)
+    up, down = shift(up, Y, 1, 8), shift(down, Y, -1, 8)
     qkd, value, stats = merge(own, theirs, wide)
     gains, stats = tie((jnp.stack([gain_query, gain_key]), stats))
     sums = to_all(stats, ("x", "zh"))
     weighted, stats = attend(sums, qkd, value, gains, wide, total)
     gq = grad(sums, to_all(stats, ("x", "zh")), qkd, weighted, total)
 
-    gq_near = shift(gq, "yl", 1, 2)
+    gq_up, gq_down = shift(gq, Y, 1, 8), shift(gq, Y, -1, 8)
     gq_core = shift(gq, "c", 1, 2)
     halves, gq = tie((x.reshape(2, -1, x.shape[1]), gq))
     mine = lax.dynamic_index_in_dim(halves, lax.axis_index("yl"), 0, keepdims=False)
-    term = outer(mine, near, (gq, gq_core, gq_near, shift(gq_near, "c", 1, 2)))
+    gq_cores = shift(jnp.concatenate([gq_up, gq_down], axis=0), "c", 1, 2)
+    term = outer(place, mine, up, down, gq, gq_core, gq_up, gq_down, gq_cores)
     got = to_all(term.reshape(8, -1, wide), ("zl", "yh"))
     return jnp.sum(got.astype(F32), axis=0)
 

time: 202 us -> 208 us (1.030)
  the two profiles are of different devices: /device:TPU:1 before, /device:TPU:8 now
where the time goes in v6:
time: 208 us; the launch traced here: 207 us
  starting transfers between devices  58.8 us (28%)
  blocking collectives  56.1 us (27%)
  waiting for transfers between devices  52.8 us (25%)
  Pallas kernels  16.3 us (8%)
  between operations  13.8 us (7%)
  local copies, waits for them, and re-layouts  5.7 us (3%)
  other arithmetic  3.25 us (2%)
    ppermute x19, starting transfers between devices, shift(): lax.ppermute(value, axis, [(i, (i + by) % size) for i in range(size)])  58.8 us
    all_to_all x3, blocking collectives, to_all(): return lax.all_to_all(value, axes, 0, 0, tiled=True)  56.1 us
    ppermute x19, waiting for transfers between devices, shift(): lax.ppermute(value, axis, [(i, (i + by) % size) for i in range(size)])  47 us
    pallas_call x1, Pallas kernels, project(): pl.pallas_call(functools.partial(project_kernel, layout=tuple(layout), wi...  9.24 us
    all_gather x1, waiting for transfers between devices, on_device(): x = lax.all_gather(x, ('zh', 'x'), axis=0, tiled=True)  5.72 us
  transfers between devices with their start and end apart: 20, of which 12 were waited for; matrix products, arithmetic and copies ran while one was open for 2% of the time, Pallas kernels for 2%

profile of v6, /device:TPU:8, one launch (start us, length us, event | category | flops | bytes accessed | tf_op | source)
XLA Modules:
  0.0 206.8 jit_solution(626150836743113754)
XLA Ops:
  6.5 1.0 dynamic-slice_bitcast_fusion.2
  7.5 1.9 collective-permute-start
  9.5 1.3 collective-permute-done
  10.8 0.7 pad_maximum_fusion.4
  11.5 1.1 pad_maximum_fusion.3.refs_0_
  12.6 4.3 %collective-permute-start.1 = (bf16[4,160,256]{2,1,0:T(8,128)(2,1)S(1)}, bf16[4,160,256]{2,1,0:T(8,128)(2,1)S(1)}, u32[]{:S(2)}, u32[]{:S(2)}) collective-permute-start(bf16[4,160,256]{2,1,0:T(8,128)(2,1)S(1)} %pad_maximum_fusion.3.refs_0_), channel_id=1, source_target_pairs={{0,32},{32,0},{1,33},{33,1},{2,34},{34,2},{3,35},{35,3},{4,36},{36... | collective-permute-start | bytes 983048 | tf_op jit(solution)/shard_map/ppermute | solution.py:20
  16.9 5.4 %collective-permute-start.2 = (bf16[4,160,256]{2,1,0:T(8,128)(2,1)S(1)}, bf16[4,160,256]{2,1,0:T(8,128)(2,1)S(1)}, u32[]{:S(2)}, u32[]{:S(2)}) collective-permute-start(bf16[4,160,256]{2,1,0:T(8,128)(2,1)S(1)} %pad_maximum_fusion.3.refs_0_), channel_id=1, source_target_pairs={{0,448},{64,0},{128,64},{192,128},{256,192},{320,256},{384,320},{4... | collective-permute-start | bytes 983048 | tf_op jit(solution)/shard_map/ppermute | solution.py:20
  22.2 1.9 collective-permute-start.7
  24.2 0.7 collective-permute-done.1.refs_1_
  24.9 4.6 %collective-permute-done.2.refs_3_ = bf16[4,160,256]{2,1,0:T(8,128)(2,1)S(1)} collective-permute-done((bf16[4,160,256]{2,1,0:T(8,128)(2,1)S(1)}, bf16[4,160,256]{2,1,0:T(8,128)(2,1)S(1)}, u32[]{:S(2)}, u32[]{:S(2)}) %collective-permute-start.2) | collective-permute-done | bytes 327712 | tf_op jit(solution)/shard_map/ppermute | solution.py:20
  29.5 4.1 %collective-permute-done.7.refs_2_ = bf16[4,160,256]{2,1,0:T(8,128)(2,1)S(1)} collective-permute-done((bf16[4,160,256]{2,1,0:T(8,128)(2,1)S(1)}, bf16[4,160,256]{2,1,0:T(8,128)(2,1)S(1)}, u32[]{:S(2)}, u32[]{:S(2)}) %collective-permute-start.7) | collective-permute-done | bytes 327712 | tf_op jit(solution)/shard_map/ppermute | solution.py:20
  33.7 2.2 %collective-permute-start.8 = (bf16[8,160,256]{2,1,0:T(8,128)(2,1)S(1)}, bf16[8,160,256]{2,1,0:T(8,128)(2,1)S(1)}, u32[]{:S(2)}, u32[]{:S(2)}) collective-permute-start(bf16[8,160,256]{2,1,0:T(8,128)(2,1)S(1)} %get-tuple-element.37), channel_id=1, source_target_pairs={{0,64},{64,128},{128,192},{192,256},{256,320},{320,384},{384,448},... | collective-permute-start | bytes 1966088 | tf_op jit(solution)/shard_map/ppermute | solution.py:20
  35.9 3.6 %collective-permute-start.3 = (bf16[8,160,256]{2,1,0:T(8,128)(2,1)S(1)}, bf16[8,160,256]{2,1,0:T(8,128)(2,1)S(1)}, u32[]{:S(2)}, u32[]{:S(2)}) collective-permute-start(bf16[8,160,256]{2,1,0:T(8,128)(2,1)S(1)} %get-tuple-element.38), channel_id=1, source_target_pairs={{0,448},{64,0},{128,64},{192,128},{256,192},{320,256},{384,320},{4... | collective-permute-start | bytes 1966088 | tf_op jit(solution)/shard_map/ppermute | solution.py:20
  39.6 11.7 %collective-permute-done.8.refs_4_ = bf16[8,160,256]{2,1,0:T(8,128)(2,1)S(1)} collective-permute-done((bf16[8,160,256]{2,1,0:T(8,128)(2,1)S(1)}, bf16[8,160,256]{2,1,0:T(8,128)(2,1)S(1)}, u32[]{:S(2)}, u32[]{:S(2)}) %collective-permute-start.8) | collective-permute-done | bytes 655392 | tf_op jit(solution)/shard_map/ppermute | solution.py:20
  51.3 2.5 %collective-permute-start.9 = (bf16[8,160,256]{2,1,0:T(8,128)(2,1)S(1)}, bf16[8,160,256]{2,1,0:T(8,128)(2,1)S(1)}, u32[]{:S(2)}, u32[]{:S(2)}) collective-permute-start(bf16[8,160,256]{2,1,0:T(8,128)(2,1)S(1)} %collective-permute-done.8.refs_4_), channel_id=1, source_target_pairs={{0,64},{64,128},{128,192},{192,256},{256,320},{320,384},{384,448},... | collective-permute-start | bytes 1966088 | tf_op jit(solution)/shard_map/ppermute | solution.py:20
  53.8 3.8 %collective-permute-start.4 = (bf16[8,160,256]{2,1,0:T(8,128)(2,1)S(1)}, bf16[8,160,256]{2,1,0:T(8,128)(2,1)S(1)}, u32[]{:S(2)}, u32[]{:S(2)}) collective-permute-start(bf16[8,160,256]{2,1,0:T(8,128)(2,1)S(1)} %collective-permute-done.3.refs_5_), channel_id=1, source_target_pairs={{0,448},{64,0},{128,64},{192,128},{256,192},{320,256},{384,320},{4... | collective-permute-start | bytes 1966088 | tf_op jit(solution)/shard_map/ppermute | solution.py:20
  57.7 10.8 %collective-permute-done.9.refs_6_ = bf16[8,160,256]{2,1,0:T(8,128)(2,1)S(1)} collective-permute-done((bf16[8,160,256]{2,1,0:T(8,128)(2,1)S(1)}, bf16[8,160,256]{2,1,0:T(8,128)(2,1)S(1)}, u32[]{:S(2)}, u32[]{:S(2)}) %collective-permute-start.9) | collective-permute-done | bytes 655392 | tf_op jit(solution)/shard_map/ppermute | solution.py:20
  68.6 2.3 %collective-permute-start.10 = (bf16[6,160,256]{2,1,0:T(8,128)(2,1)S(1)}, bf16[6,160,256]{2,1,0:T(8,128)(2,1)S(1)}, u32[]{:S(2)}, u32[]{:S(2)}) collective-permute-start(bf16[6,160,256]{2,1,0:T(8,128)(2,1)S(1)} %slice.18), channel_id=1, source_target_pairs={{0,64},{64,128},{128,192},{192,256},{256,320},{320,384},{384,448},... | collective-permute-start | bytes 1474568 | tf_op jit(solution)/shard_map/ppermute | solution.py:20
  71.0 4.4 %collective-permute-start.5 = (bf16[6,160,256]{2,1,0:T(8,128)(2,1)S(1)}, bf16[6,160,256]{2,1,0:T(8,128)(2,1)S(1)}, u32[]{:S(2)}, u32[]{:S(2)}) collective-permute-start(bf16[6,160,256]{2,1,0:T(8,128)(2,1)S(1)} %slice.16), channel_id=1, source_target_pairs={{0,448},{64,0},{128,64},{192,128},{256,192},{320,256},{384,320},{4... | collective-permute-start | bytes 1474568 | tf_op jit(solution)/shard_map/ppermute | solution.py:20
  75.4 6.4 %collective-permute-done.10.refs_8_ = bf16[6,160,256]{2,1,0:T(8,128)(2,1)S(1)} collective-permute-done((bf16[6,160,256]{2,1,0:T(8,128)(2,1)S(1)}, bf16[6,160,256]{2,1,0:T(8,128)(2,1)S(1)}, u32[]{:S(2)}, u32[]{:S(2)}) %collective-permute-start.10) | collective-permute-done | bytes 491552 | tf_op jit(solution)/shard_map/ppermute | solution.py:20
  81.9 1.9 collective-permute-start.11
  83.9 4.9 %collective-permute-start.6 = (bf16[2,160,256]{2,1,0:T(8,128)(2,1)S(1)}, bf16[2,160,256]{2,1,0:T(8,128)(2,1)S(1)}, u32[]{:S(2)}, u32[]{:S(2)}) collective-permute-start(bf16[2,160,256]{2,1,0:T(8,128)(2,1)S(1)} %slice.17), channel_id=1, source_target_pairs={{0,448},{64,0},{128,64},{192,128},{256,192},{320,256},{384,320},{4... | collective-permute-start | bytes 491528 | tf_op jit(solution)/shard_map/ppermute | solution.py:20
  88.7 0.6 pad_add_fusion.place
  89.3 0.7 collective-permute-done.11.refs_10_
  90.0 1.5 collective-permute-done.6.refs_11_
  91.5 0.7 copy-done.19
  92.2 5.7 %all-gather.2.cloned.1.call-done.x_hbm = bf16[2560,768]{1,0:T(8,128)(2,1)} async-done(((bf16[160,768]{1,0:T(8,128)(2,1)}), bf16[2560,768]{1,0:T(8,128)(2,1)}) %all-gather.2.cloned.1.call-update) | async-done | bytes 3932176 | tf_op jit(solution)/shard_map/all_gather | solution.py:283
  97.9 9.2 %project.1 = (f32[384,1024]{1,0:T(8,128)}, f32[384,1024]{1,0:T(8,128)}, bf16[640,768]{1,0:T(8,128)(2,1)}, bf16[640,768]{1,0:T(8,128)(2,1)}) custom-call(s32[2]{0:T(128)} %pad_add_fusion.place, bf16[2560,768]{1,0:T(8,128)(2,1)} %all-gather.2.cloned.1.call-done.x_hbm, bf16[4,160,256]{2,1,0:T(8,128)(2,1)} %copy-done.11, bf16[4,160,256]{2,1,0:T(8,128)(2,1)} %copy-done.8, ...), custom_call_target="tpu_custom_call" | custom-call | flops 4026531840 | bytes 9175040 | tf_op jit(solution)/shard_map/project/pallas_call | solution.py:95
  107.2 1.9 collective-permute-start.12
  109.1 3.4 %collective-permute-start.13 = (bf16[640,768]{1,0:T(8,128)(2,1)}, bf16[640,768]{1,0:T(8,128)(2,1)S(1)}, u32[]{:S(2)}, u32[]{:S(2)}) collective-permute-start(bf16[640,768]{1,0:T(8,128)(2,1)} %get-tuple-element.34), channel_id=1, source_target_pairs={{0,64},{64,128},{128,192},{192,256},{256,320},{320,384},{384,448},... | collective-permute-start | bytes 2949128 | tf_op jit(solution)/shard_map/ppermute | solution.py:20
  112.5 2.4 %collective-permute-start.14 = (bf16[640,768]{1,0:T(8,128)(2,1)}, bf16[640,768]{1,0:T(8,128)(2,1)S(1)}, u32[]{:S(2)}, u32[]{:S(2)}) collective-permute-start(bf16[640,768]{1,0:T(8,128)(2,1)} %get-tuple-element.35), channel_id=1, source_target_pairs={{0,448},{64,0},{128,64},{192,128},{256,192},{320,256},{384,320},{4... | collective-permute-start | bytes 2949128 | tf_op jit(solution)/shard_map/ppermute | solution.py:20
  115.0 1.4 copy-done.1
  116.4 0.4 merge.1
  116.8 17.3 %all_to_all.15.sums = f32[16,1,1152]{2,1,0:T(1,128)S(1)} all-to-all(f32[16,1,1152]{2,1,0:T(1,128)S(1)} %get-tuple-element.27), channel_id=1, replica_groups=mesh['yh'=4,'yl'=2,'zl'=2,'c'=2,'x'=4,'zh'=4] {'x','zh'}, dimensions={0} | all-to-all | bytes 147456 | tf_op jit(solution)/shard_map/all_to_all | solution.py:269
  134.1 2.4 %attend.1 = (f32[384,256]{1,0:T(8,128)S(1)}, f32[16,1,384]{2,1,0:T(1,128)S(1)}) custom-call(f32[16,1,1152]{2,1,0:T(1,128)S(1)} %all_to_all.15.sums, f32[384,768]{1,0:T(8,128)S(1)} %get-tuple-element.28.qkd.q, bf16[384,256]{1,0:T(8,128)(2,1)S(1)} %get-tuple-element.29.value, f32[2,256]{1,0:T(2,128)S(1)} %pad_maximum_fusion.5.gains), custom_call_target="tpu_custom_call" | custom-call | tf_op jit(solution)/shard_map/attend/pallas_call | solution.py:209
  136.5 0.8 copy-done.4
  137.3 13.2 %all_to_all.16.back = f32[16,1,384]{2,1,0:T(1,128)} all-to-all(f32[16,1,384]{2,1,0:T(1,128)S(1)} %get-tuple-element.31), channel_id=1, replica_groups=mesh['yh'=4,'yl'=2,'zl'=2,'c'=2,'x'=4,'zh'=4] {'x','zh'}, dimensions={0} | all-to-all | bytes 49152 | tf_op jit(solution)/shard_map/all_to_all | solution.py:269
  150.5 2.3 %grad.1.gq = bf16[384,256]{1,0:T(8,128)(2,1)} custom-call(f32[16,1,1152]{2,1,0:T(1,128)} %copy-done.3, f32[16,1,384]{2,1,0:T(1,128)} %all_to_all.16.back, f32[384,768]{1,0:T(8,128)} %copy-done, f32[384,256]{1,0:T(8,128)} %copy-done.4), custom_call_target="tpu_custom_call" | custom-call | tf_op jit(solution)/shard_map/grad/pallas_call | solution.py:228
  152.8 4.8 %collective-permute-start.16 = (bf16[384,256]{1,0:T(8,128)(2,1)}, bf16[384,256]{1,0:T(8,128)(2,1)S(1)}, u32[]{:S(2)}, u32[]{:S(2)}) collective-permute-start(bf16[384,256]{1,0:T(8,128)(2,1)} %grad.1.gq), channel_id=1, source_target_pairs={{0,64},{64,128},{128,192},{192,256},{256,320},{320,384},{384,448},... | collective-permute-start | bytes 589832 | tf_op jit(solution)/shard_map/ppermute | solution.py:20
  157.6 2.7 %collective-permute-start.17 = (bf16[384,256]{1,0:T(8,128)(2,1)}, bf16[384,256]{1,0:T(8,128)(2,1)S(1)}, u32[]{:S(2)}, u32[]{:S(2)}) collective-permute-start(bf16[384,256]{1,0:T(8,128)(2,1)} %grad.1.gq), channel_id=1, source_target_pairs={{0,448},{64,0},{128,64},{192,128},{256,192},{320,256},{384,320},{4... | collective-permute-start | bytes 589832 | tf_op jit(solution)/shard_map/ppermute | solution.py:20
  160.3 1.9 collective-permute-done.16.gq_up
  162.2 3.2 %collective-permute-done.17.gq_down = bf16[384,256]{1,0:T(8,128)(2,1)S(1)} collective-permute-done((bf16[384,256]{1,0:T(8,128)(2,1)}, bf16[384,256]{1,0:T(8,128)(2,1)S(1)}, u32[]{:S(2)}, u32[]{:S(2)}) %collective-permute-start.17) | collective-permute-done | bytes 196640 | tf_op jit(solution)/shard_map/ppermute | solution.py:20
  165.4 1.9 collective-permute-start.18
  167.4 2.4 %collective-permute-start.15 = (bf16[384,256]{1,0:T(8,128)(2,1)}, bf16[384,256]{1,0:T(8,128)(2,1)S(1)}, u32[]{:S(2)}, u32[]{:S(2)}) collective-permute-start(bf16[384,256]{1,0:T(8,128)(2,1)} %grad.1.gq), channel_id=1, source_target_pairs={{0,16},{16,0},{1,17},{17,1},{2,18},{18,2},{3,19},{19,3},{4,20},{20... | collective-permute-start | bytes 589832 | tf_op jit(solution)/shard_map/ppermute | solution.py:20
  169.8 1.7 dynamic-slice_bitcast_fusion.x
  171.6 2.1 outer.1
  173.6 25.6 %all_to_all.17 = bf16[8,160,256]{2,1,0:T(8,128)(2,1)S(1)} all-to-all(bf16[8,160,256]{2,1,0:T(8,128)(2,1)S(1)} %bitcast.21), channel_id=1, replica_groups=mesh['yh'=4,'yl'=2,'zl'=2,'c'=2,'x'=4,'zh'=4] {'zl','yh'}, dimensions={0} | all-to-all | bytes 1310720 | tf_op jit(solution)/shard_map/all_to_all | solution.py:269
  199.3 0.8 convert_reduce_fusion
  (54 shorter events, 0.4 us)
Async XLA Ops:
  6.5 91.4 %all-gather.2.cloned.1.call-start = ((), (), s32[]{:S(2)}) async-start(), calls=%async_computation.3 | async-start | bytes 4177920 | tf_op jit(solution)/shard_map/all_gather | solution.py:283
  7.5 3.2 %collective-permute-start = (bf16[160,384]{1,0:T(8,128)(2,1)S(1)}, bf16[160,384]{1,0:T(8,128)(2,1)S(1)}, u32[]{:S(2)}, u32[]{:S(2)}) collective-permute-start(bf16[160,384]{1,0:T(8,128)(2,1)S(1)} %get-tuple-element.40), channel_id=1, source_target_pairs={{0,16},{16,0},{1,17},{17,1},{2,18},{18,2},{3,19},{19,3},{4,20},{20... | collective-permute-start | bytes 368648 | tf_op jit(solution)/shard_map/ppermute | solution.py:20
  12.6 16.9 %copy-start.11 = (bf16[4,160,256]{2,1,0:T(8,128)(2,1)}, bf16[4,160,256]{2,1,0:T(8,128)(2,1)S(1)}, u32[]{:S(2)}) copy-start(bf16[4,160,256]{2,1,0:T(8,128)(2,1)S(1)} %pad_maximum_fusion.3.refs_0_) | copy-start | bytes 983044
  12.6 12.3 %collective-permute-start.1 = (bf16[4,160,256]{2,1,0:T(8,128)(2,1)S(1)}, bf16[4,160,256]{2,1,0:T(8,128)(2,1)S(1)}, u32[]{:S(2)}, u32[]{:S(2)}) collective-permute-start(bf16[4,160,256]{2,1,0:T(8,128)(2,1)S(1)} %pad_maximum_fusion.3.refs_0_), channel_id=1, source_target_pairs={{0,32},{32,0},{1,33},{33,1},{2,34},{34,2},{3,35},{35,3},{4,36},{36... | collective-permute-start | bytes 983048 | tf_op jit(solution)/shard_map/ppermute | solution.py:20
  16.9 12.6 %collective-permute-start.2 = (bf16[4,160,256]{2,1,0:T(8,128)(2,1)S(1)}, bf16[4,160,256]{2,1,0:T(8,128)(2,1)S(1)}, u32[]{:S(2)}, u32[]{:S(2)}) collective-permute-start(bf16[4,160,256]{2,1,0:T(8,128)(2,1)S(1)} %pad_maximum_fusion.3.refs_0_), channel_id=1, source_target_pairs={{0,448},{64,0},{128,64},{192,128},{256,192},{320,256},{384,320},{4... | collective-permute-start | bytes 983048 | tf_op jit(solution)/shard_map/ppermute | solution.py:20
  22.2 11.4 %collective-permute-start.7 = (bf16[4,160,256]{2,1,0:T(8,128)(2,1)S(1)}, bf16[4,160,256]{2,1,0:T(8,128)(2,1)S(1)}, u32[]{:S(2)}, u32[]{:S(2)}) collective-permute-start(bf16[4,160,256]{2,1,0:T(8,128)(2,1)S(1)} %pad_maximum_fusion.3.refs_0_), channel_id=1, source_target_pairs={{0,64},{64,128},{128,192},{192,256},{256,320},{320,384},{384,448},... | collective-permute-start | bytes 983048 | tf_op jit(solution)/shard_map/ppermute | solution.py:20
  24.9 43.7 %copy-start.8 = (bf16[4,160,256]{2,1,0:T(8,128)(2,1)}, bf16[4,160,256]{2,1,0:T(8,128)(2,1)S(1)}, u32[]{:S(2)}) copy-start(bf16[4,160,256]{2,1,0:T(8,128)(2,1)S(1)} %collective-permute-done.1.refs_1_) | copy-start | bytes 983044
  29.5 39.0 %copy-start.9 = (bf16[4,160,256]{2,1,0:T(8,128)(2,1)}, bf16[4,160,256]{2,1,0:T(8,128)(2,1)S(1)}, u32[]{:S(2)}) copy-start(bf16[4,160,256]{2,1,0:T(8,128)(2,1)S(1)} %collective-permute-done.2.refs_3_) | copy-start | bytes 983044
  33.6 34.9 %copy-start.10 = (bf16[4,160,256]{2,1,0:T(8,128)(2,1)}, bf16[4,160,256]{2,1,0:T(8,128)(2,1)S(1)}, u32[]{:S(2)}) copy-start(bf16[4,160,256]{2,1,0:T(8,128)(2,1)S(1)} %collective-permute-done.7.refs_2_) | copy-start | bytes 983044
  33.7 17.5 %collective-permute-start.8 = (bf16[8,160,256]{2,1,0:T(8,128)(2,1)S(1)}, bf16[8,160,256]{2,1,0:T(8,128)(2,1)S(1)}, u32[]{:S(2)}, u32[]{:S(2)}) collective-permute-start(bf16[8,160,256]{2,1,0:T(8,128)(2,1)S(1)} %get-tuple-element.37), channel_id=1, source_target_pairs={{0,64},{64,128},{128,192},{192,256},{256,320},{320,384},{384,448},... | collective-permute-start | bytes 1966088 | tf_op jit(solution)/shard_map/ppermute | solution.py:20
  35.9 17.8 %collective-permute-start.3 = (bf16[8,160,256]{2,1,0:T(8,128)(2,1)S(1)}, bf16[8,160,256]{2,1,0:T(8,128)(2,1)S(1)}, u32[]{:S(2)}, u32[]{:S(2)}) collective-permute-start(bf16[8,160,256]{2,1,0:T(8,128)(2,1)S(1)} %get-tuple-element.38), channel_id=1, source_target_pairs={{0,448},{64,0},{128,64},{192,128},{256,192},{320,256},{384,320},{4... | collective-permute-start | bytes 1966088 | tf_op jit(solution)/shard_map/ppermute | solution.py:20
  51.3 6.4 %copy-start.16 = (bf16[8,160,256]{2,1,0:T(8,128)(2,1)}, bf16[8,160,256]{2,1,0:T(8,128)(2,1)S(1)}, u32[]{:S(2)}) copy-start(bf16[8,160,256]{2,1,0:T(8,128)(2,1)S(1)} %collective-permute-done.8.refs_4_) | copy-start | bytes 1966084
  51.3 17.2 %collective-permute-start.9 = (bf16[8,160,256]{2,1,0:T(8,128)(2,1)S(1)}, bf16[8,160,256]{2,1,0:T(8,128)(2,1)S(1)}, u32[]{:S(2)}, u32[]{:S(2)}) collective-permute-start(bf16[8,160,256]{2,1,0:T(8,128)(2,1)S(1)} %collective-permute-done.8.refs_4_), channel_id=1, source_target_pairs={{0,64},{64,128},{128,192},{192,256},{256,320},{320,384},{384,448},... | collective-permute-start | bytes 1966088 | tf_op jit(solution)/shard_map/ppermute | solution.py:20
  53.8 17.1 %copy-start.17 = (bf16[8,160,256]{2,1,0:T(8,128)(2,1)}, bf16[8,160,256]{2,1,0:T(8,128)(2,1)S(1)}, u32[]{:S(2)}) copy-start(bf16[8,160,256]{2,1,0:T(8,128)(2,1)S(1)} %collective-permute-done.3.refs_5_) | copy-start | bytes 1966084
  53.8 17.1 %collective-permute-start.4 = (bf16[8,160,256]{2,1,0:T(8,128)(2,1)S(1)}, bf16[8,160,256]{2,1,0:T(8,128)(2,1)S(1)}, u32[]{:S(2)}, u32[]{:S(2)}) collective-permute-start(bf16[8,160,256]{2,1,0:T(8,128)(2,1)S(1)} %collective-permute-done.3.refs_5_), channel_id=1, source_target_pairs={{0,448},{64,0},{128,64},{192,128},{256,192},{320,256},{384,320},{4... | collective-permute-start | bytes 1966088 | tf_op jit(solution)/shard_map/ppermute | solution.py:20
  68.5 29.4 %copy-start.6 = (bf16[8,160,256]{2,1,0:T(8,128)(2,1)}, bf16[8,160,256]{2,1,0:T(8,128)(2,1)S(1)}, u32[]{:S(2)}) copy-start(bf16[8,160,256]{2,1,0:T(8,128)(2,1)S(1)} %collective-permute-done.9.refs_6_) | copy-start | bytes 1966084
  68.6 13.3 %collective-permute-start.10 = (bf16[6,160,256]{2,1,0:T(8,128)(2,1)S(1)}, bf16[6,160,256]{2,1,0:T(8,128)(2,1)S(1)}, u32[]{:S(2)}, u32[]{:S(2)}) collective-permute-start(bf16[6,160,256]{2,1,0:T(8,128)(2,1)S(1)} %slice.18), channel_id=1, source_target_pairs={{0,64},{64,128},{128,192},{192,256},{256,320},{320,384},{384,448},... | collective-permute-start | bytes 1474568 | tf_op jit(solution)/shard_map/ppermute | solution.py:20
  70.9 27.0 %copy-start.7 = (bf16[8,160,256]{2,1,0:T(8,128)(2,1)}, bf16[8,160,256]{2,1,0:T(8,128)(2,1)S(1)}, u32[]{:S(2)}) copy-start(bf16[8,160,256]{2,1,0:T(8,128)(2,1)S(1)} %collective-permute-done.4.refs_7_) | copy-start | bytes 1966084
  71.0 12.9 %collective-permute-start.5 = (bf16[6,160,256]{2,1,0:T(8,128)(2,1)S(1)}, bf16[6,160,256]{2,1,0:T(8,128)(2,1)S(1)}, u32[]{:S(2)}, u32[]{:S(2)}) collective-permute-start(bf16[6,160,256]{2,1,0:T(8,128)(2,1)S(1)} %slice.16), channel_id=1, source_target_pairs={{0,448},{64,0},{128,64},{192,128},{256,192},{320,256},{384,320},{4... | collective-permute-start | bytes 1474568 | tf_op jit(solution)/shard_map/ppermute | solution.py:20
  81.9 1.9 copy-start.12
  81.9 8.1 %collective-permute-start.11 = (bf16[2,160,256]{2,1,0:T(8,128)(2,1)S(1)}, bf16[2,160,256]{2,1,0:T(8,128)(2,1)S(1)}, u32[]{:S(2)}, u32[]{:S(2)}) collective-permute-start(bf16[2,160,256]{2,1,0:T(8,128)(2,1)S(1)} %slice.19), channel_id=1, source_target_pairs={{0,64},{64,128},{128,192},{192,256},{256,320},{320,384},{384,448},... | collective-permute-start | bytes 491528 | tf_op jit(solution)/shard_map/ppermute | solution.py:20
  83.8 14.1 %copy-start.13 = (bf16[6,160,256]{2,1,0:T(8,128)(2,1)}, bf16[6,160,256]{2,1,0:T(8,128)(2,1)S(1)}, u32[]{:S(2)}) copy-start(bf16[6,160,256]{2,1,0:T(8,128)(2,1)S(1)} %collective-permute-done.5.refs_9_) | copy-start | bytes 1474564
  83.9 7.7 %collective-permute-start.6 = (bf16[2,160,256]{2,1,0:T(8,128)(2,1)S(1)}, bf16[2,160,256]{2,1,0:T(8,128)(2,1)S(1)}, u32[]{:S(2)}, u32[]{:S(2)}) collective-permute-start(bf16[2,160,256]{2,1,0:T(8,128)(2,1)S(1)} %slice.17), channel_id=1, source_target_pairs={{0,448},{64,0},{128,64},{192,128},{256,192},{320,256},{384,320},{4... | collective-permute-start | bytes 491528 | tf_op jit(solution)/shard_map/ppermute | solution.py:20
  89.3 25.7 %copy-start.14 = (f32[256]{0:T(256)S(1)}, f32[256]{0:T(256)}, u32[]{:S(2)}) copy-start(f32[256]{0:T(256)} %param.13) | copy-start | bytes 3076
  89.3 25.7 %copy-start.15 = (f32[256]{0:T(256)S(1)}, f32[256]{0:T(256)}, u32[]{:S(2)}) copy-start(f32[256]{0:T(256)} %param.12) | copy-start | bytes 3076
  90.0 7.9 %copy-start.18 = (bf16[2,160,256]{2,1,0:T(8,128)(2,1)}, bf16[2,160,256]{2,1,0:T(8,128)(2,1)S(1)}, u32[]{:S(2)}) copy-start(bf16[2,160,256]{2,1,0:T(8,128)(2,1)S(1)} %collective-permute-done.11.refs_10_) | copy-start | bytes 491524
  91.5 0.7 copy-start.19
  107.2 7.8 %collective-permute-start.12 = (f32[384,1024]{1,0:T(8,128)}, f32[384,1024]{1,0:T(8,128)S(1)}, u32[]{:S(2)}, u32[]{:S(2)}) collective-permute-start(f32[384,1024]{1,0:T(8,128)} %get-tuple-element.25), channel_id=1, source_target_pairs={{0,16},{16,0},{1,17},{17,1},{2,18},{18,2},{3,19},{19,3},{4,20},{20... | collective-permute-start | bytes 4718600 | tf_op jit(solution)/shard_map/ppermute | solution.py:20
  109.1 62.4 %collective-permute-start.13 = (bf16[640,768]{1,0:T(8,128)(2,1)}, bf16[640,768]{1,0:T(8,128)(2,1)S(1)}, u32[]{:S(2)}, u32[]{:S(2)}) collective-permute-start(bf16[640,768]{1,0:T(8,128)(2,1)} %get-tuple-element.34), channel_id=1, source_target_pairs={{0,64},{64,128},{128,192},{192,256},{256,320},{320,384},{384,448},... | collective-permute-start | bytes 2949128 | tf_op jit(solution)/shard_map/ppermute | solution.py:20
  112.5 59.0 %collective-permute-start.14 = (bf16[640,768]{1,0:T(8,128)(2,1)}, bf16[640,768]{1,0:T(8,128)(2,1)S(1)}, u32[]{:S(2)}, u32[]{:S(2)}) collective-permute-start(bf16[640,768]{1,0:T(8,128)(2,1)} %get-tuple-element.35), channel_id=1, source_target_pairs={{0,448},{64,0},{128,64},{192,128},{256,192},{320,256},{384,320},{4... | collective-permute-start | bytes 2949128 | tf_op jit(solution)/shard_map/ppermute | solution.py:20
  115.0 1.4 copy-start.1
  116.8 33.7 %copy-start = (f32[384,768]{1,0:T(8,128)}, f32[384,768]{1,0:T(8,128)S(1)}, u32[]{:S(2)}) copy-start(f32[384,768]{1,0:T(8,128)S(1)} %get-tuple-element.28.qkd.q) | copy-start | bytes 3538948
  134.1 16.4 %copy-start.3 = (f32[16,1,1152]{2,1,0:T(1,128)}, f32[16,1,1152]{2,1,0:T(1,128)S(1)}, u32[]{:S(2)}) copy-start(f32[16,1,1152]{2,1,0:T(1,128)S(1)} %all_to_all.15.sums) | copy-start | bytes 221188
  136.5 0.8 copy-start.4
  152.8 9.4 %collective-permute-start.16 = (bf16[384,256]{1,0:T(8,128)(2,1)}, bf16[384,256]{1,0:T(8,128)(2,1)S(1)}, u32[]{:S(2)}, u32[]{:S(2)}) collective-permute-start(bf16[384,256]{1,0:T(8,128)(2,1)} %grad.1.gq), channel_id=1, source_target_pairs={{0,64},{64,128},{128,192},{192,256},{256,320},{320,384},{384,448},... | collective-permute-start | bytes 589832 | tf_op jit(solution)/shard_map/ppermute | solution.py:20
  157.6 7.8 %collective-permute-start.17 = (bf16[384,256]{1,0:T(8,128)(2,1)}, bf16[384,256]{1,0:T(8,128)(2,1)S(1)}, u32[]{:S(2)}, u32[]{:S(2)}) collective-permute-start(bf16[384,256]{1,0:T(8,128)(2,1)} %grad.1.gq), channel_id=1, source_target_pairs={{0,448},{64,0},{128,64},{192,128},{256,192},{320,256},{384,320},{4... | collective-permute-start | bytes 589832 | tf_op jit(solution)/shard_map/ppermute | solution.py:20
  165.4 6.1 %collective-permute-start.18 = (bf16[768,256]{1,0:T(8,128)(2,1)S(1)}, bf16[768,256]{1,0:T(8,128)(2,1)S(1)}, u32[]{:S(2)}, u32[]{:S(2)}) collective-permute-start(bf16[768,256]{1,0:T(8,128)(2,1)S(1)} %pad_maximum_fusion.2), channel_id=1, source_target_pairs={{0,16},{16,0},{1,17},{17,1},{2,18},{18,2},{3,19},{19,3},{4,20},{20... | collective-permute-start | bytes 1179656 | tf_op jit(solution)/shard_map/ppermute | solution.py:20
  167.4 4.2 %collective-permute-start.15 = (bf16[384,256]{1,0:T(8,128)(2,1)}, bf16[384,256]{1,0:T(8,128)(2,1)S(1)}, u32[]{:S(2)}, u32[]{:S(2)}) collective-permute-start(bf16[384,256]{1,0:T(8,128)(2,1)} %grad.1.gq), channel_id=1, source_target_pairs={{0,16},{16,0},{1,17},{17,1},{2,18},{18,2},{3,19},{19,3},{4,20},{20... | collective-permute-start | bytes 589832 | tf_op jit(solution)/shard_map/ppermute | solution.py:20
  169.8 1.8 copy-start.2
  169.8 1.8 copy-start.5
Sparse Core Ops, SparseCore 0:
  11.6 86.2 all-gather.1

commit v7 on v4

--- a/solution.py
+++ b/solution.py
@@ -111,7 +111,7 @@
             pltpu.SemaphoreType.DMA((2, 2)),
             pltpu.SemaphoreType.DMA,
         ],
-        compiler_params=pltpu.CompilerParams(vmem_limit_bytes=62 * MIB),
+        compiler_params=pltpu.CompilerParams(vmem_limit_bytes=44 * MIB),
         cost_estimate=pl.CostEstimate(
             flops=16 * length * depth * wide, bytes_accessed=4 * depth * (length + 2 * wide), transcendentals=0
         ),

time: 202 us -> 202 us (level)
  local copies, waits for them, and re-layouts: 5.64 us -> 9.74 us
  Pallas kernels: 15.9 us -> 13.3 us
  waiting for transfers between devices: 47.3 us -> 44.7 us
    unnamed x38 -> x24, local copies, waits for them, and re-layouts: 2.89 us -> 5.65 us
    pallas_call x1, Pallas kernels: 9.24 us -> 6.78 us  [project(): pl.pallas_call(functools.partial(project_kernel, layout=tuple(layout), wi...]
  transfers between devices with their start and end apart: 18 -> 18, of which waited for: 12 -> 10; matrix products, arithmetic and copies ran while one was open for 2% -> 2% of each run, Pallas kernels for 3% -> 3%
where the time goes in v7:
time: 202 us; the launch traced here: 201 us
  starting transfers between devices  59.2 us (29%)
  blocking collectives  57.3 us (28%)
  waiting for transfers between devices  44.7 us (22%)
  between operations  13.7 us (7%)
  Pallas kernels  13.3 us (7%)
  local copies, waits for them, and re-layouts  9.74 us (5%)
  other arithmetic  2.72 us (1%)
    ppermute x17, starting transfers between devices, shift(): lax.ppermute(value, axis, [(i, (i + by) % size) for i in range(size)])  59.2 us
    all_to_all x3, blocking collectives, to_all(): return lax.all_to_all(value, axes, 0, 0, tiled=True)  57.3 us
    ppermute x17, waiting for transfers between devices, shift(): lax.ppermute(value, axis, [(i, (i + by) % size) for i in range(size)])  38.7 us
    pallas_call x1, Pallas kernels, project(): pl.pallas_call(functools.partial(project_kernel, layout=tuple(layout), wi...  6.78 us
    all_gather x1, waiting for transfers between devices, on_device(): x = lax.all_gather(x, ('zh', 'x'), axis=0, tiled=True)  6.03 us
    unnamed x24, local copies, waits for them, and re-layouts  5.65 us
  transfers between devices with their start and end apart: 18, of which 10 were waited for; matrix products, arithmetic and copies ran while one was open for 2% of the time, Pallas kernels for 3%

profile of v7, /device:TPU:1, one launch (start us, length us, event | category | flops | bytes accessed | tf_op | source)
XLA Modules:
  0.0 200.8 jit_solution(16980063168701540301)
XLA Ops:
  6.5 1.0 dynamic-slice_bitcast_fusion.2
  7.5 8.8 %collective-permute-start = (bf16[160,384]{1,0:T(8,128)(2,1)S(1)}, bf16[160,384]{1,0:T(8,128)(2,1)S(1)}, u32[]{:S(2)}, u32[]{:S(2)}) collective-permute-start(bf16[160,384]{1,0:T(8,128)(2,1)S(1)} %get-tuple-element.38), channel_id=1, source_target_pairs={{0,16},{16,0},{1,17},{17,1},{2,18},{18,2},{3,19},{19,3},{4,20},{20... | collective-permute-start | bytes 368648 | tf_op jit(solution)/shard_map/ppermute | solution.py:20
  16.3 1.0 collective-permute-done
  17.3 0.7 pad_maximum_fusion.3
  18.0 1.1 pad_maximum_fusion.2.refs_0_
  19.1 1.9 collective-permute-start.1
  21.0 1.9 collective-permute-start.2
  22.9 3.4 %collective-permute-start.7 = (bf16[4,160,256]{2,1,0:T(8,128)(2,1)S(1)}, bf16[4,160,256]{2,1,0:T(8,128)(2,1)S(1)}, u32[]{:S(2)}, u32[]{:S(2)}) collective-permute-start(bf16[4,160,256]{2,1,0:T(8,128)(2,1)S(1)} %pad_maximum_fusion.2.refs_0_), channel_id=1, source_target_pairs={{0,64},{64,128},{128,192},{192,256},{256,320},{320,384},{384,448},... | collective-permute-start | bytes 983048 | tf_op jit(solution)/shard_map/ppermute | solution.py:20
  26.3 3.6 %collective-permute-done.1.refs_1_ = bf16[4,160,256]{2,1,0:T(8,128)(2,1)S(1)} collective-permute-done((bf16[4,160,256]{2,1,0:T(8,128)(2,1)S(1)}, bf16[4,160,256]{2,1,0:T(8,128)(2,1)S(1)}, u32[]{:S(2)}, u32[]{:S(2)}) %collective-permute-start.1) | collective-permute-done | bytes 327712 | tf_op jit(solution)/shard_map/ppermute | solution.py:20
  29.9 1.9 collective-permute-done.2.refs_3_
  31.8 2.6 %collective-permute-done.7.refs_2_ = bf16[4,160,256]{2,1,0:T(8,128)(2,1)S(1)} collective-permute-done((bf16[4,160,256]{2,1,0:T(8,128)(2,1)S(1)}, bf16[4,160,256]{2,1,0:T(8,128)(2,1)S(1)}, u32[]{:S(2)}, u32[]{:S(2)}) %collective-permute-start.7) | collective-permute-done | bytes 327712 | tf_op jit(solution)/shard_map/ppermute | solution.py:20
  34.6 2.3 %collective-permute-start.8 = (bf16[8,160,256]{2,1,0:T(8,128)(2,1)S(1)}, bf16[8,160,256]{2,1,0:T(8,128)(2,1)S(1)}, u32[]{:S(2)}, u32[]{:S(2)}) collective-permute-start(bf16[8,160,256]{2,1,0:T(8,128)(2,1)S(1)} %get-tuple-element.35), channel_id=1, source_target_pairs={{0,64},{64,128},{128,192},{192,256},{256,320},{320,384},{384,448},... | collective-permute-start | bytes 1966088 | tf_op jit(solution)/shard_map/ppermute | solution.py:20
  36.9 4.2 %collective-permute-start.3 = (bf16[8,160,256]{2,1,0:T(8,128)(2,1)S(1)}, bf16[8,160,256]{2,1,0:T(8,128)(2,1)S(1)}, u32[]{:S(2)}, u32[]{:S(2)}) collective-permute-start(bf16[8,160,256]{2,1,0:T(8,128)(2,1)S(1)} %get-tuple-element.36), channel_id=1, source_target_pairs={{0,448},{64,0},{128,64},{192,128},{256,192},{320,256},{384,320},{4... | collective-permute-start | bytes 1966088 | tf_op jit(solution)/shard_map/ppermute | solution.py:20
  41.1 11.1 %collective-permute-done.8.refs_4_ = bf16[8,160,256]{2,1,0:T(8,128)(2,1)S(1)} collective-permute-done((bf16[8,160,256]{2,1,0:T(8,128)(2,1)S(1)}, bf16[8,160,256]{2,1,0:T(8,128)(2,1)S(1)}, u32[]{:S(2)}, u32[]{:S(2)}) %collective-permute-start.8) | collective-permute-done | bytes 655392 | tf_op jit(solution)/shard_map/ppermute | solution.py:20
  52.2 1.9 collective-permute-start.9
  54.1 0.8 copy-done.6
  55.0 4.6 %collective-permute-start.4 = (bf16[8,160,256]{2,1,0:T(8,128)(2,1)S(1)}, bf16[8,160,256]{2,1,0:T(8,128)(2,1)S(1)}, u32[]{:S(2)}, u32[]{:S(2)}) collective-permute-start(bf16[8,160,256]{2,1,0:T(8,128)(2,1)S(1)} %collective-permute-done.3.refs_5_), channel_id=1, source_target_pairs={{0,448},{64,0},{128,64},{192,128},{256,192},{320,256},{384,320},{4... | collective-permute-start | bytes 1966088 | tf_op jit(solution)/shard_map/ppermute | solution.py:20
  59.6 9.5 %collective-permute-done.9.refs_6_ = bf16[8,160,256]{2,1,0:T(8,128)(2,1)S(1)} collective-permute-done((bf16[8,160,256]{2,1,0:T(8,128)(2,1)S(1)}, bf16[8,160,256]{2,1,0:T(8,128)(2,1)S(1)}, u32[]{:S(2)}, u32[]{:S(2)}) %collective-permute-start.9) | collective-permute-done | bytes 655392 | tf_op jit(solution)/shard_map/ppermute | solution.py:20
  69.1 1.9 collective-permute-start.10
  71.0 5.1 %collective-permute-start.5 = (bf16[6,160,256]{2,1,0:T(8,128)(2,1)S(1)}, bf16[6,160,256]{2,1,0:T(8,128)(2,1)S(1)}, u32[]{:S(2)}, u32[]{:S(2)}) collective-permute-start(bf16[6,160,256]{2,1,0:T(8,128)(2,1)S(1)} %slice.16), channel_id=1, source_target_pairs={{0,448},{64,0},{128,64},{192,128},{256,192},{320,256},{384,320},{4... | collective-permute-start | bytes 1474568 | tf_op jit(solution)/shard_map/ppermute | solution.py:20
  76.1 5.4 %collective-permute-done.10.refs_8_ = bf16[6,160,256]{2,1,0:T(8,128)(2,1)S(1)} collective-permute-done((bf16[6,160,256]{2,1,0:T(8,128)(2,1)S(1)}, bf16[6,160,256]{2,1,0:T(8,128)(2,1)S(1)}, u32[]{:S(2)}, u32[]{:S(2)}) %collective-permute-start.10) | collective-permute-done | bytes 491552 | tf_op jit(solution)/shard_map/ppermute | solution.py:20
  81.6 0.7 slice.19
  82.2 1.9 collective-permute-start.11
  84.2 0.7 slice.17
  84.8 0.8 copy-done.4
  85.6 4.6 %collective-permute-start.6 = (bf16[2,160,256]{2,1,0:T(8,128)(2,1)}, bf16[2,160,256]{2,1,0:T(8,128)(2,1)S(1)}, u32[]{:S(2)}, u32[]{:S(2)}) collective-permute-start(bf16[2,160,256]{2,1,0:T(8,128)(2,1)} %slice.17), channel_id=1, source_target_pairs={{0,448},{64,0},{128,64},{192,128},{256,192},{320,256},{384,320},{4... | collective-permute-start | bytes 491528 | tf_op jit(solution)/shard_map/ppermute | solution.py:20
  90.3 2.4 %collective-permute-done.6.refs_11_ = bf16[2,160,256]{2,1,0:T(8,128)(2,1)S(1)} collective-permute-done((bf16[2,160,256]{2,1,0:T(8,128)(2,1)}, bf16[2,160,256]{2,1,0:T(8,128)(2,1)S(1)}, u32[]{:S(2)}, u32[]{:S(2)}) %collective-permute-start.6) | collective-permute-done | bytes 163872 | tf_op jit(solution)/shard_map/ppermute | solution.py:20
  92.8 6.0 %all-gather.2.cloned.1.call-done.x_hbm = bf16[2560,768]{1,0:T(8,128)(2,1)} async-done(((bf16[160,768]{1,0:T(8,128)(2,1)}), bf16[2560,768]{1,0:T(8,128)(2,1)}) %all-gather.2.cloned.1.call-update) | async-done | bytes 3932176 | tf_op jit(solution)/shard_map/all_gather | solution.py:275
  98.8 1.0 copy-done.5
  99.8 1.1 copy-done.7
  100.9 1.1 copy-done.9
  102.0 6.8 %project.1 = (f32[384,1024]{1,0:T(8,128)S(1)}, f32[384,1024]{1,0:T(8,128)S(1)}, bf16[1280,768]{1,0:T(8,128)(2,1)}) custom-call(s32[2]{0:T(128)S(1)} %pad_add_fusion.place, bf16[2560,768]{1,0:T(8,128)(2,1)} %all-gather.2.cloned.1.call-done.x_hbm, bf16[4,160,256]{2,1,0:T(8,128)(2,1)S(1)} %pad_maximum_fusion.2.refs_0_, ...), custom_call_target="tpu_custom_call" | custom-call | flops 4026531840 | bytes 9175040 | tf_op jit(solution)/shard_map/project/pallas_call | solution.py:94
  108.8 2.6 %collective-permute-start.12 = (f32[384,1024]{1,0:T(8,128)S(1)}, f32[384,1024]{1,0:T(8,128)S(1)}, u32[]{:S(2)}, u32[]{:S(2)}) collective-permute-start(f32[384,1024]{1,0:T(8,128)S(1)} %get-tuple-element.24), channel_id=1, source_target_pairs={{0,16},{16,0},{1,17},{17,1},{2,18},{18,2},{3,19},{19,3},{4,20},{20... | collective-permute-start | bytes 4718600 | tf_op jit(solution)/shard_map/ppermute | solution.py:20
  111.4 3.1 %collective-permute-start.13 = (bf16[1280,768]{1,0:T(8,128)(2,1)}, bf16[1280,768]{1,0:T(8,128)(2,1)S(1)}, u32[]{:S(2)}, u32[]{:S(2)}) collective-permute-start(bf16[1280,768]{1,0:T(8,128)(2,1)} %get-tuple-element.33), channel_id=1, source_target_pairs={{0,64},{64,0},{1,65},{65,1},{2,66},{66,2},{3,67},{67,3},{4,68},{68... | collective-permute-start | bytes 5898248 | tf_op jit(solution)/shard_map/ppermute | solution.py:20
  114.6 0.4 merge.1
  115.0 20.2 %all_to_all.15.sums = f32[16,9,128]{2,1,0:T(8,128)S(1)} all-to-all(f32[16,9,128]{2,1,0:T(8,128)S(1)} %get-tuple-element.26), channel_id=1, replica_groups=mesh['yh'=4,'yl'=2,'zl'=2,'c'=2,'x'=4,'zh'=4] {'x','zh'}, dimensions={0} | all-to-all | bytes 147456 | tf_op jit(solution)/shard_map/all_to_all | solution.py:261
  135.1 2.4 %attend.1 = (f32[384,256]{1,0:T(8,128)S(1)}, f32[16,3,128]{2,1,0:T(4,128)S(1)}) custom-call(f32[16,9,128]{2,1,0:T(8,128)S(1)} %all_to_all.15.sums, f32[384,768]{1,0:T(8,128)S(1)} %get-tuple-element.27.qkd.q, bf16[384,256]{1,0:T(8,128)(2,1)S(1)} %get-tuple-element.28.value, f32[2,256]{1,0:T(2,128)S(1)} %pad_maximum_fusion.4.gains), custom_call_target="tpu_custom_call" | custom-call | tf_op jit(solution)/shard_map/attend/pallas_call | solution.py:205
  137.5 0.8 copy-done.3
  138.3 12.1 %all_to_all.16.back = f32[16,3,128]{2,1,0:T(4,128)} all-to-all(f32[16,3,128]{2,1,0:T(4,128)S(1)} %get-tuple-element.30), channel_id=1, replica_groups=mesh['yh'=4,'yl'=2,'zl'=2,'c'=2,'x'=4,'zh'=4] {'x','zh'}, dimensions={0} | all-to-all | bytes 49152 | tf_op jit(solution)/shard_map/all_to_all | solution.py:261
  150.4 2.3 %grad.1.gq = bf16[384,256]{1,0:T(8,128)(2,1)} custom-call(f32[16,9,128]{2,1,0:T(8,128)} %copy-done.1, f32[16,3,128]{2,1,0:T(4,128)} %all_to_all.16.back, f32[384,768]{1,0:T(8,128)} %copy-done, f32[384,256]{1,0:T(8,128)} %copy-done.3), custom_call_target="tpu_custom_call" | custom-call | tf_op jit(solution)/shard_map/grad/pallas_call | solution.py:224
  152.7 2.3 %collective-permute-start.15 = (bf16[384,256]{1,0:T(8,128)(2,1)}, bf16[384,256]{1,0:T(8,128)(2,1)S(1)}, u32[]{:S(2)}, u32[]{:S(2)}) collective-permute-start(bf16[384,256]{1,0:T(8,128)(2,1)} %grad.1.gq), channel_id=1, source_target_pairs={{0,64},{64,0},{1,65},{65,1},{2,66},{66,2},{3,67},{67,3},{4,68},{68... | collective-permute-start | bytes 589832 | tf_op jit(solution)/shard_map/ppermute | solution.py:20
  155.0 4.5 %collective-permute-start.14 = (bf16[384,256]{1,0:T(8,128)(2,1)}, bf16[384,256]{1,0:T(8,128)(2,1)S(1)}, u32[]{:S(2)}, u32[]{:S(2)}) collective-permute-start(bf16[384,256]{1,0:T(8,128)(2,1)} %grad.1.gq), channel_id=1, source_target_pairs={{0,16},{16,0},{1,17},{17,1},{2,18},{18,2},{3,19},{19,3},{4,20},{20... | collective-permute-start | bytes 589832 | tf_op jit(solution)/shard_map/ppermute | solution.py:20
  159.5 1.1 collective-permute-done.15.gq_near
  160.6 4.3 %collective-permute-start.16 = (bf16[384,256]{1,0:T(8,128)(2,1)S(1)}, bf16[384,256]{1,0:T(8,128)(2,1)S(1)}, u32[]{:S(2)}, u32[]{:S(2)}) collective-permute-start(bf16[384,256]{1,0:T(8,128)(2,1)S(1)} %collective-permute-done.15.gq_near), channel_id=1, source_target_pairs={{0,16},{16,0},{1,17},{17,1},{2,18},{18,2},{3,19},{19,3},{4,20},{20... | collective-permute-start | bytes 589832 | tf_op jit(solution)/shard_map/ppermute | solution.py:20
  164.9 1.7 dynamic-slice_bitcast_fusion.x
  166.6 1.5 outer.1
  168.1 25.1 %all_to_all.17 = bf16[8,160,256]{2,1,0:T(8,128)(2,1)S(1)} all-to-all(bf16[8,160,256]{2,1,0:T(8,128)(2,1)S(1)} %bitcast.21), channel_id=1, replica_groups=mesh['yh'=4,'yl'=2,'zl'=2,'c'=2,'x'=4,'zh'=4] {'zl','yh'}, dimensions={0} | all-to-all | bytes 1310720 | tf_op jit(solution)/shard_map/all_to_all | solution.py:261
  193.2 0.8 convert_reduce_fusion
  (33 shorter events, 0.3 us)
Async XLA Ops:
  6.5 92.3 %all-gather.2.cloned.1.call-start = ((), (), s32[]{:S(2)}) async-start(), calls=%async_computation.3 | async-start | bytes 4177920 | tf_op jit(solution)/shard_map/all_gather | solution.py:275
  7.5 9.7 %collective-permute-start = (bf16[160,384]{1,0:T(8,128)(2,1)S(1)}, bf16[160,384]{1,0:T(8,128)(2,1)S(1)}, u32[]{:S(2)}, u32[]{:S(2)}) collective-permute-start(bf16[160,384]{1,0:T(8,128)(2,1)S(1)} %get-tuple-element.38), channel_id=1, source_target_pairs={{0,16},{16,0},{1,17},{17,1},{2,18},{18,2},{3,19},{19,3},{4,20},{20... | collective-permute-start | bytes 368648 | tf_op jit(solution)/shard_map/ppermute | solution.py:20
  19.1 10.8 %collective-permute-start.1 = (bf16[4,160,256]{2,1,0:T(8,128)(2,1)S(1)}, bf16[4,160,256]{2,1,0:T(8,128)(2,1)S(1)}, u32[]{:S(2)}, u32[]{:S(2)}) collective-permute-start(bf16[4,160,256]{2,1,0:T(8,128)(2,1)S(1)} %pad_maximum_fusion.2.refs_0_), channel_id=1, source_target_pairs={{0,32},{32,0},{1,33},{33,1},{2,34},{34,2},{3,35},{35,3},{4,36},{36... | collective-permute-start | bytes 983048 | tf_op jit(solution)/shard_map/ppermute | solution.py:20
  21.0 10.8 %collective-permute-start.2 = (bf16[4,160,256]{2,1,0:T(8,128)(2,1)S(1)}, bf16[4,160,256]{2,1,0:T(8,128)(2,1)S(1)}, u32[]{:S(2)}, u32[]{:S(2)}) collective-permute-start(bf16[4,160,256]{2,1,0:T(8,128)(2,1)S(1)} %pad_maximum_fusion.2.refs_0_), channel_id=1, source_target_pairs={{0,448},{64,0},{128,64},{192,128},{256,192},{320,256},{384,320},{4... | collective-permute-start | bytes 983048 | tf_op jit(solution)/shard_map/ppermute | solution.py:20
  22.9 11.5 %collective-permute-start.7 = (bf16[4,160,256]{2,1,0:T(8,128)(2,1)S(1)}, bf16[4,160,256]{2,1,0:T(8,128)(2,1)S(1)}, u32[]{:S(2)}, u32[]{:S(2)}) collective-permute-start(bf16[4,160,256]{2,1,0:T(8,128)(2,1)S(1)} %pad_maximum_fusion.2.refs_0_), channel_id=1, source_target_pairs={{0,64},{64,128},{128,192},{192,256},{256,320},{320,384},{384,448},... | collective-permute-start | bytes 983048 | tf_op jit(solution)/shard_map/ppermute | solution.py:20
  34.6 17.6 %collective-permute-start.8 = (bf16[8,160,256]{2,1,0:T(8,128)(2,1)S(1)}, bf16[8,160,256]{2,1,0:T(8,128)(2,1)S(1)}, u32[]{:S(2)}, u32[]{:S(2)}) collective-permute-start(bf16[8,160,256]{2,1,0:T(8,128)(2,1)S(1)} %get-tuple-element.35), channel_id=1, source_target_pairs={{0,64},{64,128},{128,192},{192,256},{256,320},{320,384},{384,448},... | collective-permute-start | bytes 1966088 | tf_op jit(solution)/shard_map/ppermute | solution.py:20
  36.9 18.1 %collective-permute-start.3 = (bf16[8,160,256]{2,1,0:T(8,128)(2,1)S(1)}, bf16[8,160,256]{2,1,0:T(8,128)(2,1)S(1)}, u32[]{:S(2)}, u32[]{:S(2)}) collective-permute-start(bf16[8,160,256]{2,1,0:T(8,128)(2,1)S(1)} %get-tuple-element.36), channel_id=1, source_target_pairs={{0,448},{64,0},{128,64},{192,128},{256,192},{320,256},{384,320},{4... | collective-permute-start | bytes 1966088 | tf_op jit(solution)/shard_map/ppermute | solution.py:20
  52.2 16.8 %collective-permute-start.9 = (bf16[8,160,256]{2,1,0:T(8,128)(2,1)S(1)}, bf16[8,160,256]{2,1,0:T(8,128)(2,1)S(1)}, u32[]{:S(2)}, u32[]{:S(2)}) collective-permute-start(bf16[8,160,256]{2,1,0:T(8,128)(2,1)S(1)} %collective-permute-done.8.refs_4_), channel_id=1, source_target_pairs={{0,64},{64,128},{128,192},{192,256},{256,320},{320,384},{384,448},... | collective-permute-start | bytes 1966088 | tf_op jit(solution)/shard_map/ppermute | solution.py:20
  54.1 0.8 copy-start.6
  55.0 29.9 %copy-start.8 = (bf16[8,160,256]{2,1,0:T(8,128)(2,1)}, bf16[8,160,256]{2,1,0:T(8,128)(2,1)S(1)}, u32[]{:S(2)}) copy-start(bf16[8,160,256]{2,1,0:T(8,128)(2,1)S(1)} %collective-permute-done.3.refs_5_) | copy-start | bytes 1966084
  55.0 16.0 %collective-permute-start.4 = (bf16[8,160,256]{2,1,0:T(8,128)(2,1)S(1)}, bf16[8,160,256]{2,1,0:T(8,128)(2,1)S(1)}, u32[]{:S(2)}, u32[]{:S(2)}) collective-permute-start(bf16[8,160,256]{2,1,0:T(8,128)(2,1)S(1)} %collective-permute-done.3.refs_5_), channel_id=1, source_target_pairs={{0,448},{64,0},{128,64},{192,128},{256,192},{320,256},{384,320},{4... | collective-permute-start | bytes 1966088 | tf_op jit(solution)/shard_map/ppermute | solution.py:20
  69.1 12.5 %collective-permute-start.10 = (bf16[6,160,256]{2,1,0:T(8,128)(2,1)S(1)}, bf16[6,160,256]{2,1,0:T(8,128)(2,1)S(1)}, u32[]{:S(2)}, u32[]{:S(2)}) collective-permute-start(bf16[6,160,256]{2,1,0:T(8,128)(2,1)S(1)} %slice.18), channel_id=1, source_target_pairs={{0,64},{64,128},{128,192},{192,256},{256,320},{320,384},{384,448},... | collective-permute-start | bytes 1474568 | tf_op jit(solution)/shard_map/ppermute | solution.py:20
  71.0 13.1 %collective-permute-start.5 = (bf16[6,160,256]{2,1,0:T(8,128)(2,1)S(1)}, bf16[6,160,256]{2,1,0:T(8,128)(2,1)S(1)}, u32[]{:S(2)}, u32[]{:S(2)}) collective-permute-start(bf16[6,160,256]{2,1,0:T(8,128)(2,1)S(1)} %slice.16), channel_id=1, source_target_pairs={{0,448},{64,0},{128,64},{192,128},{256,192},{320,256},{384,320},{4... | collective-permute-start | bytes 1474568 | tf_op jit(solution)/shard_map/ppermute | solution.py:20
  82.2 8.1 %collective-permute-start.11 = (bf16[2,160,256]{2,1,0:T(8,128)(2,1)}, bf16[2,160,256]{2,1,0:T(8,128)(2,1)S(1)}, u32[]{:S(2)}, u32[]{:S(2)}) collective-permute-start(bf16[2,160,256]{2,1,0:T(8,128)(2,1)} %slice.19), channel_id=1, source_target_pairs={{0,64},{64,128},{128,192},{192,256},{256,320},{320,384},{384,448},... | collective-permute-start | bytes 491528 | tf_op jit(solution)/shard_map/ppermute | solution.py:20
  84.8 0.8 copy-start.4
  85.6 7.1 %collective-permute-start.6 = (bf16[2,160,256]{2,1,0:T(8,128)(2,1)}, bf16[2,160,256]{2,1,0:T(8,128)(2,1)S(1)}, u32[]{:S(2)}, u32[]{:S(2)}) collective-permute-start(bf16[2,160,256]{2,1,0:T(8,128)(2,1)} %slice.17), channel_id=1, source_target_pairs={{0,448},{64,0},{128,64},{192,128},{256,192},{320,256},{384,320},{4... | collective-permute-start | bytes 491528 | tf_op jit(solution)/shard_map/ppermute | solution.py:20
  90.2 24.3 %copy-start.11 = (f32[256]{0:T(256)S(1)}, f32[256]{0:T(256)}, u32[]{:S(2)}) copy-start(f32[256]{0:T(256)} %param.12) | copy-start | bytes 3076
  90.2 24.3 %copy-start.10 = (f32[256]{0:T(256)S(1)}, f32[256]{0:T(256)}, u32[]{:S(2)}) copy-start(f32[256]{0:T(256)} %param.13) | copy-start | bytes 3076
  98.8 1.0 copy-start.5
  99.8 1.1 copy-start.7
  100.9 1.1 copy-start.9
  108.8 5.8 %collective-permute-start.12 = (f32[384,1024]{1,0:T(8,128)S(1)}, f32[384,1024]{1,0:T(8,128)S(1)}, u32[]{:S(2)}, u32[]{:S(2)}) collective-permute-start(f32[384,1024]{1,0:T(8,128)S(1)} %get-tuple-element.24), channel_id=1, source_target_pairs={{0,16},{16,0},{1,17},{17,1},{2,18},{18,2},{3,19},{19,3},{4,20},{20... | collective-permute-start | bytes 4718600 | tf_op jit(solution)/shard_map/ppermute | solution.py:20
  111.4 55.2 %collective-permute-start.13 = (bf16[1280,768]{1,0:T(8,128)(2,1)}, bf16[1280,768]{1,0:T(8,128)(2,1)S(1)}, u32[]{:S(2)}, u32[]{:S(2)}) collective-permute-start(bf16[1280,768]{1,0:T(8,128)(2,1)} %get-tuple-element.33), channel_id=1, source_target_pairs={{0,64},{64,0},{1,65},{65,1},{2,66},{66,2},{3,67},{67,3},{4,68},{68... | collective-permute-start | bytes 5898248 | tf_op jit(solution)/shard_map/ppermute | solution.py:20
  114.9 35.4 %copy-start = (f32[384,768]{1,0:T(8,128)}, f32[384,768]{1,0:T(8,128)S(1)}, u32[]{:S(2)}) copy-start(f32[384,768]{1,0:T(8,128)S(1)} %get-tuple-element.27.qkd.q) | copy-start | bytes 3538948
  135.1 15.2 %copy-start.1 = (f32[16,9,128]{2,1,0:T(8,128)}, f32[16,9,128]{2,1,0:T(8,128)S(1)}, u32[]{:S(2)}) copy-start(f32[16,9,128]{2,1,0:T(8,128)S(1)} %all_to_all.15.sums) | copy-start | bytes 221188
  137.5 0.8 copy-start.3
  152.7 7.9 %collective-permute-start.15 = (bf16[384,256]{1,0:T(8,128)(2,1)}, bf16[384,256]{1,0:T(8,128)(2,1)S(1)}, u32[]{:S(2)}, u32[]{:S(2)}) collective-permute-start(bf16[384,256]{1,0:T(8,128)(2,1)} %grad.1.gq), channel_id=1, source_target_pairs={{0,64},{64,0},{1,65},{65,1},{2,66},{66,2},{3,67},{67,3},{4,68},{68... | collective-permute-start | bytes 589832 | tf_op jit(solution)/shard_map/ppermute | solution.py:20
  155.0 11.5 %collective-permute-start.14 = (bf16[384,256]{1,0:T(8,128)(2,1)}, bf16[384,256]{1,0:T(8,128)(2,1)S(1)}, u32[]{:S(2)}, u32[]{:S(2)}) collective-permute-start(bf16[384,256]{1,0:T(8,128)(2,1)} %grad.1.gq), channel_id=1, source_target_pairs={{0,16},{16,0},{1,17},{17,1},{2,18},{18,2},{3,19},{19,3},{4,20},{20... | collective-permute-start | bytes 589832 | tf_op jit(solution)/shard_map/ppermute | solution.py:20
  159.5 7.1 %copy-start.2 = (bf16[384,256]{1,0:T(8,128)(2,1)S(1)}, bf16[384,256]{1,0:T(8,128)(2,1)}, u32[]{:S(2)}) copy-start(bf16[384,256]{1,0:T(8,128)(2,1)} %grad.1.gq) | copy-start | bytes 589828
  160.6 6.0 %collective-permute-start.16 = (bf16[384,256]{1,0:T(8,128)(2,1)S(1)}, bf16[384,256]{1,0:T(8,128)(2,1)S(1)}, u32[]{:S(2)}, u32[]{:S(2)}) collective-permute-start(bf16[384,256]{1,0:T(8,128)(2,1)S(1)} %collective-permute-done.15.gq_near), channel_id=1, source_target_pairs={{0,16},{16,0},{1,17},{17,1},{2,18},{18,2},{3,19},{19,3},{4,20},{20... | collective-permute-start | bytes 589832 | tf_op jit(solution)/shard_map/ppermute | solution.py:20
Sparse Core Ops, SparseCore 0:
  18.1 80.6 all-gather.1
